TPU v7x, 256 devices: a whole 4x4x8 slice. The times are simulated.
256 devices in a mesh: dp: 32 (over z, y), expert: 8 (over x, core).
Axes of the slice: x: 4, y: 4, z: 8, core: 2. Of those that a mesh axis runs over, the one named last changes fastest.
Arguments:
- tokens: bfloat16 [4096, 2048], P(('dp', 'expert')), may hold values from -6 to 6
- expert_ids: int32 [4096, 8], P(('dp', 'expert')), may hold values from 0 to 127, as said below
- route_weight: float32 [4096, 8], P(('dp', 'expert')), may hold values from 0.03 to 0.6
- out_grad: bfloat16 [4096, 2048], P(('dp', 'expert')), may hold values from -6 to 6
- gate_weight: bfloat16 [256, 2048, 384], P(('dp', 'expert')), may hold values from -0.125 to 0.125
- up_weight: bfloat16 [256, 2048, 384], P(('dp', 'expert')), may hold values from -0.125 to 0.125
- down_weight: bfloat16 [256, 384, 2048], P(('dp', 'expert')), may hold values from -0.21875 to 0.21875
Outputs:
- layer_out: bfloat16 [4096, 2048], P(('dp', 'expert'))
- token_grad: bfloat16 [4096, 2048], P(('dp', 'expert'))
- route_grad: float32 [4096, 8], P(('dp', 'expert'))
- gate_grad: bfloat16 [256, 2048, 384], P(('dp', 'expert'))
- up_grad: bfloat16 [256, 2048, 384], P(('dp', 'expert'))
- down_grad: bfloat16 [256, 384, 2048], P(('dp', 'expert'))
Inputs may be any that keep to these rules, and one draw needn't show every extreme that they name: `expert_ids`: each row names 8 different experts. The rows of one device name no expert more than 2 times, and one expert is named exactly 2 times by the rows of every device.
All inputs are finite; a program needn't handle non-finite values.
Results may differ from a plain program's by a relative error of at most 0.0071.
Values may be sent and summed in bfloat16 or wider, within the bound.
No kernel may reach another device: no remote copies, remote signals or barrier semaphores. Data moves between devices by JAX's collectives and lax.ppermute only.
A program may use at most 128 MiB of HBM per device.

v0:
```python
import functools

import jax
import jax.numpy as jnp
from jax import lax
from jax.experimental import pallas as pl
from jax.experimental.pallas import tpu as pltpu
from jax.sharding import Mesh, PartitionSpec as P

AXES = ("z", "y", "x", "core")
SIZES = (8, 4, 4, 2)
PLANES = 8
CHIPS = 16
TOK = 16
TOP = 8
SLOTS = 2
D = 2048
HALF = 384
META = 128
COLS = 2 * D + META
GROUP = PLANES * TOK
ROWS = CHIPS * PLANES * SLOTS
F32 = jnp.float32
BF16 = jnp.bfloat16
VMEM = pl.BlockSpec(memory_space=pltpu.VMEM)
SMEM = pl.BlockSpec(memory_space=pltpu.SMEM)


def params(mib):
    return pltpu.CompilerParams(vmem_limit_bytes=mib * 2**20)


def dot(a, b, a_dim, b_dim):
    return lax.dot_general(a, b, (((a_dim,), (b_dim,)), ((), ())), preferred_element_type=F32)


def three_pieces(value):
    high = value.astype(BF16)
    rest = value - high.astype(F32)
    middle = rest.astype(BF16)
    low = (rest - middle.astype(F32)).astype(BF16)
    return high, middle, low


def pack_kernel(tok_ref, grad_ref, ids_ref, weight_ref, out_ref):
    pieces = (ids_ref[...].astype(F32).astype(BF16),) + three_pieces(weight_ref[...])
    rows = lax.broadcasted_iota(jnp.int32, (TOP, META), 0)
    lanes = lax.broadcasted_iota(jnp.int32, (TOP, META), 1)
    meta = jnp.zeros((TOK, META), F32)
    for i, piece in enumerate(pieces):
        place = jnp.where(lanes == rows + i * TOP, 1.0, 0.0).astype(BF16)
        meta = meta + dot(piece, place, 0, 0)
    meta = meta.astype(BF16)
    for z in range(PLANES):
        out_ref[z, :, :D] = tok_ref[...]
        out_ref[z, :, D : 2 * D] = grad_ref[...]
        out_ref[z, :, 2 * D :] = meta


def pack(tokens, out_grad, ids_t, weight_t):
    return pl.pallas_call(
        pack_kernel,
        out_shape=jax.ShapeDtypeStruct((PLANES, TOK, COLS), BF16),
        in_specs=[VMEM] * 4,
        out_specs=VMEM,
        compiler_params=params(16),
        name="pack_rows",
    )(tokens, out_grad, ids_t, weight_t)


def spread_kernel(first_ref, all_ref, send_ref, mask_ref, weight_ref):
    meta = all_ref[:, 2 * D :].astype(F32)
    shape = (GROUP, ROWS)
    lane = lax.broadcasted_iota(jnp.int32, shape, 1)
    row = lax.broadcasted_iota(jnp.int32, shape, 0)
    expert = (first_ref[0] + lane // (PLANES * SLOTS)).astype(F32)
    named = jnp.zeros(shape, F32)
    weight = jnp.zeros(shape, F32)
    for k in range(TOP):
        hit = meta[:, k : k + 1] == expert
        w = meta[:, TOP + k : TOP + k + 1] + meta[:, 2 * TOP + k : 2 * TOP + k + 1]
        w = w + meta[:, 3 * TOP + k : 3 * TOP + k + 1]
        named = jnp.where(hit, 1.0, named)
        weight = jnp.where(hit, w, weight)
    ri = lax.broadcasted_iota(jnp.int32, (GROUP, GROUP), 0)
    ci = lax.broadcasted_iota(jnp.int32, (GROUP, GROUP), 1)
    earlier = jnp.where((ri // TOK == ci // TOK) & (ci < ri), 1.0, 0.0).astype(BF16)
    slot = dot(earlier, named.astype(BF16), 1, 0)
    wanted = (lane % SLOTS).astype(F32)
    source = (lane // SLOTS) % PLANES
    mask = jnp.where((slot == wanted) & (source == row // TOK), named, 0.0)
    weight = weight * mask
    mask_ref[...] = mask.astype(BF16)
    weight_ref[...] = weight
    pick = mask.T.astype(BF16)
    scale = jnp.sum(weight.T, axis=1, keepdims=True)
    for i in range(0, D, 512):
        send_ref[:, i : i + 512] = dot(pick, all_ref[:, i : i + 512], 1, 0).astype(BF16)
    for i in range(D, 2 * D, 512):
        send_ref[:, i : i + 512] = (dot(pick, all_ref[:, i : i + 512], 1, 0) * scale).astype(BF16)


def spread(first, gathered):
    return pl.pallas_call(
        spread_kernel,
        out_shape=(
            jax.ShapeDtypeStruct((ROWS, 2 * D), BF16),
            jax.ShapeDtypeStruct((GROUP, ROWS), BF16),
            jax.ShapeDtypeStruct((GROUP, ROWS), F32),
        ),
        in_specs=[SMEM, VMEM],
        out_specs=(VMEM, VMEM, VMEM),
        compiler_params=params(24),
        name="spread_rows",
    )(first, gathered)


def expert_kernel(in_ref, gate_ref, up_ref, down_ref, back_ref, hidden_ref, pre_ref, up_pre_ref):
    w_gate = gate_ref[0]
    w_up = up_ref[0]
    w_down = down_ref[0]
    rows = in_ref[:, :D]
    gate = dot(rows, w_gate, 1, 0)
    up = dot(rows, w_up, 1, 0)
    sig = jax.nn.sigmoid(gate)
    act = gate * sig
    hidden = (act * up).astype(BF16)
    hidden_ref[...] = hidden
    hidden_grad = dot(in_ref[:, D:], w_down, 1, 1)
    pre = (hidden_grad * up * sig * (1.0 + gate * (1.0 - sig))).astype(BF16)
    up_pre = (hidden_grad * act).astype(BF16)
    pre_ref[...] = pre
    up_pre_ref[...] = up_pre
    for i in range(0, D, 512):
        back_ref[:, i : i + 512] = dot(hidden, down_ref[0, :, i : i + 512], 1, 0).astype(BF16)
    for i in range(0, D, 512):
        back_ref[:, D + i : D + i + 512] = (
            dot(pre, gate_ref[0, i : i + 512, :], 1, 1) + dot(up_pre, up_ref[0, i : i + 512, :], 1, 1)
        ).astype(BF16)


def expert(rows, gate_weight, up_weight, down_weight):
    act = jax.ShapeDtypeStruct((ROWS, HALF), BF16)
    return pl.pallas_call(
        expert_kernel,
        out_shape=(jax.ShapeDtypeStruct((ROWS, 2 * D), BF16), act, act, act),
        in_specs=[VMEM] * 4,
        out_specs=(VMEM,) * 4,
        compiler_params=params(40),
        cost_estimate=pl.CostEstimate(
            flops=12 * ROWS * D * HALF, bytes_accessed=8 * 2**20, transcendentals=ROWS * HALF
        ),
        name="expert_rows",
    )(rows, gate_weight, up_weight, down_weight)


def weight_grad_kernel(x_a, g_a, x_b, g_b, h_a, p_a, u_a, h_b, p_b, u_b, gate_ref, up_ref, down_ref):
    gate_ref[0] = (dot(x_a[...], p_a[...], 0, 0) + dot(x_b[...], p_b[...], 0, 0)).astype(BF16)
    up_ref[0] = (dot(x_a[...], u_a[...], 0, 0) + dot(x_b[...], u_b[...], 0, 0)).astype(BF16)
    down_ref[0] = (dot(h_a[...], g_a[...], 0, 0) + dot(h_b[...], g_b[...], 0, 0)).astype(BF16)


def weight_grads(own, other, own_acts, other_acts):
    width = 512
    steps = D // width
    x_spec = pl.BlockSpec((ROWS, width), lambda i: (0, i))
    g_spec = pl.BlockSpec((ROWS, width), lambda i: (0, i + steps))
    act_spec = pl.BlockSpec((ROWS, HALF), lambda i: (0, 0))
    wide = pl.BlockSpec((1, width, HALF), lambda i: (0, i, 0))
    return pl.pallas_call(
        weight_grad_kernel,
        grid=(steps,),
        out_shape=(
            jax.ShapeDtypeStruct((1, D, HALF), BF16),
            jax.ShapeDtypeStruct((1, D, HALF), BF16),
            jax.ShapeDtypeStruct((1, HALF, D), BF16),
        ),
        in_specs=[x_spec, g_spec, x_spec, g_spec] + [act_spec] * 6,
        out_specs=(wide, wide, pl.BlockSpec((1, HALF, width), lambda i: (0, 0, i))),
        compiler_params=params(32),
        cost_estimate=pl.CostEstimate(
            flops=12 * ROWS * D * HALF, bytes_accessed=12 * 2**20, transcendentals=0
        ),
        name="weight_grads",
    )(own, own, other, other, *own_acts, *other_acts)


def combine_kernel(first_ref, back_ref, all_ref, mask_ref, weight_ref, out_ref):
    mask = mask_ref[...]
    weight = weight_ref[...]
    high = weight.astype(BF16)
    low = (weight - high.astype(F32)).astype(BF16)
    products = jnp.zeros((GROUP, ROWS), F32)
    for i in range(0, D, 512):
        part = back_ref[:, i : i + 512]
        total = dot(high, part, 1, 0) + dot(low, part, 1, 0)
        out_ref[:, i : i + 512] = total.astype(BF16)
        products = products + dot(all_ref[:, D + i : D + i + 512], part, 1, 1)
    for i in range(D, 2 * D, 512):
        out_ref[:, i : i + 512] = dot(mask, back_ref[:, i : i + 512], 1, 0).astype(BF16)
    meta = all_ref[:, 2 * D :].astype(F32)
    products = products * mask.astype(F32)
    lane = lax.broadcasted_iota(jnp.int32, (GROUP, ROWS), 1)
    expert_of = (first_ref[0] + lane // (PLANES * SLOTS)).astype(F32)
    place = lax.broadcasted_iota(jnp.int32, (GROUP, META), 1)
    tail = jnp.zeros((GROUP, META), F32)
    for k in range(TOP):
        hit = meta[:, k : k + 1] == expert_of
        value = jnp.sum(jnp.where(hit, products, 0.0), axis=1, keepdims=True)
        for i, piece in enumerate(three_pieces(value)):
            tail = jnp.where(place == i * TOP + k, piece.astype(F32), tail)
    out_ref[:, 2 * D :] = tail.astype(BF16)


def combine(first, back, gathered, mask, weight):
    return pl.pallas_call(
        combine_kernel,
        out_shape=jax.ShapeDtypeStruct((GROUP, COLS), BF16),
        in_specs=[SMEM] + [VMEM] * 4,
        out_specs=VMEM,
        compiler_params=params(24),
        name="combine_rows",
    )(first, back, gathered, mask, weight)


def total_kernel(in_ref, out_ref, grad_ref, route_ref):
    total = in_ref[0].astype(F32)
    for z in range(1, PLANES):
        total = total + in_ref[z].astype(F32)
    out_ref[...] = total[:, :D].astype(BF16)
    grad_ref[...] = total[:, D : 2 * D].astype(BF16)
    tail = total[:, 2 * D :].T
    route_ref[...] = tail[:TOP] + tail[TOP : 2 * TOP] + tail[2 * TOP : 3 * TOP]


def totals(arrived):
    return pl.pallas_call(
        total_kernel,
        out_shape=(
            jax.ShapeDtypeStruct((TOK, D), BF16),
            jax.ShapeDtypeStruct((TOK, D), BF16),
            jax.ShapeDtypeStruct((TOP, TOK), F32),
        ),
        in_specs=[VMEM],
        out_specs=(VMEM, VMEM, VMEM),
        compiler_params=params(16),
        name="total_rows",
    )(arrived)


def swap_cores(value):
    return lax.ppermute(value, "core", [(0, 1), (1, 0)])


def over_plane(value):
    blocks = value.reshape(CHIPS, PLANES * SLOTS, 2 * D)
    return lax.all_to_all(blocks, ("y", "x"), 0, 0, tiled=True).reshape(ROWS, 2 * D)


def over_z(value):
    return lax.all_to_all(value, "z", 0, 0, tiled=True)


def body(tokens, expert_ids, route_weight, out_grad, gate_weight, up_weight, down_weight):
    first = (lax.axis_index("z") * CHIPS).astype(jnp.int32).reshape(1)
    gathered = over_z(pack(tokens, out_grad, expert_ids.T, route_weight.T)).reshape(GROUP, COLS)
    send, mask, weight = spread(first, gathered)
    own = over_plane(send)
    other = swap_cores(own)
    own_back, *own_acts = expert(own, gate_weight, up_weight, down_weight)
    other_back, *other_acts = expert(other, gate_weight, up_weight, down_weight)
    from_other = swap_cores(other_back)
    summed = (own_back.astype(F32) + from_other.astype(F32)).astype(BF16)
    back = over_plane(summed)
    gate_grad, up_grad, down_grad = weight_grads(own, other, own_acts, other_acts)
    partial = combine(first, back, gathered, mask, weight)
    layer_out, token_grad, route_t = totals(over_z(partial.reshape(PLANES, TOK, COLS)))
    return layer_out, token_grad, route_t.T, gate_grad, up_grad, down_grad


def solution(mesh):
    fine = Mesh(mesh.devices.reshape(SIZES), AXES)
    rows, pieces = P(AXES, None), P(AXES, None, None)
    return jax.shard_map(
        body,
        mesh=fine,
        in_specs=(rows, rows, rows, rows, pieces, pieces, pieces),
        out_specs=(rows, rows, rows, pieces, pieces, pieces),
        check_vma=False,
    )
```

profile of v0, /device:TPU:32, one launch (start us, length us, event | category | flops | bytes accessed | tf_op | source)
XLA Modules:
  0.0 157.8 jit_solution(9269743065450596652)
XLA Ops:
  0.6 0.8 copy-done.13
  1.5 0.8 copy-done.14
  3.7 1.2 pack_rows.1
  4.9 8.6 %all-to-all-start = ((bf16[8,16,4224]{2,1,0:T(8,128)(2,1)}), bf16[8,16,4224]{2,1,0:T(8,128)(2,1)S(1)}, u32[]{:S(2)}, u32[]{:S(2)}) async-start(bf16[8,16,4224]{2,1,0:T(8,128)(2,1)} %pack_rows.1), calls=%async_computation | async-start | bytes 2162688 | tf_op jit(solution)/shard_map/all_to_all | solution.py:261
  13.4 28.0 %all-to-all-done = bf16[8,16,4224]{2,1,0:T(8,128)(2,1)S(1)} async-done(((bf16[8,16,4224]{2,1,0:T(8,128)(2,1)}), bf16[8,16,4224]{2,1,0:T(8,128)(2,1)S(1)}, u32[]{:S(2)}, u32[]{:S(2)}) %all-to-all-start) | async-done | bytes 1081376 | tf_op jit(solution)/shard_map/all_to_all | solution.py:261
  41.4 1.1 spread_rows.1
  42.6 33.8 %all_to_all.20 = bf16[16,16,4096]{2,1,0:T(8,128)(2,1)S(1)} all-to-all(bf16[16,16,4096]{2,1,0:T(8,128)(2,1)S(1)} %bitcast.18), channel_id=1, replica_groups=mesh['z'=8,'y'=4,'x'=4,'core'=2] {'y','x'}, dimensions={0} | all-to-all | bytes 4194304 | tf_op jit(solution)/shard_map/all_to_all | solution.py:257
  76.4 4.2 %collective-permute-done.in_ref.x_b.g_b = bf16[256,4096]{1,0:T(8,128)(2,1)S(1)} collective-permute-done((bf16[256,4096]{1,0:T(8,128)(2,1)S(1)}, bf16[256,4096]{1,0:T(8,128)(2,1)S(1)}, u32[]{:S(2)}, u32[]{:S(2)}) %collective-permute-start) | collective-permute-done | bytes 2097184 | tf_op jit(solution)/shard_map/ppermute | solution.py:252
  80.6 3.5 %expert_rows.3 = (bf16[256,4096]{1,0:T(8,128)(2,1)S(1)}, bf16[256,384]{1,0:T(8,128)(2,1)S(1)}, bf16[256,384]{1,0:T(8,128)(2,1)S(1)}, bf16[256,384]{1,0:T(8,128)(2,1)S(1)}) custom-call(bf16[256,4096]{1,0:T(8,128)(2,1)S(1)} %collective-permute-done.in_ref.x_b.g_b, bf16[1,2048,384]{2,1,0:T(8,128)(2,1)S(1)} %copy-done.17, bf16[1,2048,384]{2,1,0:T(8,128)(2,1)S(1)} %copy-done.18, ...), custom_call_target="tpu_custom_call" | custom-call | flops 2415919104 | bytes 8388608 | tf_op jit(solution)/shard_map/expert_rows/pallas_call | solution.py:144
  84.3 3.5 %expert_rows.2 = (bf16[256,4096]{1,0:T(8,128)(2,1)S(1)}, bf16[256,384]{1,0:T(8,128)(2,1)S(1)}, bf16[256,384]{1,0:T(8,128)(2,1)S(1)}, bf16[256,384]{1,0:T(8,128)(2,1)S(1)}) custom-call(bf16[256,4096]{1,0:T(8,128)(2,1)S(1)} %bitcast.11, bf16[1,2048,384]{2,1,0:T(8,128)(2,1)S(1)} %copy-done.17, bf16[1,2048,384]{2,1,0:T(8,128)(2,1)S(1)} %copy-done.18, ...), custom_call_target="tpu_custom_call" | custom-call | flops 2415919104 | bytes 8388608 | tf_op jit(solution)/shard_map/expert_rows/pallas_call | solution.py:144
  88.3 0.8 add_convert_fusion
  89.1 31.6 %all_to_all.21 = bf16[16,16,4096]{2,1,0:T(8,128)(2,1)S(1)} all-to-all(bf16[16,16,4096]{2,1,0:T(8,128)(2,1)S(1)} %bitcast.21), channel_id=1, replica_groups=mesh['z'=8,'y'=4,'x'=4,'core'=2] {'y','x'}, dimensions={0} | all-to-all | bytes 4194304 | tf_op jit(solution)/shard_map/all_to_all | solution.py:257
  120.7 1.2 combine_rows.1
  122.0 1.0 copy-done.2
  123.0 6.8 %all-to-all-start.3 = ((bf16[8,16,4224]{2,1,0:T(8,128)(2,1)}), bf16[8,16,4224]{2,1,0:T(8,128)(2,1)S(1)}, u32[]{:S(2)}, u32[]{:S(2)}) async-start(bf16[8,16,4224]{2,1,0:T(8,128)(2,1)} %bitcast.17), calls=%async_computation.3 | async-start | bytes 2162688 | tf_op jit(solution)/shard_map/all_to_all | solution.py:261
  129.8 1.6 %copy-done.1 = bf16[256,4096]{1,0:T(8,128)(2,1)S(1)} copy-done((bf16[256,4096]{1,0:T(8,128)(2,1)S(1)}, bf16[256,4096]{1,0:T(8,128)(2,1)}, u32[]{:S(2)}) %copy-start.1) | copy-done | bytes 2097176
  131.4 0.9 copy-done.4
  132.3 0.9 copy-done.6
  133.2 0.9 copy-done.8
  134.2 0.9 copy-done.10
  135.1 0.9 copy-done.12
  136.0 5.0 %weight_grads.1 = (bf16[1,2048,384]{2,1,0:T(8,128)(2,1)}, bf16[1,2048,384]{2,1,0:T(8,128)(2,1)}, bf16[1,384,2048]{2,1,0:T(8,128)(2,1)}) custom-call(bf16[256,4096]{1,0:T(8,128)(2,1)S(1)} %bitcast.12, bf16[256,4096]{1,0:T(8,128)(2,1)S(1)} %bitcast.13, bf16[256,4096]{1,0:T(8,128)(2,1)S(1)} %copy-done.1, bf16[256,4096]{1,0:T(8,128)(2,1)S(1)} %copy-done.1, ...), custom_call_target="tpu_custom_call" | custom-call | flops 2415919104 | bytes 12582912 | tf_op jit(solution)/shard_map/weight_grads/pallas_call | solution.py:170
  141.1 15.9 %all-to-all-done.3.in_ref = bf16[8,16,4224]{2,1,0:T(8,128)(2,1)S(1)} async-done(((bf16[8,16,4224]{2,1,0:T(8,128)(2,1)}), bf16[8,16,4224]{2,1,0:T(8,128)(2,1)S(1)}, u32[]{:S(2)}, u32[]{:S(2)}) %all-to-all-start.3) | async-done | bytes 1081376 | tf_op jit(solution)/shard_map/all_to_all | solution.py:261
  157.0 0.8 total_rows.1
  (34 shorter events, 2.1 us)
Async XLA Ops:
  0.6 0.8 copy-start.13
  1.5 0.8 copy-start.14
  2.3 0.7 copy-start.15
  3.0 0.7 copy-start.16
  4.9 36.5 %all-to-all-start = ((bf16[8,16,4224]{2,1,0:T(8,128)(2,1)}), bf16[8,16,4224]{2,1,0:T(8,128)(2,1)S(1)}, u32[]{:S(2)}, u32[]{:S(2)}) async-start(bf16[8,16,4224]{2,1,0:T(8,128)(2,1)} %pack_rows.1), calls=%async_computation | async-start | bytes 2162688 | tf_op jit(solution)/shard_map/all_to_all | solution.py:261
  41.4 39.1 %copy-start.19 = (bf16[1,384,2048]{2,1,0:T(8,128)(2,1)S(1)}, bf16[1,384,2048]{2,1,0:T(8,128)(2,1)}, u32[]{:S(2)}) copy-start(bf16[1,384,2048]{2,1,0:T(8,128)(2,1)} %down_ref.3) | copy-start | bytes 4718596
  42.5 38.0 %copy-start.17 = (bf16[1,2048,384]{2,1,0:T(8,128)(2,1)S(1)}, bf16[1,2048,384]{2,1,0:T(8,128)(2,1)}, u32[]{:S(2)}) copy-start(bf16[1,2048,384]{2,1,0:T(8,128)(2,1)} %gate_ref.3) | copy-start | bytes 4718596
  42.6 38.0 %copy-start.18 = (bf16[1,2048,384]{2,1,0:T(8,128)(2,1)S(1)}, bf16[1,2048,384]{2,1,0:T(8,128)(2,1)}, u32[]{:S(2)}) copy-start(bf16[1,2048,384]{2,1,0:T(8,128)(2,1)} %up_ref.3) | copy-start | bytes 4718596
  76.4 4.2 %collective-permute-start = (bf16[256,4096]{1,0:T(8,128)(2,1)S(1)}, bf16[256,4096]{1,0:T(8,128)(2,1)S(1)}, u32[]{:S(2)}, u32[]{:S(2)}) collective-permute-start(bf16[256,4096]{1,0:T(8,128)(2,1)S(1)} %bitcast.10), channel_id=1, source_target_pairs={{0,1},{1,0},{2,3},{3,2},{4,5},{5,4},{6,7},{7,6},{8,9},{9,8},{10,11... | collective-permute-start | bytes 6291464 | tf_op jit(solution)/shard_map/ppermute | solution.py:252
  80.6 3.5 %copy-start = (bf16[256,4096]{1,0:T(8,128)(2,1)}, bf16[256,4096]{1,0:T(8,128)(2,1)S(1)}, u32[]{:S(2)}) copy-start(bf16[256,4096]{1,0:T(8,128)(2,1)S(1)} %collective-permute-done.in_ref.x_b.g_b) | copy-start | bytes 6291460
  84.1 3.7 %copy-start.3 = (bf16[256,384]{1,0:T(8,128)(2,1)}, bf16[256,384]{1,0:T(8,128)(2,1)S(1)}, u32[]{:S(2)}) copy-start(bf16[256,384]{1,0:T(8,128)(2,1)S(1)} %get-tuple-element.35.p_b) | copy-start | bytes 589828
  84.1 3.7 %copy-start.5 = (bf16[256,384]{1,0:T(8,128)(2,1)}, bf16[256,384]{1,0:T(8,128)(2,1)S(1)}, u32[]{:S(2)}) copy-start(bf16[256,384]{1,0:T(8,128)(2,1)S(1)} %get-tuple-element.36.u_b) | copy-start | bytes 589828
  84.1 4.2 %collective-permute-start.1 = (bf16[256,4096]{1,0:T(8,128)(2,1)S(1)}, bf16[256,4096]{1,0:T(8,128)(2,1)S(1)}, u32[]{:S(2)}, u32[]{:S(2)}) collective-permute-start(bf16[256,4096]{1,0:T(8,128)(2,1)S(1)} %get-tuple-element.25), channel_id=1, source_target_pairs={{0,1},{1,0},{2,3},{3,2},{4,5},{5,4},{6,7},{7,6},{8,9},{9,8},{10,11... | collective-permute-start | bytes 6291464 | tf_op jit(solution)/shard_map/ppermute | solution.py:252
  87.8 1.3 copy-start.7
  87.8 1.3 copy-start.9
  87.8 1.3 copy-start.11
  122.0 1.0 copy-start.2
  123.0 34.0 %all-to-all-start.3 = ((bf16[8,16,4224]{2,1,0:T(8,128)(2,1)}), bf16[8,16,4224]{2,1,0:T(8,128)(2,1)S(1)}, u32[]{:S(2)}, u32[]{:S(2)}) async-start(bf16[8,16,4224]{2,1,0:T(8,128)(2,1)} %bitcast.17), calls=%async_computation.3 | async-start | bytes 2162688 | tf_op jit(solution)/shard_map/all_to_all | solution.py:261
  129.8 1.6 %copy-start.1 = (bf16[256,4096]{1,0:T(8,128)(2,1)S(1)}, bf16[256,4096]{1,0:T(8,128)(2,1)}, u32[]{:S(2)}) copy-start(bf16[256,4096]{1,0:T(8,128)(2,1)} %copy-done) | copy-start | bytes 6291460
  131.4 0.9 copy-start.4
  132.3 0.9 copy-start.6
  133.2 0.9 copy-start.8
  134.2 0.9 copy-start.10
  135.1 0.9 copy-start.12
where the time goes:
time: 161 us; the launch traced here: 158 us
  blocking collectives  65.4 us (41%)
  waiting for transfers between devices  48.5 us (30%)
  Pallas kernels  16.3 us (10%)
  starting transfers between devices  15.6 us (10%)
  local copies, waits for them, and re-layouts  10.3 us (6%)
    all_to_all x2, blocking collectives, over_plane(): lax.all_to_all(blocks, ('y', 'x'), 0, 0, tiled=True).reshape(ROWS, 2 * D)  65.4 us
    all_to_all x2, waiting for transfers between devices, over_z(): return lax.all_to_all(value, 'z', 0, 0, tiled=True)  43.9 us
    all_to_all x2, starting transfers between devices, over_z(): return lax.all_to_all(value, 'z', 0, 0, tiled=True)  15.4 us
    unnamed x40, local copies, waits for them, and re-layouts  10.3 us
    pallas_call x2, Pallas kernels, expert(): pl.pallas_call(expert_kernel, out_shape=(jax.ShapeDtypeStruct((ROWS, 2 *...  6.96 us
    pallas_call x1, Pallas kernels, weight_grads(): pl.pallas_call(weight_grad_kernel, grid=(steps,), out_shape=(jax.ShapeDty...  5.03 us
    ppermute x2, waiting for transfers between devices, swap_cores(): return lax.ppermute(value, 'core', [(0, 1), (1, 0)])  4.64 us
  transfers between devices with their start and end apart: 4, of which 4 were waited for; matrix products, arithmetic and copies ran while one was open for 0% of the time, Pallas kernels for 5%

commit v1 on v0

--- a/solution.py
+++ b/solution.py
@@ -20,6 +20,7 @@
 COLS = 2 * D + META
 GROUP = PLANES * TOK
 ROWS = CHIPS * PLANES * SLOTS
+BLOCKS = PLANES + 1
 F32 = jnp.float32
 BF16 = jnp.bfloat16
 VMEM = pl.BlockSpec(memory_space=pltpu.VMEM)
@@ -42,7 +43,17 @@
     return high, middle, low
 
 
-def pack_kernel(tok_ref, grad_ref, ids_ref, weight_ref, out_ref):
+def pack_kernel(tok_hbm, grad_hbm, ids_hbm, weight_hbm, out_ref, ids_ref, weight_ref, sems):
+    copies = [
+        pltpu.make_async_copy(ids_hbm, ids_ref, sems.at[0]),
+        pltpu.make_async_copy(weight_hbm, weight_ref, sems.at[1]),
+        pltpu.make_async_copy(tok_hbm, out_ref.at[:, pl.ds(0, D)], sems.at[2]),
+        pltpu.make_async_copy(grad_hbm, out_ref.at[:, pl.ds(D, D)], sems.at[3]),
+    ]
+    for copy in copies:
+        copy.start()
+    copies[0].wait()
+    copies[1].wait()
     pieces = (ids_ref[...].astype(F32).astype(BF16),) + three_pieces(weight_ref[...])
     rows = lax.broadcasted_iota(jnp.int32, (TOP, META), 0)
     lanes = lax.broadcasted_iota(jnp.int32, (TOP, META), 1)
@@ -50,25 +61,32 @@
     for i, piece in enumerate(pieces):
         place = jnp.where(lanes == rows + i * TOP, 1.0, 0.0).astype(BF16)
         meta = meta + dot(piece, place, 0, 0)
-    meta = meta.astype(BF16)
-    for z in range(PLANES):
-        out_ref[z, :, :D] = tok_ref[...]
-        out_ref[z, :, D : 2 * D] = grad_ref[...]
-        out_ref[z, :, 2 * D :] = meta
+    out_ref[:, 2 * D :] = meta.astype(BF16)
+    copies[2].wait()
+    copies[3].wait()
 
 
 def pack(tokens, out_grad, ids_t, weight_t):
     return pl.pallas_call(
         pack_kernel,
-        out_shape=jax.ShapeDtypeStruct((PLANES, TOK, COLS), BF16),
-        in_specs=[VMEM] * 4,
+        out_shape=jax.ShapeDtypeStruct((TOK, COLS), BF16),
+        in_specs=[pl.BlockSpec(memory_space=pltpu.HBM)] * 4,
         out_specs=VMEM,
-        compiler_params=params(16),
+        scratch_shapes=[
+            pltpu.VMEM((TOP, TOK), jnp.int32),
+            pltpu.VMEM((TOP, TOK), F32),
+            pltpu.SemaphoreType.DMA((4,)),
+        ],
+        compiler_params=params(4),
         name="pack_rows",
     )(tokens, out_grad, ids_t, weight_t)
 
 
-def spread_kernel(first_ref, all_ref, send_ref, mask_ref, weight_ref):
+def spread_kernel(first_ref, *refs):
+    blocks, (send_ref, all_ref, mask_ref, weight_ref) = refs[:BLOCKS], refs[BLOCKS:]
+    for j, block in enumerate(blocks[:-1]):
+        all_ref[min(j, PLANES - 1) * TOK : min(j, PLANES - 1) * TOK + TOK, : block.shape[1]] = block[...]
+    all_ref[GROUP - TOK :, D:] = blocks[-1][...]
     meta = all_ref[:, 2 * D :].astype(F32)
     shape = (GROUP, ROWS)
     lane = lax.broadcasted_iota(jnp.int32, shape, 1)
@@ -100,19 +118,20 @@
         send_ref[:, i : i + 512] = (dot(pick, all_ref[:, i : i + 512], 1, 0) * scale).astype(BF16)
 
 
-def spread(first, gathered):
+def spread(first, blocks):
     return pl.pallas_call(
         spread_kernel,
         out_shape=(
             jax.ShapeDtypeStruct((ROWS, 2 * D), BF16),
+            jax.ShapeDtypeStruct((GROUP, COLS), BF16),
             jax.ShapeDtypeStruct((GROUP, ROWS), BF16),
             jax.ShapeDtypeStruct((GROUP, ROWS), F32),
         ),
-        in_specs=[SMEM, VMEM],
-        out_specs=(VMEM, VMEM, VMEM),
-        compiler_params=params(24),
+        in_specs=[SMEM] + [VMEM] * BLOCKS,
+        out_specs=(VMEM,) * 4,
+        compiler_params=params(10),
         name="spread_rows",
-    )(first, gathered)
+    )(first, *blocks)
 
 
 def expert_kernel(in_ref, gate_ref, up_ref, down_ref, back_ref, hidden_ref, pre_ref, up_pre_ref):
@@ -146,7 +165,7 @@
         out_shape=(jax.ShapeDtypeStruct((ROWS, 2 * D), BF16), act, act, act),
         in_specs=[VMEM] * 4,
         out_specs=(VMEM,) * 4,
-        compiler_params=params(40),
+        compiler_params=params(16),
         cost_estimate=pl.CostEstimate(
             flops=12 * ROWS * D * HALF, bytes_accessed=8 * 2**20, transcendentals=ROWS * HALF
         ),
@@ -177,7 +196,7 @@
         ),
         in_specs=[x_spec, g_spec, x_spec, g_spec] + [act_spec] * 6,
         out_specs=(wide, wide, pl.BlockSpec((1, HALF, width), lambda i: (0, 0, i))),
-        compiler_params=params(32),
+        compiler_params=params(20),
         cost_estimate=pl.CostEstimate(
             flops=12 * ROWS * D * HALF, bytes_accessed=12 * 2**20, transcendentals=0
         ),
@@ -185,7 +204,17 @@
     )(own, own, other, other, *own_acts, *other_acts)
 
 
-def combine_kernel(first_ref, back_ref, all_ref, mask_ref, weight_ref, out_ref):
+def combine_kernel(first_ref, back_ref, all_ref, mask_ref, weight_ref, *out_refs):
+    def put(value, begin):
+        value = value.astype(BF16)
+        end = begin + value.shape[1]
+        for j in range(PLANES - 1):
+            out_refs[j][:, begin:end] = value[j * TOK : (j + 1) * TOK]
+        if begin < D:
+            out_refs[PLANES - 1][:, begin:end] = value[GROUP - TOK :]
+        else:
+            out_refs[PLANES][:, begin - D : end - D] = value[GROUP - TOK :]
+
     mask = mask_ref[...]
     weight = weight_ref[...]
     high = weight.astype(BF16)
@@ -193,11 +222,10 @@
     products = jnp.zeros((GROUP, ROWS), F32)
     for i in range(0, D, 512):
         part = back_ref[:, i : i + 512]
-        total = dot(high, part, 1, 0) + dot(low, part, 1, 0)
-        out_ref[:, i : i + 512] = total.astype(BF16)
+        put(dot(high, part, 1, 0) + dot(low, part, 1, 0), i)
         products = products + dot(all_ref[:, D + i : D + i + 512], part, 1, 1)
     for i in range(D, 2 * D, 512):
-        out_ref[:, i : i + 512] = dot(mask, back_ref[:, i : i + 512], 1, 0).astype(BF16)
+        put(dot(mask, back_ref[:, i : i + 512], 1, 0), i)
     meta = all_ref[:, 2 * D :].astype(F32)
     products = products * mask.astype(F32)
     lane = lax.broadcasted_iota(jnp.int32, (GROUP, ROWS), 1)
@@ -209,31 +237,55 @@
         value = jnp.sum(jnp.where(hit, products, 0.0), axis=1, keepdims=True)
         for i, piece in enumerate(three_pieces(value)):
             tail = jnp.where(place == i * TOP + k, piece.astype(F32), tail)
-    out_ref[:, 2 * D :] = tail.astype(BF16)
+    put(tail, 2 * D)
 
 
 def combine(first, back, gathered, mask, weight):
+    block = jax.ShapeDtypeStruct((TOK, COLS), BF16)
+    halves = (jax.ShapeDtypeStruct((TOK, D), BF16), jax.ShapeDtypeStruct((TOK, COLS - D), BF16))
     return pl.pallas_call(
         combine_kernel,
-        out_shape=jax.ShapeDtypeStruct((GROUP, COLS), BF16),
+        out_shape=(block,) * (PLANES - 1) + halves,
         in_specs=[SMEM] + [VMEM] * 4,
-        out_specs=VMEM,
-        compiler_params=params(24),
+        out_specs=(VMEM,) * BLOCKS,
+        compiler_params=params(10),
         name="combine_rows",
     )(first, back, gathered, mask, weight)
 
 
-def total_kernel(in_ref, out_ref, grad_ref, route_ref):
-    total = in_ref[0].astype(F32)
-    for z in range(1, PLANES):
-        total = total + in_ref[z].astype(F32)
+def relay_kernel(mine_up, next_up, first_half, mine_down, next_down, second_half, up_ref, down_ref):
+    up = mine_up[...].astype(F32) + next_up[...].astype(F32)
+    up_ref[:, D:] = up[:, D:].astype(BF16)
+    up_ref[:, :D] = (up[:, :D] + first_half[...].astype(F32)).astype(BF16)
+    down = mine_down[...].astype(F32) + next_down[...].astype(F32)
+    down_ref[:, :D] = down[:, :D].astype(BF16)
+    down_ref[:, D:] = (down[:, D:] + second_half[...].astype(F32)).astype(BF16)
+
+
+def relay(*parts):
+    block = jax.ShapeDtypeStruct((TOK, COLS), BF16)
+    return pl.pallas_call(
+        relay_kernel,
+        out_shape=(block, block),
+        in_specs=[VMEM] * 6,
+        out_specs=(VMEM, VMEM),
+        compiler_params=params(4),
+        name="relay_rows",
+    )(*parts)
+
+
+def total_kernel(*refs):
+    *in_refs, out_ref, grad_ref, route_ref = refs
+    total = in_refs[0][...].astype(F32)
+    for ref in in_refs[1:]:
+        total = total + ref[...].astype(F32)
     out_ref[...] = total[:, :D].astype(BF16)
     grad_ref[...] = total[:, D : 2 * D].astype(BF16)
     tail = total[:, 2 * D :].T
     route_ref[...] = tail[:TOP] + tail[TOP : 2 * TOP] + tail[2 * TOP : 3 * TOP]
 
 
-def totals(arrived):
+def totals(*parts):
     return pl.pallas_call(
         total_kernel,
         out_shape=(
@@ -241,11 +293,11 @@
             jax.ShapeDtypeStruct((TOK, D), BF16),
             jax.ShapeDtypeStruct((TOP, TOK), F32),
         ),
-        in_specs=[VMEM],
+        in_specs=[VMEM] * len(parts),
         out_specs=(VMEM, VMEM, VMEM),
-        compiler_params=params(16),
+        compiler_params=params(4),
         name="total_rows",
-    )(arrived)
+    )(*parts)
 
 
 def swap_cores(value):
@@ -257,14 +309,31 @@
     return lax.all_to_all(blocks, ("y", "x"), 0, 0, tiled=True).reshape(ROWS, 2 * D)
 
 
-def over_z(value):
-    return lax.all_to_all(value, "z", 0, 0, tiled=True)
+def shift(value, step):
+    return lax.ppermute(value, "z", [(i, (i + step) % PLANES) for i in range(PLANES)])
+
+
+def spread_z(own):
+    below, above = shift(own, 1), shift(own, -1)
+    below2, above2 = shift(own, 2), shift(own, -2)
+    half, other_half = shift(below2[:, :D], 2), shift(above2[:, D:], -2)
+    below3, above3 = shift(below2, 1), shift(above2, -1)
+    return own, below, above, below2, above2, below3, above3, half, other_half
+
+
+def reduce_z(blocks):
+    own, below, above, below2, above2, below3, above3, half, other_half = blocks
+    up = (above2, shift(above3, 1), shift(half, 2))
+    down = (below2, shift(below3, -1), shift(other_half, -2))
+    near = (shift(above, 1), shift(below, -1))
+    up, down = relay(*up, *down)
+    return totals(own, *near, shift(up, 2), shift(down, -2))
 
 
 def body(tokens, expert_ids, route_weight, out_grad, gate_weight, up_weight, down_weight):
     first = (lax.axis_index("z") * CHIPS).astype(jnp.int32).reshape(1)
-    gathered = over_z(pack(tokens, out_grad, expert_ids.T, route_weight.T)).reshape(GROUP, COLS)
-    send, mask, weight = spread(first, gathered)
+    blocks = spread_z(pack(tokens, out_grad, expert_ids.T, route_weight.T))
+    send, gathered, mask, weight = spread(first, blocks)
     own = over_plane(send)
     other = swap_cores(own)
     own_back, *own_acts = expert(own, gate_weight, up_weight, down_weight)
@@ -273,8 +342,7 @@
     summed = (own_back.astype(F32) + from_other.astype(F32)).astype(BF16)
     back = over_plane(summed)
     gate_grad, up_grad, down_grad = weight_grads(own, other, own_acts, other_acts)
-    partial = combine(first, back, gathered, mask, weight)
-    layer_out, token_grad, route_t = totals(over_z(partial.reshape(PLANES, TOK, COLS)))
+    layer_out, token_grad, route_t = reduce_z(combine(first, back, gathered, mask, weight))
     return layer_out, token_grad, route_t.T, gate_grad, up_grad, down_grad
 
 

time: 161 us -> 131 us (0.81); the launches traced: 158 us -> 131 us
  waiting for transfers between devices: 48.5 us -> 18.1 us
  starting transfers between devices: 15.6 us -> 28.8 us
  local copies, waits for them, and re-layouts: 10.3 us -> 3.07 us
    all_to_all x2 -> x0, waiting for transfers between devices: 43.9 us -> none  [over_z(): return lax.all_to_all(value, 'z', 0, 0, tiled=True)]
    ppermute x0 -> x16, starting transfers between devices: none -> 28.4 us  [shift(): lax.ppermute(value, 'z', [(i, (i + step) % PLANES) for i in range(PLANES)])]
    all_to_all x2 -> x0, starting transfers between devices: 15.4 us -> none  [over_z(): return lax.all_to_all(value, 'z', 0, 0, tiled=True)]
    ppermute x0 -> x16, waiting for transfers between devices: none -> 13.4 us  [shift(): lax.ppermute(value, 'z', [(i, (i + step) % PLANES) for i in range(PLANES)])]
    unnamed x40 -> x14, local copies, waits for them, and re-layouts: 10.3 us -> 3.06 us
  transfers between devices with their start and end apart: 4 -> 18, of which waited for: 4 -> 5; matrix products, arithmetic and copies ran while one was open for 0% -> 0% of each run, Pallas kernels for 5% -> 7%
where the time goes in v1:
time: 131 us
  blocking collectives  63.8 us (49%)
  starting transfers between devices  28.8 us (22%)
  waiting for transfers between devices  18.1 us (14%)
  Pallas kernels  15.5 us (12%)
  local copies, waits for them, and re-layouts  3.07 us (2%)
    all_to_all x2, blocking collectives, over_plane(): lax.all_to_all(blocks, ('y', 'x'), 0, 0, tiled=True).reshape(ROWS, 2 * D)  63.8 us
    ppermute x16, starting transfers between devices, shift(): lax.ppermute(value, 'z', [(i, (i + step) % PLANES) for i in range(PLANES)])  28.4 us
    ppermute x16, waiting for transfers between devices, shift(): lax.ppermute(value, 'z', [(i, (i + step) % PLANES) for i in range(PLANES)])  13.4 us
    pallas_call x2, Pallas kernels, expert(): pl.pallas_call(expert_kernel, out_shape=(jax.ShapeDtypeStruct((ROWS, 2 *...  6.96 us
    pallas_call x1, Pallas kernels, weight_grads(): pl.pallas_call(weight_grad_kernel, grid=(steps,), out_shape=(jax.ShapeDty...  5.02 us
    ppermute x2, waiting for transfers between devices, swap_cores(): return lax.ppermute(value, 'core', [(0, 1), (1, 0)])  4.7 us
    unnamed x14, local copies, waits for them, and re-layouts  3.06 us
  transfers between devices with their start and end apart: 18, of which 5 were waited for; matrix products, arithmetic and copies ran while one was open for 0% of the time, Pallas kernels for 7%

profile of v1, /device:TPU:32, one launch (start us, length us, event | category | flops | bytes accessed | tf_op | source)
XLA Modules:
  0.0 130.9 jit_solution(12898597180083063507)
XLA Ops:
  4.0 3.3 %collective-permute-start.2 = (bf16[16,4224]{1,0:T(8,128)(2,1)S(1)}, bf16[16,4224]{1,0:T(8,128)(2,1)S(1)}, u32[]{:S(2)}, u32[]{:S(2)}) collective-permute-start(bf16[16,4224]{1,0:T(8,128)(2,1)S(1)} %pack_rows.1.refs_0_), channel_id=1, source_target_pairs={{0,64},{32,96},{64,128},{96,160},{128,192},{160,224},{192,0},{224,... | collective-permute-start | bytes 405512 | tf_op jit(solution)/shard_map/ppermute | solution.py:313
  7.3 2.2 %collective-permute-start.3 = (bf16[16,4224]{1,0:T(8,128)(2,1)S(1)}, bf16[16,4224]{1,0:T(8,128)(2,1)S(1)}, u32[]{:S(2)}, u32[]{:S(2)}) collective-permute-start(bf16[16,4224]{1,0:T(8,128)(2,1)S(1)} %pack_rows.1.refs_0_), channel_id=1, source_target_pairs={{0,192},{32,224},{64,0},{96,32},{128,64},{160,96},{192,128},{224,1... | collective-permute-start | bytes 405512 | tf_op jit(solution)/shard_map/ppermute | solution.py:313
  9.6 0.9 collective-permute-start
  10.5 1.1 collective-permute-start.1
  11.6 4.9 %collective-permute-done.2.refs_3_ = bf16[16,4224]{1,0:T(8,128)(2,1)S(1)} collective-permute-done((bf16[16,4224]{1,0:T(8,128)(2,1)S(1)}, bf16[16,4224]{1,0:T(8,128)(2,1)S(1)}, u32[]{:S(2)}, u32[]{:S(2)}) %collective-permute-start.2) | collective-permute-done | bytes 135200 | tf_op jit(solution)/shard_map/ppermute | solution.py:313
  16.7 2.0 %collective-permute-start.5 = (bf16[16,4224]{1,0:T(8,128)(2,1)S(1)}, bf16[16,4224]{1,0:T(8,128)(2,1)S(1)}, u32[]{:S(2)}, u32[]{:S(2)}) collective-permute-start(bf16[16,4224]{1,0:T(8,128)(2,1)S(1)} %collective-permute-done.3.refs_4_), channel_id=1, source_target_pairs={{0,224},{32,0},{64,32},{96,64},{128,96},{160,128},{192,160},{224,1... | collective-permute-start | bytes 405512 | tf_op jit(solution)/shard_map/ppermute | solution.py:313
  18.7 2.9 %collective-permute-start.7 = (bf16[16,2176]{1,0:T(8,128)(2,1)S(1)}, bf16[16,2176]{1,0:T(8,128)(2,1)S(1)}, u32[]{:S(2)}, u32[]{:S(2)}) collective-permute-start(bf16[16,2176]{1,0:T(8,128)(2,1)S(1)} %slice.9), channel_id=1, source_target_pairs={{0,192},{32,224},{64,0},{96,32},{128,64},{160,96},{192,128},{224,1... | collective-permute-start | bytes 208904 | tf_op jit(solution)/shard_map/ppermute | solution.py:313
  21.6 1.4 %collective-permute-start.6 = (bf16[16,2048]{1,0:T(8,128)(2,1)S(1)}, bf16[16,2048]{1,0:T(8,128)(2,1)S(1)}, u32[]{:S(2)}, u32[]{:S(2)}) collective-permute-start(bf16[16,2048]{1,0:T(8,128)(2,1)S(1)} %slice.8), channel_id=1, source_target_pairs={{0,64},{32,96},{64,128},{96,160},{128,192},{160,224},{192,0},{224,... | collective-permute-start | bytes 196616 | tf_op jit(solution)/shard_map/ppermute | solution.py:313
  23.0 5.6 %collective-permute-done.6.refs_7_ = bf16[16,2048]{1,0:T(8,128)(2,1)S(1)} collective-permute-done((bf16[16,2048]{1,0:T(8,128)(2,1)S(1)}, bf16[16,2048]{1,0:T(8,128)(2,1)S(1)}, u32[]{:S(2)}, u32[]{:S(2)}) %collective-permute-start.6) | collective-permute-done | bytes 65568 | tf_op jit(solution)/shard_map/ppermute | solution.py:313
  28.7 1.2 spread_rows.1
  29.9 32.2 %all_to_all.10 = bf16[16,16,4096]{2,1,0:T(8,128)(2,1)S(1)} all-to-all(bf16[16,16,4096]{2,1,0:T(8,128)(2,1)S(1)} %bitcast.13), channel_id=1, replica_groups=mesh['z'=8,'y'=4,'x'=4,'core'=2] {'y','x'}, dimensions={0} | all-to-all | bytes 4194304 | tf_op jit(solution)/shard_map/all_to_all | solution.py:309
  62.1 4.2 %collective-permute-done.8.in_ref.x_b.g_b = bf16[256,4096]{1,0:T(8,128)(2,1)S(1)} collective-permute-done((bf16[256,4096]{1,0:T(8,128)(2,1)S(1)}, bf16[256,4096]{1,0:T(8,128)(2,1)S(1)}, u32[]{:S(2)}, u32[]{:S(2)}) %collective-permute-start.8) | collective-permute-done | bytes 2097184 | tf_op jit(solution)/shard_map/ppermute | solution.py:304
  66.3 3.5 %expert_rows.3 = (bf16[256,4096]{1,0:T(8,128)(2,1)S(1)}, bf16[256,384]{1,0:T(8,128)(2,1)S(1)}, bf16[256,384]{1,0:T(8,128)(2,1)S(1)}, bf16[256,384]{1,0:T(8,128)(2,1)S(1)}) custom-call(bf16[256,4096]{1,0:T(8,128)(2,1)S(1)} %collective-permute-done.8.in_ref.x_b.g_b, bf16[1,2048,384]{2,1,0:T(8,128)(2,1)S(1)} %copy-done.4, bf16[1,2048,384]{2,1,0:T(8,128)(2,1)S(1)} %copy-done.5, ...), custom_call_target="tpu_custom_call" | custom-call | flops 2415919104 | bytes 8388608 | tf_op jit(solution)/shard_map/expert_rows/pallas_call | solution.py:163
  70.1 3.5 %expert_rows.2 = (bf16[256,4096]{1,0:T(8,128)(2,1)S(1)}, bf16[256,384]{1,0:T(8,128)(2,1)S(1)}, bf16[256,384]{1,0:T(8,128)(2,1)S(1)}, bf16[256,384]{1,0:T(8,128)(2,1)S(1)}) custom-call(bf16[256,4096]{1,0:T(8,128)(2,1)S(1)} %bitcast.9, bf16[1,2048,384]{2,1,0:T(8,128)(2,1)S(1)} %copy-done.4, bf16[1,2048,384]{2,1,0:T(8,128)(2,1)S(1)} %copy-done.5, ...), custom_call_target="tpu_custom_call" | custom-call | flops 2415919104 | bytes 8388608 | tf_op jit(solution)/shard_map/expert_rows/pallas_call | solution.py:163
  75.0 31.6 %all_to_all.11 = bf16[16,16,4096]{2,1,0:T(8,128)(2,1)S(1)} all-to-all(bf16[16,16,4096]{2,1,0:T(8,128)(2,1)S(1)} %bitcast.16), channel_id=1, replica_groups=mesh['z'=8,'y'=4,'x'=4,'core'=2] {'y','x'}, dimensions={0} | all-to-all | bytes 4194304 | tf_op jit(solution)/shard_map/all_to_all | solution.py:309
  106.6 1.2 combine_rows.1
  107.8 2.1 %collective-permute-start.12 = (bf16[16,4224]{1,0:T(8,128)(2,1)S(1)}, bf16[16,4224]{1,0:T(8,128)(2,1)S(1)}, u32[]{:S(2)}, u32[]{:S(2)}) collective-permute-start(bf16[16,4224]{1,0:T(8,128)(2,1)S(1)} %get-tuple-element.45), channel_id=1, source_target_pairs={{0,32},{32,64},{64,96},{96,128},{128,160},{160,192},{192,224},{224... | collective-permute-start | bytes 405512 | tf_op jit(solution)/shard_map/ppermute | solution.py:313
  109.9 1.8 %collective-permute-start.15 = (bf16[16,2176]{1,0:T(8,128)(2,1)S(1)}, bf16[16,2176]{1,0:T(8,128)(2,1)S(1)}, u32[]{:S(2)}, u32[]{:S(2)}) collective-permute-start(bf16[16,2176]{1,0:T(8,128)(2,1)S(1)} %get-tuple-element.49), channel_id=1, source_target_pairs={{0,192},{32,224},{64,0},{96,32},{128,64},{160,96},{192,128},{224,1... | collective-permute-start | bytes 208904 | tf_op jit(solution)/shard_map/ppermute | solution.py:313
  111.7 1.1 collective-permute-start.13
  112.8 3.2 %collective-permute-start.10 = (bf16[16,4224]{1,0:T(8,128)(2,1)S(1)}, bf16[16,4224]{1,0:T(8,128)(2,1)S(1)}, u32[]{:S(2)}, u32[]{:S(2)}) collective-permute-start(bf16[16,4224]{1,0:T(8,128)(2,1)S(1)} %get-tuple-element.42), channel_id=1, source_target_pairs={{0,32},{32,64},{64,96},{96,128},{128,160},{160,192},{192,224},{224... | collective-permute-start | bytes 405512 | tf_op jit(solution)/shard_map/ppermute | solution.py:313
  116.1 2.8 %collective-permute-done.13.first_half = bf16[16,2048]{1,0:T(8,128)(2,1)S(1)} collective-permute-done((bf16[16,2048]{1,0:T(8,128)(2,1)S(1)}, bf16[16,2048]{1,0:T(8,128)(2,1)S(1)}, u32[]{:S(2)}, u32[]{:S(2)}) %collective-permute-start.13) | collective-permute-done | bytes 65568 | tf_op jit(solution)/shard_map/ppermute | solution.py:313
  118.9 1.9 %collective-permute-start.11 = (bf16[16,4224]{1,0:T(8,128)(2,1)S(1)}, bf16[16,4224]{1,0:T(8,128)(2,1)S(1)}, u32[]{:S(2)}, u32[]{:S(2)}) collective-permute-start(bf16[16,4224]{1,0:T(8,128)(2,1)S(1)} %get-tuple-element.43), channel_id=1, source_target_pairs={{0,224},{32,0},{64,32},{96,64},{128,96},{160,128},{192,160},{224,1... | collective-permute-start | bytes 405512 | tf_op jit(solution)/shard_map/ppermute | solution.py:313
  121.0 4.1 %collective-permute-start.17 = (bf16[16,4224]{1,0:T(8,128)(2,1)S(1)}, bf16[16,4224]{1,0:T(8,128)(2,1)S(1)}, u32[]{:S(2)}, u32[]{:S(2)}) collective-permute-start(bf16[16,4224]{1,0:T(8,128)(2,1)S(1)} %get-tuple-element.51), channel_id=1, source_target_pairs={{0,192},{32,224},{64,0},{96,32},{128,64},{160,96},{192,128},{224,1... | collective-permute-start | bytes 405512 | tf_op jit(solution)/shard_map/ppermute | solution.py:313
  125.1 5.0 %weight_grads.1 = (bf16[1,2048,384]{2,1,0:T(8,128)(2,1)}, bf16[1,2048,384]{2,1,0:T(8,128)(2,1)}, bf16[1,384,2048]{2,1,0:T(8,128)(2,1)}) custom-call(bf16[256,4096]{1,0:T(8,128)(2,1)S(1)} %bitcast.10, bf16[256,4096]{1,0:T(8,128)(2,1)S(1)} %bitcast.11, bf16[256,4096]{1,0:T(8,128)(2,1)S(1)} %collective-permute-done.8.in_ref.x_b.g_b, ...), custom_call_target="tpu_custom_call" | custom-call | flops 2415919104 | bytes 12582912 | tf_op jit(solution)/shard_map/weight_grads/pallas_call | solution.py:189
  (39 shorter events, 6.3 us)
Async XLA Ops:
  0.6 0.8 copy-start
  1.5 0.8 copy-start.1
  2.3 0.7 copy-start.2
  4.0 12.5 %collective-permute-start.2 = (bf16[16,4224]{1,0:T(8,128)(2,1)S(1)}, bf16[16,4224]{1,0:T(8,128)(2,1)S(1)}, u32[]{:S(2)}, u32[]{:S(2)}) collective-permute-start(bf16[16,4224]{1,0:T(8,128)(2,1)S(1)} %pack_rows.1.refs_0_), channel_id=1, source_target_pairs={{0,64},{32,96},{64,128},{96,160},{128,192},{160,224},{192,0},{224,... | collective-permute-start | bytes 405512 | tf_op jit(solution)/shard_map/ppermute | solution.py:313
  7.3 9.4 %collective-permute-start.3 = (bf16[16,4224]{1,0:T(8,128)(2,1)S(1)}, bf16[16,4224]{1,0:T(8,128)(2,1)S(1)}, u32[]{:S(2)}, u32[]{:S(2)}) collective-permute-start(bf16[16,4224]{1,0:T(8,128)(2,1)S(1)} %pack_rows.1.refs_0_), channel_id=1, source_target_pairs={{0,192},{32,224},{64,0},{96,32},{128,64},{160,96},{192,128},{224,1... | collective-permute-start | bytes 405512 | tf_op jit(solution)/shard_map/ppermute | solution.py:313
  9.6 12.1 %collective-permute-start = (bf16[16,4224]{1,0:T(8,128)(2,1)S(1)}, bf16[16,4224]{1,0:T(8,128)(2,1)S(1)}, u32[]{:S(2)}, u32[]{:S(2)}) collective-permute-start(bf16[16,4224]{1,0:T(8,128)(2,1)S(1)} %pack_rows.1.refs_0_), channel_id=1, source_target_pairs={{0,32},{32,64},{64,96},{96,128},{128,160},{160,192},{192,224},{224... | collective-permute-start | bytes 405512 | tf_op jit(solution)/shard_map/ppermute | solution.py:313
  10.5 12.5 %collective-permute-start.1 = (bf16[16,4224]{1,0:T(8,128)(2,1)S(1)}, bf16[16,4224]{1,0:T(8,128)(2,1)S(1)}, u32[]{:S(2)}, u32[]{:S(2)}) collective-permute-start(bf16[16,4224]{1,0:T(8,128)(2,1)S(1)} %pack_rows.1.refs_0_), channel_id=1, source_target_pairs={{0,224},{32,0},{64,32},{96,64},{128,96},{160,128},{192,160},{224,1... | collective-permute-start | bytes 405512 | tf_op jit(solution)/shard_map/ppermute | solution.py:313
  16.5 12.2 %collective-permute-start.4 = (bf16[16,4224]{1,0:T(8,128)(2,1)S(1)}, bf16[16,4224]{1,0:T(8,128)(2,1)S(1)}, u32[]{:S(2)}, u32[]{:S(2)}) collective-permute-start(bf16[16,4224]{1,0:T(8,128)(2,1)S(1)} %collective-permute-done.2.refs_3_), channel_id=1, source_target_pairs={{0,32},{32,64},{64,96},{96,128},{128,160},{160,192},{192,224},{224... | collective-permute-start | bytes 405512 | tf_op jit(solution)/shard_map/ppermute | solution.py:313
  16.7 11.9 %collective-permute-start.5 = (bf16[16,4224]{1,0:T(8,128)(2,1)S(1)}, bf16[16,4224]{1,0:T(8,128)(2,1)S(1)}, u32[]{:S(2)}, u32[]{:S(2)}) collective-permute-start(bf16[16,4224]{1,0:T(8,128)(2,1)S(1)} %collective-permute-done.3.refs_4_), channel_id=1, source_target_pairs={{0,224},{32,0},{64,32},{96,64},{128,96},{160,128},{192,160},{224,1... | collective-permute-start | bytes 405512 | tf_op jit(solution)/shard_map/ppermute | solution.py:313
  18.7 9.9 %collective-permute-start.7 = (bf16[16,2176]{1,0:T(8,128)(2,1)S(1)}, bf16[16,2176]{1,0:T(8,128)(2,1)S(1)}, u32[]{:S(2)}, u32[]{:S(2)}) collective-permute-start(bf16[16,2176]{1,0:T(8,128)(2,1)S(1)} %slice.9), channel_id=1, source_target_pairs={{0,192},{32,224},{64,0},{96,32},{128,64},{160,96},{192,128},{224,1... | collective-permute-start | bytes 208904 | tf_op jit(solution)/shard_map/ppermute | solution.py:313
  21.6 7.0 %collective-permute-start.6 = (bf16[16,2048]{1,0:T(8,128)(2,1)S(1)}, bf16[16,2048]{1,0:T(8,128)(2,1)S(1)}, u32[]{:S(2)}, u32[]{:S(2)}) collective-permute-start(bf16[16,2048]{1,0:T(8,128)(2,1)S(1)} %slice.8), channel_id=1, source_target_pairs={{0,64},{32,96},{64,128},{96,160},{128,192},{160,224},{192,0},{224,... | collective-permute-start | bytes 196616 | tf_op jit(solution)/shard_map/ppermute | solution.py:313
  28.6 37.6 %copy-start.6 = (bf16[1,384,2048]{2,1,0:T(8,128)(2,1)S(1)}, bf16[1,384,2048]{2,1,0:T(8,128)(2,1)}, u32[]{:S(2)}) copy-start(bf16[1,384,2048]{2,1,0:T(8,128)(2,1)} %down_ref.3) | copy-start | bytes 4718596
  29.8 36.4 %copy-start.4 = (bf16[1,2048,384]{2,1,0:T(8,128)(2,1)S(1)}, bf16[1,2048,384]{2,1,0:T(8,128)(2,1)}, u32[]{:S(2)}) copy-start(bf16[1,2048,384]{2,1,0:T(8,128)(2,1)} %gate_ref.3) | copy-start | bytes 4718596
  29.9 36.4 %copy-start.5 = (bf16[1,2048,384]{2,1,0:T(8,128)(2,1)S(1)}, bf16[1,2048,384]{2,1,0:T(8,128)(2,1)}, u32[]{:S(2)}) copy-start(bf16[1,2048,384]{2,1,0:T(8,128)(2,1)} %up_ref.3) | copy-start | bytes 4718596
  62.1 4.2 %collective-permute-start.8 = (bf16[256,4096]{1,0:T(8,128)(2,1)S(1)}, bf16[256,4096]{1,0:T(8,128)(2,1)S(1)}, u32[]{:S(2)}, u32[]{:S(2)}) collective-permute-start(bf16[256,4096]{1,0:T(8,128)(2,1)S(1)} %bitcast.8), channel_id=1, source_target_pairs={{0,1},{1,0},{2,3},{3,2},{4,5},{5,4},{6,7},{7,6},{8,9},{9,8},{10,11... | collective-permute-start | bytes 6291464 | tf_op jit(solution)/shard_map/ppermute | solution.py:304
  69.7 4.4 %collective-permute-start.9 = (bf16[256,4096]{1,0:T(8,128)(2,1)S(1)}, bf16[256,4096]{1,0:T(8,128)(2,1)S(1)}, u32[]{:S(2)}, u32[]{:S(2)}) collective-permute-start(bf16[256,4096]{1,0:T(8,128)(2,1)S(1)} %get-tuple-element.37), channel_id=1, source_target_pairs={{0,1},{1,0},{2,3},{3,2},{4,5},{5,4},{6,7},{7,6},{8,9},{9,8},{10,11... | collective-permute-start | bytes 6291464 | tf_op jit(solution)/shard_map/ppermute | solution.py:304
  107.8 13.0 %collective-permute-start.12 = (bf16[16,4224]{1,0:T(8,128)(2,1)S(1)}, bf16[16,4224]{1,0:T(8,128)(2,1)S(1)}, u32[]{:S(2)}, u32[]{:S(2)}) collective-permute-start(bf16[16,4224]{1,0:T(8,128)(2,1)S(1)} %get-tuple-element.45), channel_id=1, source_target_pairs={{0,32},{32,64},{64,96},{96,128},{128,160},{160,192},{192,224},{224... | collective-permute-start | bytes 405512 | tf_op jit(solution)/shard_map/ppermute | solution.py:313
  109.9 10.9 %collective-permute-start.14 = (bf16[16,4224]{1,0:T(8,128)(2,1)S(1)}, bf16[16,4224]{1,0:T(8,128)(2,1)S(1)}, u32[]{:S(2)}, u32[]{:S(2)}) collective-permute-start(bf16[16,4224]{1,0:T(8,128)(2,1)S(1)} %get-tuple-element.48), channel_id=1, source_target_pairs={{0,224},{32,0},{64,32},{96,64},{128,96},{160,128},{192,160},{224,1... | collective-permute-start | bytes 405512 | tf_op jit(solution)/shard_map/ppermute | solution.py:313
  109.9 10.9 %collective-permute-start.15 = (bf16[16,2176]{1,0:T(8,128)(2,1)S(1)}, bf16[16,2176]{1,0:T(8,128)(2,1)S(1)}, u32[]{:S(2)}, u32[]{:S(2)}) collective-permute-start(bf16[16,2176]{1,0:T(8,128)(2,1)S(1)} %get-tuple-element.49), channel_id=1, source_target_pairs={{0,192},{32,224},{64,0},{96,32},{128,64},{160,96},{192,128},{224,1... | collective-permute-start | bytes 208904 | tf_op jit(solution)/shard_map/ppermute | solution.py:313
  111.7 7.2 %collective-permute-start.13 = (bf16[16,2048]{1,0:T(8,128)(2,1)S(1)}, bf16[16,2048]{1,0:T(8,128)(2,1)S(1)}, u32[]{:S(2)}, u32[]{:S(2)}) collective-permute-start(bf16[16,2048]{1,0:T(8,128)(2,1)S(1)} %get-tuple-element.46), channel_id=1, source_target_pairs={{0,64},{32,96},{64,128},{96,160},{128,192},{160,224},{192,0},{224,... | collective-permute-start | bytes 196616 | tf_op jit(solution)/shard_map/ppermute | solution.py:313
  112.8 17.3 %collective-permute-start.10 = (bf16[16,4224]{1,0:T(8,128)(2,1)S(1)}, bf16[16,4224]{1,0:T(8,128)(2,1)S(1)}, u32[]{:S(2)}, u32[]{:S(2)}) collective-permute-start(bf16[16,4224]{1,0:T(8,128)(2,1)S(1)} %get-tuple-element.42), channel_id=1, source_target_pairs={{0,32},{32,64},{64,96},{96,128},{128,160},{160,192},{192,224},{224... | collective-permute-start | bytes 405512 | tf_op jit(solution)/shard_map/ppermute | solution.py:313
  118.9 11.2 %collective-permute-start.11 = (bf16[16,4224]{1,0:T(8,128)(2,1)S(1)}, bf16[16,4224]{1,0:T(8,128)(2,1)S(1)}, u32[]{:S(2)}, u32[]{:S(2)}) collective-permute-start(bf16[16,4224]{1,0:T(8,128)(2,1)S(1)} %get-tuple-element.43), channel_id=1, source_target_pairs={{0,224},{32,0},{64,32},{96,64},{128,96},{160,128},{192,160},{224,1... | collective-permute-start | bytes 405512 | tf_op jit(solution)/shard_map/ppermute | solution.py:313
  120.9 9.2 %collective-permute-start.16 = (bf16[16,4224]{1,0:T(8,128)(2,1)S(1)}, bf16[16,4224]{1,0:T(8,128)(2,1)S(1)}, u32[]{:S(2)}, u32[]{:S(2)}) collective-permute-start(bf16[16,4224]{1,0:T(8,128)(2,1)S(1)} %get-tuple-element.50), channel_id=1, source_target_pairs={{0,64},{32,96},{64,128},{96,160},{128,192},{160,224},{192,0},{224,... | collective-permute-start | bytes 405512 | tf_op jit(solution)/shard_map/ppermute | solution.py:313
  121.0 9.2 %collective-permute-start.17 = (bf16[16,4224]{1,0:T(8,128)(2,1)S(1)}, bf16[16,4224]{1,0:T(8,128)(2,1)S(1)}, u32[]{:S(2)}, u32[]{:S(2)}) collective-permute-start(bf16[16,4224]{1,0:T(8,128)(2,1)S(1)} %get-tuple-element.51), channel_id=1, source_target_pairs={{0,192},{32,224},{64,0},{96,32},{128,64},{160,96},{192,128},{224,1... | collective-permute-start | bytes 405512 | tf_op jit(solution)/shard_map/ppermute | solution.py:313
  (1 other events, 0.7 us)

commit v2 on v1

--- a/solution.py
+++ b/solution.py
@@ -19,7 +19,8 @@
 META = 128
 COLS = 2 * D + META
 GROUP = PLANES * TOK
-ROWS = CHIPS * PLANES * SLOTS
+SENT = PLANES * SLOTS
+ROWS = CHIPS * SENT
 BLOCKS = PLANES + 1
 F32 = jnp.float32
 BF16 = jnp.bfloat16
@@ -77,7 +78,7 @@
             pltpu.VMEM((TOP, TOK), F32),
             pltpu.SemaphoreType.DMA((4,)),
         ],
-        compiler_params=params(4),
+        compiler_params=params(63),
         name="pack_rows",
     )(tokens, out_grad, ids_t, weight_t)
 
@@ -113,16 +114,17 @@
     pick = mask.T.astype(BF16)
     scale = jnp.sum(weight.T, axis=1, keepdims=True)
     for i in range(0, D, 512):
-        send_ref[:, i : i + 512] = dot(pick, all_ref[:, i : i + 512], 1, 0).astype(BF16)
-    for i in range(D, 2 * D, 512):
-        send_ref[:, i : i + 512] = (dot(pick, all_ref[:, i : i + 512], 1, 0) * scale).astype(BF16)
+        picked = dot(pick, all_ref[:, i : i + 512], 1, 0)
+        send_ref[:, :SENT, i : i + 512] = picked.astype(BF16).reshape(CHIPS, SENT, 512)
+        picked = dot(pick, all_ref[:, D + i : D + i + 512], 1, 0) * scale
+        send_ref[:, SENT:, i : i + 512] = picked.astype(BF16).reshape(CHIPS, SENT, 512)
 
 
 def spread(first, blocks):
     return pl.pallas_call(
         spread_kernel,
         out_shape=(
-            jax.ShapeDtypeStruct((ROWS, 2 * D), BF16),
+            jax.ShapeDtypeStruct((CHIPS, 2 * SENT, D), BF16),
             jax.ShapeDtypeStruct((GROUP, COLS), BF16),
             jax.ShapeDtypeStruct((GROUP, ROWS), BF16),
             jax.ShapeDtypeStruct((GROUP, ROWS), F32),
@@ -134,43 +136,77 @@
     )(first, *blocks)
 
 
-def expert_kernel(in_ref, gate_ref, up_ref, down_ref, back_ref, hidden_ref, pre_ref, up_pre_ref):
-    w_gate = gate_ref[0]
-    w_up = up_ref[0]
-    w_down = down_ref[0]
-    rows = in_ref[:, :D]
-    gate = dot(rows, w_gate, 1, 0)
-    up = dot(rows, w_up, 1, 0)
+def forward_kernel(in_ref, gate_ref, up_ref, down_ref, back_ref, hidden_ref, gate_out, up_out):
+    rows = in_ref[...]
+    gate = dot(rows, gate_ref[0], 1, 0)
+    up = dot(rows, up_ref[0], 1, 0)
+    gate_out[...] = gate
+    up_out[...] = up
+    hidden = (gate * jax.nn.sigmoid(gate) * up).astype(BF16)
+    hidden_ref[...] = hidden
+    for i in range(0, D, 512):
+        back_ref[:, i : i + 512] = dot(hidden, down_ref[0, :, i : i + 512], 1, 0).astype(BF16)
+
+
+def backward_kernel(in_ref, gate_in, up_in, gate_ref, up_ref, down_ref, back_ref, pre_ref, up_pre_ref):
+    gate = gate_in[...]
     sig = jax.nn.sigmoid(gate)
-    act = gate * sig
-    hidden = (act * up).astype(BF16)
-    hidden_ref[...] = hidden
-    hidden_grad = dot(in_ref[:, D:], w_down, 1, 1)
-    pre = (hidden_grad * up * sig * (1.0 + gate * (1.0 - sig))).astype(BF16)
-    up_pre = (hidden_grad * act).astype(BF16)
+    hidden_grad = dot(in_ref[...], down_ref[0], 1, 1)
+    pre = (hidden_grad * up_in[...] * sig * (1.0 + gate * (1.0 - sig))).astype(BF16)
+    up_pre = (hidden_grad * gate * sig).astype(BF16)
     pre_ref[...] = pre
     up_pre_ref[...] = up_pre
     for i in range(0, D, 512):
-        back_ref[:, i : i + 512] = dot(hidden, down_ref[0, :, i : i + 512], 1, 0).astype(BF16)
-    for i in range(0, D, 512):
-        back_ref[:, D + i : D + i + 512] = (
+        back_ref[:, i : i + 512] = (
             dot(pre, gate_ref[0, i : i + 512, :], 1, 1) + dot(up_pre, up_ref[0, i : i + 512, :], 1, 1)
         ).astype(BF16)
 
 
-def expert(rows, gate_weight, up_weight, down_weight):
-    act = jax.ShapeDtypeStruct((ROWS, HALF), BF16)
-    return pl.pallas_call(
-        expert_kernel,
-        out_shape=(jax.ShapeDtypeStruct((ROWS, 2 * D), BF16), act, act, act),
+COST = pl.CostEstimate(flops=6 * ROWS * D * HALF, bytes_accessed=5 * 2**20, transcendentals=ROWS * HALF)
+WIDE = jax.ShapeDtypeStruct((ROWS, D), BF16)
+ACT = jax.ShapeDtypeStruct((ROWS, HALF), BF16)
+ACT32 = jax.ShapeDtypeStruct((ROWS, HALF), F32)
+
+
+def forward(rows, weights):
+    return pl.pallas_call(
+        forward_kernel,
+        out_shape=(WIDE, ACT, ACT32, ACT32),
         in_specs=[VMEM] * 4,
         out_specs=(VMEM,) * 4,
         compiler_params=params(16),
-        cost_estimate=pl.CostEstimate(
-            flops=12 * ROWS * D * HALF, bytes_accessed=8 * 2**20, transcendentals=ROWS * HALF
-        ),
-        name="expert_rows",
-    )(rows, gate_weight, up_weight, down_weight)
+        cost_estimate=COST,
+        name="forward_rows",
+    )(rows, *weights)
+
+
+def backward(rows, gate, up, weights):
+    return pl.pallas_call(
+        backward_kernel,
+        out_shape=(WIDE, ACT, ACT),
+        in_specs=[VMEM] * 6,
+        out_specs=(VMEM,) * 3,
+        compiler_params=params(16),
+        cost_estimate=COST,
+        name="backward_rows",
+    )(rows, gate, up, *weights)
+
+
+def pair_sum_kernel(out_a, out_b, grad_a, grad_b, sum_ref):
+    for begin, a_ref, b_ref in ((0, out_a, out_b), (SENT, grad_a, grad_b)):
+        total = a_ref[...].astype(F32) + b_ref[...].astype(F32)
+        sum_ref[:, begin : begin + SENT, :] = total.astype(BF16).reshape(CHIPS, SENT, D)
+
+
+def pair_sum(*parts):
+    return pl.pallas_call(
+        pair_sum_kernel,
+        out_shape=jax.ShapeDtypeStruct((CHIPS, 2 * SENT, D), BF16),
+        in_specs=[VMEM] * 4,
+        out_specs=VMEM,
+        compiler_params=params(12),
+        name="sum_halves",
+    )(*parts)
 
 
 def weight_grad_kernel(x_a, g_a, x_b, g_b, h_a, p_a, u_a, h_b, p_b, u_b, gate_ref, up_ref, down_ref):
@@ -179,11 +215,10 @@
     down_ref[0] = (dot(h_a[...], g_a[...], 0, 0) + dot(h_b[...], g_b[...], 0, 0)).astype(BF16)
 
 
-def weight_grads(own, other, own_acts, other_acts):
+def weight_grads(own_rows, own_grads, other_rows, other_grads, own_acts, other_acts):
     width = 512
     steps = D // width
     x_spec = pl.BlockSpec((ROWS, width), lambda i: (0, i))
-    g_spec = pl.BlockSpec((ROWS, width), lambda i: (0, i + steps))
     act_spec = pl.BlockSpec((ROWS, HALF), lambda i: (0, 0))
     wide = pl.BlockSpec((1, width, HALF), lambda i: (0, i, 0))
     return pl.pallas_call(
@@ -194,26 +229,29 @@
             jax.ShapeDtypeStruct((1, D, HALF), BF16),
             jax.ShapeDtypeStruct((1, HALF, D), BF16),
         ),
-        in_specs=[x_spec, g_spec, x_spec, g_spec] + [act_spec] * 6,
+        in_specs=[x_spec] * 4 + [act_spec] * 6,
         out_specs=(wide, wide, pl.BlockSpec((1, HALF, width), lambda i: (0, 0, i))),
         compiler_params=params(20),
         cost_estimate=pl.CostEstimate(
             flops=12 * ROWS * D * HALF, bytes_accessed=12 * 2**20, transcendentals=0
         ),
         name="weight_grads",
-    )(own, own, other, other, *own_acts, *other_acts)
+    )(own_rows, own_grads, other_rows, other_grads, *own_acts, *other_acts)
 
 
 def combine_kernel(first_ref, back_ref, all_ref, mask_ref, weight_ref, *out_refs):
+    own, below2, above2, down_pair, up_pair, half, other_half = out_refs
+    places = ((own, 0), (down_pair, TOK), (up_pair, TOK), (below2, 0), (above2, 0), (down_pair, 0), (up_pair, 0))
+
     def put(value, begin):
         value = value.astype(BF16)
         end = begin + value.shape[1]
-        for j in range(PLANES - 1):
-            out_refs[j][:, begin:end] = value[j * TOK : (j + 1) * TOK]
+        for j, (ref, row) in enumerate(places):
+            ref[row : row + TOK, begin:end] = value[j * TOK : (j + 1) * TOK]
         if begin < D:
-            out_refs[PLANES - 1][:, begin:end] = value[GROUP - TOK :]
+            half[:, begin:end] = value[GROUP - TOK :]
         else:
-            out_refs[PLANES][:, begin - D : end - D] = value[GROUP - TOK :]
+            other_half[:, begin - D : end - D] = value[GROUP - TOK :]
 
     mask = mask_ref[...]
     weight = weight_ref[...]
@@ -221,11 +259,10 @@
     low = (weight - high.astype(F32)).astype(BF16)
     products = jnp.zeros((GROUP, ROWS), F32)
     for i in range(0, D, 512):
-        part = back_ref[:, i : i + 512]
+        part = back_ref[:, :SENT, i : i + 512].reshape(ROWS, 512)
         put(dot(high, part, 1, 0) + dot(low, part, 1, 0), i)
         products = products + dot(all_ref[:, D + i : D + i + 512], part, 1, 1)
-    for i in range(D, 2 * D, 512):
-        put(dot(mask, back_ref[:, i : i + 512], 1, 0), i)
+        put(dot(mask, back_ref[:, SENT:, i : i + 512].reshape(ROWS, 512), 1, 0), D + i)
     meta = all_ref[:, 2 * D :].astype(F32)
     products = products * mask.astype(F32)
     lane = lax.broadcasted_iota(jnp.int32, (GROUP, ROWS), 1)
@@ -242,22 +279,23 @@
 
 def combine(first, back, gathered, mask, weight):
     block = jax.ShapeDtypeStruct((TOK, COLS), BF16)
+    pair = jax.ShapeDtypeStruct((2 * TOK, COLS), BF16)
     halves = (jax.ShapeDtypeStruct((TOK, D), BF16), jax.ShapeDtypeStruct((TOK, COLS - D), BF16))
     return pl.pallas_call(
         combine_kernel,
-        out_shape=(block,) * (PLANES - 1) + halves,
+        out_shape=(block, block, block, pair, pair) + halves,
         in_specs=[SMEM] + [VMEM] * 4,
-        out_specs=(VMEM,) * BLOCKS,
+        out_specs=(VMEM,) * 7,
         compiler_params=params(10),
         name="combine_rows",
     )(first, back, gathered, mask, weight)
 
 
 def relay_kernel(mine_up, next_up, first_half, mine_down, next_down, second_half, up_ref, down_ref):
-    up = mine_up[...].astype(F32) + next_up[...].astype(F32)
+    up = mine_up[...].astype(F32) + next_up[:TOK].astype(F32)
     up_ref[:, D:] = up[:, D:].astype(BF16)
     up_ref[:, :D] = (up[:, :D] + first_half[...].astype(F32)).astype(BF16)
-    down = mine_down[...].astype(F32) + next_down[...].astype(F32)
+    down = mine_down[...].astype(F32) + next_down[:TOK].astype(F32)
     down_ref[:, :D] = down[:, :D].astype(BF16)
     down_ref[:, D:] = (down[:, D:] + second_half[...].astype(F32)).astype(BF16)
 
@@ -278,7 +316,7 @@
     *in_refs, out_ref, grad_ref, route_ref = refs
     total = in_refs[0][...].astype(F32)
     for ref in in_refs[1:]:
-        total = total + ref[...].astype(F32)
+        total = total + ref[ref.shape[0] - TOK :].astype(F32)
     out_ref[...] = total[:, :D].astype(BF16)
     grad_ref[...] = total[:, D : 2 * D].astype(BF16)
     tail = total[:, 2 * D :].T
@@ -304,9 +342,8 @@
     return lax.ppermute(value, "core", [(0, 1), (1, 0)])
 
 
-def over_plane(value):
-    blocks = value.reshape(CHIPS, PLANES * SLOTS, 2 * D)
-    return lax.all_to_all(blocks, ("y", "x"), 0, 0, tiled=True).reshape(ROWS, 2 * D)
+def over_plane(blocks):
+    return lax.all_to_all(blocks, ("y", "x"), 0, 0, tiled=True)
 
 
 def shift(value, step):
@@ -321,28 +358,32 @@
     return own, below, above, below2, above2, below3, above3, half, other_half
 
 
-def reduce_z(blocks):
-    own, below, above, below2, above2, below3, above3, half, other_half = blocks
-    up = (above2, shift(above3, 1), shift(half, 2))
-    down = (below2, shift(below3, -1), shift(other_half, -2))
-    near = (shift(above, 1), shift(below, -1))
-    up, down = relay(*up, *down)
-    return totals(own, *near, shift(up, 2), shift(down, -2))
+def reduce_z(own, below2, above2, down_pair, up_pair, half, other_half):
+    from_above, from_below = shift(down_pair, -1), shift(up_pair, 1)
+    up, down = relay(above2, from_below, shift(half, 2), below2, from_above, shift(other_half, -2))
+    return totals(own, from_above, from_below, shift(up, 2), shift(down, -2))
 
 
 def body(tokens, expert_ids, route_weight, out_grad, gate_weight, up_weight, down_weight):
     first = (lax.axis_index("z") * CHIPS).astype(jnp.int32).reshape(1)
+    weights = (gate_weight, up_weight, down_weight)
     blocks = spread_z(pack(tokens, out_grad, expert_ids.T, route_weight.T))
     send, gathered, mask, weight = spread(first, blocks)
-    own = over_plane(send)
-    other = swap_cores(own)
-    own_back, *own_acts = expert(own, gate_weight, up_weight, down_weight)
-    other_back, *other_acts = expert(other, gate_weight, up_weight, down_weight)
-    from_other = swap_cores(other_back)
-    summed = (own_back.astype(F32) + from_other.astype(F32)).astype(BF16)
+    arrived = over_plane(send)
+    rows = arrived[:, :SENT].reshape(ROWS, D)
+    grads = arrived[:, SENT:].reshape(ROWS, D)
+    other_rows, other_grads = swap_cores(rows), swap_cores(grads)
+    out_a, hidden_a, gate_a, up_a = forward(rows, weights)
+    hidden_a, other_rows = lax.optimization_barrier((hidden_a, other_rows))
+    out_b, hidden_b, gate_b, up_b = forward(other_rows, weights)
+    grad_b, pre_b, up_pre_b = backward(other_grads, gate_b, up_b, weights)
+    grad_a, pre_a, up_pre_a = backward(grads, gate_a, up_a, weights)
+    summed = pair_sum(out_a, swap_cores(out_b), grad_a, swap_cores(grad_b))
     back = over_plane(summed)
-    gate_grad, up_grad, down_grad = weight_grads(own, other, own_acts, other_acts)
-    layer_out, token_grad, route_t = reduce_z(combine(first, back, gathered, mask, weight))
+    gate_grad, up_grad, down_grad = weight_grads(
+        rows, grads, other_rows, other_grads, (hidden_a, pre_a, up_pre_a), (hidden_b, pre_b, up_pre_b)
+    )
+    layer_out, token_grad, route_t = reduce_z(*combine(first, back, gathered, mask, weight))
     return layer_out, token_grad, route_t.T, gate_grad, up_grad, down_grad
 
 

time: 131 us -> 130 us (level); the launches traced: 131 us -> 128 us
  starting transfers between devices: 28.8 us -> 24.7 us
  Pallas kernels: 15.5 us -> 18 us
    ppermute x16 -> x14, starting transfers between devices: 28.4 us -> 23.5 us  [shift(): lax.ppermute(value, 'z', [(i, (i + step) % PLANES) for i in range(PLANES)])]
    ppermute x2 -> x4, waiting for transfers between devices: 4.7 us -> 0.32 us  [swap_cores(): return lax.ppermute(value, 'core', [(0, 1), (1, 0)])]
    ppermute x16 -> x14, waiting for transfers between devices: 13.4 us -> 17.6 us  [shift(): lax.ppermute(value, 'z', [(i, (i + step) % PLANES) for i in range(PLANES)])]
    pallas_call x4 -> x7, Pallas kernels: 9.36 us -> 10.5 us  [the longest x2 3.92 us: backward(): pl.pallas_call(backward_kernel, out_shape=(WIDE, ACT, ACT), in_specs=[VME...]
    unnamed x14 -> x8, local copies, waits for them, and re-layouts: 3.06 us -> 1.94 us
  transfers between devices with their start and end apart: 18 -> 18, of which waited for: 5 -> 4; matrix products, arithmetic and copies ran while one was open for 0% -> 0% of each run, Pallas kernels for 7% -> 10%
where the time goes in v2:
time: 130 us; the launch traced here: 128 us
  blocking collectives  64.1 us (49%)
  starting transfers between devices  24.7 us (19%)
  Pallas kernels  18 us (14%)
  waiting for transfers between devices  17.9 us (14%)
  local copies, waits for them, and re-layouts  2.19 us (2%)
    all_to_all x2, blocking collectives, over_plane(): return lax.all_to_all(blocks, ('y', 'x'), 0, 0, tiled=True)  64.1 us
    ppermute x14, starting transfers between devices, shift(): lax.ppermute(value, 'z', [(i, (i + step) % PLANES) for i in range(PLANES)])  23.5 us
    ppermute x14, waiting for transfers between devices, shift(): lax.ppermute(value, 'z', [(i, (i + step) % PLANES) for i in range(PLANES)])  17.6 us
    pallas_call x1, Pallas kernels, weight_grads(): pl.pallas_call(weight_grad_kernel, grid=(steps,), out_shape=(jax.ShapeDty...  5 us
    pallas_call x2, Pallas kernels, backward(): pl.pallas_call(backward_kernel, out_shape=(WIDE, ACT, ACT), in_specs=[VME...  3.92 us
    pallas_call x2, Pallas kernels, forward(): pl.pallas_call(forward_kernel, out_shape=(WIDE, ACT, ACT32, ACT32), in_sp...  3.74 us
  transfers between devices with their start and end apart: 18, of which 4 were waited for; matrix products, arithmetic and copies ran while one was open for 0% of the time, Pallas kernels for 10%

profile of v2, /device:TPU:32, one launch (start us, length us, event | category | flops | bytes accessed | tf_op | source)
XLA Modules:
  0.0 127.7 jit_solution(14642642634063030213)
XLA Ops:
  0.6 1.6 %pack_rows.1.refs_0_ = bf16[16,4224]{1,0:T(8,128)(2,1)} custom-call(bf16[16,2048]{1,0:T(8,128)(2,1)} %tok_hbm.1, bf16[16,2048]{1,0:T(8,128)(2,1)} %grad_hbm.1, s32[8,16]{1,0:T(8,128)} %bitcast.12, f32[8,16]{1,0:T(8,128)} %bitcast.13), custom_call_target="tpu_custom_call" | custom-call | tf_op jit(solution)/shard_map/pack_rows/pallas_call | solution.py:71
  2.2 3.3 %collective-permute-start.2 = (bf16[16,4224]{1,0:T(8,128)(2,1)}, bf16[16,4224]{1,0:T(8,128)(2,1)S(1)}, u32[]{:S(2)}, u32[]{:S(2)}) collective-permute-start(bf16[16,4224]{1,0:T(8,128)(2,1)} %pack_rows.1.refs_0_), channel_id=1, source_target_pairs={{0,64},{32,96},{64,128},{96,160},{128,192},{160,224},{192,0},{224,... | collective-permute-start | bytes 405512 | tf_op jit(solution)/shard_map/ppermute | solution.py:350
  5.6 2.2 %collective-permute-start.3 = (bf16[16,4224]{1,0:T(8,128)(2,1)}, bf16[16,4224]{1,0:T(8,128)(2,1)S(1)}, u32[]{:S(2)}, u32[]{:S(2)}) collective-permute-start(bf16[16,4224]{1,0:T(8,128)(2,1)} %pack_rows.1.refs_0_), channel_id=1, source_target_pairs={{0,192},{32,224},{64,0},{96,32},{128,64},{160,96},{192,128},{224,1... | collective-permute-start | bytes 405512 | tf_op jit(solution)/shard_map/ppermute | solution.py:350
  8.7 1.1 collective-permute-start.1
  9.8 5.1 %collective-permute-done.2.refs_3_ = bf16[16,4224]{1,0:T(8,128)(2,1)S(1)} collective-permute-done((bf16[16,4224]{1,0:T(8,128)(2,1)}, bf16[16,4224]{1,0:T(8,128)(2,1)S(1)}, u32[]{:S(2)}, u32[]{:S(2)}) %collective-permute-start.2) | collective-permute-done | bytes 135200 | tf_op jit(solution)/shard_map/ppermute | solution.py:350
  15.3 1.9 %collective-permute-start.5 = (bf16[16,4224]{1,0:T(8,128)(2,1)S(1)}, bf16[16,4224]{1,0:T(8,128)(2,1)S(1)}, u32[]{:S(2)}, u32[]{:S(2)}) collective-permute-start(bf16[16,4224]{1,0:T(8,128)(2,1)S(1)} %collective-permute-done.3.refs_4_), channel_id=1, source_target_pairs={{0,224},{32,0},{64,32},{96,64},{128,96},{160,128},{192,160},{224,1... | collective-permute-start | bytes 405512 | tf_op jit(solution)/shard_map/ppermute | solution.py:350
  17.2 2.8 %collective-permute-start.7 = (bf16[16,2176]{1,0:T(8,128)(2,1)S(1)}, bf16[16,2176]{1,0:T(8,128)(2,1)S(1)}, u32[]{:S(2)}, u32[]{:S(2)}) collective-permute-start(bf16[16,2176]{1,0:T(8,128)(2,1)S(1)} %slice.17), channel_id=1, source_target_pairs={{0,192},{32,224},{64,0},{96,32},{128,64},{160,96},{192,128},{224,1... | collective-permute-start | bytes 208904 | tf_op jit(solution)/shard_map/ppermute | solution.py:350
  20.0 1.4 %collective-permute-start.6 = (bf16[16,2048]{1,0:T(8,128)(2,1)S(1)}, bf16[16,2048]{1,0:T(8,128)(2,1)S(1)}, u32[]{:S(2)}, u32[]{:S(2)}) collective-permute-start(bf16[16,2048]{1,0:T(8,128)(2,1)S(1)} %slice.16), channel_id=1, source_target_pairs={{0,64},{32,96},{64,128},{96,160},{128,192},{160,224},{192,0},{224,... | collective-permute-start | bytes 196616 | tf_op jit(solution)/shard_map/ppermute | solution.py:350
  21.5 5.5 %collective-permute-done.6.refs_7_ = bf16[16,2048]{1,0:T(8,128)(2,1)S(1)} collective-permute-done((bf16[16,2048]{1,0:T(8,128)(2,1)S(1)}, bf16[16,2048]{1,0:T(8,128)(2,1)S(1)}, u32[]{:S(2)}, u32[]{:S(2)}) %collective-permute-start.6) | collective-permute-done | bytes 65568 | tf_op jit(solution)/shard_map/ppermute | solution.py:350
  27.9 1.2 spread_rows.1
  29.1 32.2 %all_to_all.10 = bf16[16,32,2048]{2,1,0:T(8,128)(2,1)S(1)} all-to-all(bf16[16,32,2048]{2,1,0:T(8,128)(2,1)S(1)} %get-tuple-element.41), channel_id=1, replica_groups=mesh['z'=8,'y'=4,'x'=4,'core'=2] {'y','x'}, dimensions={0} | all-to-all | bytes 4194304 | tf_op jit(solution)/shard_map/all_to_all | solution.py:346
  63.2 1.9 %forward_rows.2 = (bf16[256,2048]{1,0:T(8,128)(2,1)S(1)}, bf16[256,384]{1,0:T(8,128)(2,1)S(1)}, f32[256,384]{1,0:T(8,128)S(1)}, f32[256,384]{1,0:T(8,128)S(1)}) custom-call(bf16[256,2048]{1,0:T(8,128)(2,1)S(1)} %bitcast.10, bf16[1,2048,384]{2,1,0:T(8,128)(2,1)S(1)} %copy-done, bf16[1,2048,384]{2,1,0:T(8,128)(2,1)S(1)} %copy-done.1, ...), custom_call_target="tpu_custom_call" | custom-call | flops 1207959552 | bytes 5242880 | tf_op jit(solution)/shard_map/forward_rows/pallas_call | solution.py:172
  65.0 1.9 %forward_rows.3 = (bf16[256,2048]{1,0:T(8,128)(2,1)S(1)}, bf16[256,384]{1,0:T(8,128)(2,1)S(1)}, f32[256,384]{1,0:T(8,128)S(1)}, f32[256,384]{1,0:T(8,128)S(1)}) custom-call(bf16[256,2048]{1,0:T(8,128)(2,1)S(1)} %collective-permute-done.8.in_ref.x_b, bf16[1,2048,384]{2,1,0:T(8,128)(2,1)S(1)} %copy-done, bf16[1,2048,384]{2,1,0:T(8,128)(2,1)S(1)} %copy-done.1, ...), custom_call_target="tpu_custom_call" | custom-call | flops 1207959552 | bytes 5242880 | tf_op jit(solution)/shard_map/forward_rows/pallas_call | solution.py:172
  67.0 2.0 %backward_rows.3 = (bf16[256,2048]{1,0:T(8,128)(2,1)S(1)}, bf16[256,384]{1,0:T(8,128)(2,1)S(1)}, bf16[256,384]{1,0:T(8,128)(2,1)S(1)}) custom-call(bf16[256,2048]{1,0:T(8,128)(2,1)S(1)} %collective-permute-done.10.in_ref.g_b, f32[256,384]{1,0:T(8,128)S(1)} %get-tuple-element.49.gate_in, f32[256,384]{1,0:T(8,128)S(1)} %get-tuple-element.50.up_in, ...), custom_call_target="tpu_custom_call" | custom-call | flops 1207959552 | bytes 5242880 | tf_op jit(solution)/shard_map/backward_rows/pallas_call | solution.py:184
  69.6 2.0 %backward_rows.2 = (bf16[256,2048]{1,0:T(8,128)(2,1)S(1)}, bf16[256,384]{1,0:T(8,128)(2,1)S(1)}, bf16[256,384]{1,0:T(8,128)(2,1)S(1)}) custom-call(bf16[256,2048]{1,0:T(8,128)(2,1)S(1)} %bitcast.7, f32[256,384]{1,0:T(8,128)S(1)} %get-tuple-element.46.gate_in, f32[256,384]{1,0:T(8,128)S(1)} %get-tuple-element.47.up_in, bf16[1,2048,384]{2,1,0:T(8,128)(2,1)S(1)} %copy-done, ...), custom_call_target="tpu_custom_call" | custom-call | flops 1207959552 | bytes 5242880 | tf_op jit(solution)/shard_map/backward_rows/pallas_call | solution.py:184
  72.3 32.0 %all_to_all.11.back_ref = bf16[16,32,2048]{2,1,0:T(8,128)(2,1)S(1)} all-to-all(bf16[16,32,2048]{2,1,0:T(8,128)(2,1)S(1)} %sum_halves.1), channel_id=1, replica_groups=mesh['z'=8,'y'=4,'x'=4,'core'=2] {'y','x'}, dimensions={0} | all-to-all | bytes 4194304 | tf_op jit(solution)/shard_map/all_to_all | solution.py:346
  104.3 1.2 combine_rows.1
  105.5 1.3 %collective-permute-start.12 = (bf16[32,4224]{1,0:T(8,128)(2,1)S(1)}, bf16[32,4224]{1,0:T(8,128)(2,1)S(1)}, u32[]{:S(2)}, u32[]{:S(2)}) collective-permute-start(bf16[32,4224]{1,0:T(8,128)(2,1)S(1)} %get-tuple-element.56), channel_id=1, source_target_pairs={{0,224},{32,0},{64,32},{96,64},{128,96},{160,128},{192,160},{224,1... | collective-permute-start | bytes 811016 | tf_op jit(solution)/shard_map/ppermute | solution.py:350
  106.8 0.9 collective-permute-start.13
  107.8 2.7 %collective-permute-start.15 = (bf16[16,2176]{1,0:T(8,128)(2,1)S(1)}, bf16[16,2176]{1,0:T(8,128)(2,1)S(1)}, u32[]{:S(2)}, u32[]{:S(2)}) collective-permute-start(bf16[16,2176]{1,0:T(8,128)(2,1)S(1)} %get-tuple-element.61), channel_id=1, source_target_pairs={{0,192},{32,224},{64,0},{96,32},{128,64},{160,96},{192,128},{224,1... | collective-permute-start | bytes 208904 | tf_op jit(solution)/shard_map/ppermute | solution.py:350
  110.7 6.9 %collective-permute-done.14.first_half = bf16[16,2048]{1,0:T(8,128)(2,1)S(1)} collective-permute-done((bf16[16,2048]{1,0:T(8,128)(2,1)S(1)}, bf16[16,2048]{1,0:T(8,128)(2,1)S(1)}, u32[]{:S(2)}, u32[]{:S(2)}) %collective-permute-start.14) | collective-permute-done | bytes 65568 | tf_op jit(solution)/shard_map/ppermute | solution.py:350
  117.7 1.5 %collective-permute-start.16 = (bf16[16,4224]{1,0:T(8,128)(2,1)S(1)}, bf16[16,4224]{1,0:T(8,128)(2,1)S(1)}, u32[]{:S(2)}, u32[]{:S(2)}) collective-permute-start(bf16[16,4224]{1,0:T(8,128)(2,1)S(1)} %get-tuple-element.62), channel_id=1, source_target_pairs={{0,64},{32,96},{64,128},{96,160},{128,192},{160,224},{192,0},{224,... | collective-permute-start | bytes 405512 | tf_op jit(solution)/shard_map/ppermute | solution.py:350
  119.2 2.7 %collective-permute-start.17 = (bf16[16,4224]{1,0:T(8,128)(2,1)S(1)}, bf16[16,4224]{1,0:T(8,128)(2,1)S(1)}, u32[]{:S(2)}, u32[]{:S(2)}) collective-permute-start(bf16[16,4224]{1,0:T(8,128)(2,1)S(1)} %get-tuple-element.63), channel_id=1, source_target_pairs={{0,192},{32,224},{64,0},{96,32},{128,64},{160,96},{192,128},{224,1... | collective-permute-start | bytes 405512 | tf_op jit(solution)/shard_map/ppermute | solution.py:350
  121.9 5.0 %weight_grads.1 = (bf16[1,2048,384]{2,1,0:T(8,128)(2,1)}, bf16[1,2048,384]{2,1,0:T(8,128)(2,1)}, bf16[1,384,2048]{2,1,0:T(8,128)(2,1)}) custom-call(bf16[256,2048]{1,0:T(8,128)(2,1)S(1)} %bitcast.11, bf16[256,2048]{1,0:T(8,128)(2,1)S(1)} %bitcast.8, bf16[256,2048]{1,0:T(8,128)(2,1)S(1)} %collective-permute-done.8.in_ref.x_b, ...), custom_call_target="tpu_custom_call" | custom-call | flops 2415919104 | bytes 12582912 | tf_op jit(solution)/shard_map/weight_grads/pallas_call | solution.py:224
  (36 shorter events, 6.6 us)
Async XLA Ops:
  2.2 12.7 %collective-permute-start.2 = (bf16[16,4224]{1,0:T(8,128)(2,1)}, bf16[16,4224]{1,0:T(8,128)(2,1)S(1)}, u32[]{:S(2)}, u32[]{:S(2)}) collective-permute-start(bf16[16,4224]{1,0:T(8,128)(2,1)} %pack_rows.1.refs_0_), channel_id=1, source_target_pairs={{0,64},{32,96},{64,128},{96,160},{128,192},{160,224},{192,0},{224,... | collective-permute-start | bytes 405512 | tf_op jit(solution)/shard_map/ppermute | solution.py:350
  5.6 9.7 %collective-permute-start.3 = (bf16[16,4224]{1,0:T(8,128)(2,1)}, bf16[16,4224]{1,0:T(8,128)(2,1)S(1)}, u32[]{:S(2)}, u32[]{:S(2)}) collective-permute-start(bf16[16,4224]{1,0:T(8,128)(2,1)} %pack_rows.1.refs_0_), channel_id=1, source_target_pairs={{0,192},{32,224},{64,0},{96,32},{128,64},{160,96},{192,128},{224,1... | collective-permute-start | bytes 405512 | tf_op jit(solution)/shard_map/ppermute | solution.py:350
  7.8 12.2 %collective-permute-start = (bf16[16,4224]{1,0:T(8,128)(2,1)}, bf16[16,4224]{1,0:T(8,128)(2,1)S(1)}, u32[]{:S(2)}, u32[]{:S(2)}) collective-permute-start(bf16[16,4224]{1,0:T(8,128)(2,1)} %pack_rows.1.refs_0_), channel_id=1, source_target_pairs={{0,32},{32,64},{64,96},{96,128},{128,160},{160,192},{192,224},{224... | collective-permute-start | bytes 405512 | tf_op jit(solution)/shard_map/ppermute | solution.py:350
  8.7 12.7 %collective-permute-start.1 = (bf16[16,4224]{1,0:T(8,128)(2,1)}, bf16[16,4224]{1,0:T(8,128)(2,1)S(1)}, u32[]{:S(2)}, u32[]{:S(2)}) collective-permute-start(bf16[16,4224]{1,0:T(8,128)(2,1)} %pack_rows.1.refs_0_), channel_id=1, source_target_pairs={{0,224},{32,0},{64,32},{96,64},{128,96},{160,128},{192,160},{224,1... | collective-permute-start | bytes 405512 | tf_op jit(solution)/shard_map/ppermute | solution.py:350
  14.9 12.1 %collective-permute-start.4 = (bf16[16,4224]{1,0:T(8,128)(2,1)S(1)}, bf16[16,4224]{1,0:T(8,128)(2,1)S(1)}, u32[]{:S(2)}, u32[]{:S(2)}) collective-permute-start(bf16[16,4224]{1,0:T(8,128)(2,1)S(1)} %collective-permute-done.2.refs_3_), channel_id=1, source_target_pairs={{0,32},{32,64},{64,96},{96,128},{128,160},{160,192},{192,224},{224... | collective-permute-start | bytes 405512 | tf_op jit(solution)/shard_map/ppermute | solution.py:350
  15.3 11.7 %collective-permute-start.5 = (bf16[16,4224]{1,0:T(8,128)(2,1)S(1)}, bf16[16,4224]{1,0:T(8,128)(2,1)S(1)}, u32[]{:S(2)}, u32[]{:S(2)}) collective-permute-start(bf16[16,4224]{1,0:T(8,128)(2,1)S(1)} %collective-permute-done.3.refs_4_), channel_id=1, source_target_pairs={{0,224},{32,0},{64,32},{96,64},{128,96},{160,128},{192,160},{224,1... | collective-permute-start | bytes 405512 | tf_op jit(solution)/shard_map/ppermute | solution.py:350
  17.2 9.8 %collective-permute-start.7 = (bf16[16,2176]{1,0:T(8,128)(2,1)S(1)}, bf16[16,2176]{1,0:T(8,128)(2,1)S(1)}, u32[]{:S(2)}, u32[]{:S(2)}) collective-permute-start(bf16[16,2176]{1,0:T(8,128)(2,1)S(1)} %slice.17), channel_id=1, source_target_pairs={{0,192},{32,224},{64,0},{96,32},{128,64},{160,96},{192,128},{224,1... | collective-permute-start | bytes 208904 | tf_op jit(solution)/shard_map/ppermute | solution.py:350
  20.0 7.0 %collective-permute-start.6 = (bf16[16,2048]{1,0:T(8,128)(2,1)S(1)}, bf16[16,2048]{1,0:T(8,128)(2,1)S(1)}, u32[]{:S(2)}, u32[]{:S(2)}) collective-permute-start(bf16[16,2048]{1,0:T(8,128)(2,1)S(1)} %slice.16), channel_id=1, source_target_pairs={{0,64},{32,96},{64,128},{96,160},{128,192},{160,224},{192,0},{224,... | collective-permute-start | bytes 196616 | tf_op jit(solution)/shard_map/ppermute | solution.py:350
  27.0 0.9 copy-start.3
  29.1 33.0 %copy-start.2 = (bf16[1,384,2048]{2,1,0:T(8,128)(2,1)S(1)}, bf16[1,384,2048]{2,1,0:T(8,128)(2,1)}, u32[]{:S(2)}) copy-start(bf16[1,384,2048]{2,1,0:T(8,128)(2,1)} %down_ref.7) | copy-start | bytes 4718596
  61.3 1.4 %copy-start = (bf16[1,2048,384]{2,1,0:T(8,128)(2,1)S(1)}, bf16[1,2048,384]{2,1,0:T(8,128)(2,1)}, u32[]{:S(2)}) copy-start(bf16[1,2048,384]{2,1,0:T(8,128)(2,1)} %gate_ref.7) | copy-start | bytes 4718596
  61.3 1.9 %copy-start.1 = (bf16[1,2048,384]{2,1,0:T(8,128)(2,1)S(1)}, bf16[1,2048,384]{2,1,0:T(8,128)(2,1)}, u32[]{:S(2)}) copy-start(bf16[1,2048,384]{2,1,0:T(8,128)(2,1)} %up_ref.7) | copy-start | bytes 4718596
  61.5 3.5 %collective-permute-start.8 = (bf16[256,2048]{1,0:T(8,128)(2,1)S(1)}, bf16[256,2048]{1,0:T(8,128)(2,1)S(1)}, u32[]{:S(2)}, u32[]{:S(2)}) collective-permute-start(bf16[256,2048]{1,0:T(8,128)(2,1)S(1)} %bitcast.9), channel_id=1, source_target_pairs={{0,1},{1,0},{2,3},{3,2},{4,5},{5,4},{6,7},{7,6},{8,9},{9,8},{10,11... | collective-permute-start | bytes 3145736 | tf_op jit(solution)/shard_map/ppermute | solution.py:342
  61.6 5.4 %collective-permute-start.10 = (bf16[256,2048]{1,0:T(8,128)(2,1)S(1)}, bf16[256,2048]{1,0:T(8,128)(2,1)S(1)}, u32[]{:S(2)}, u32[]{:S(2)}) collective-permute-start(bf16[256,2048]{1,0:T(8,128)(2,1)S(1)} %bitcast.6), channel_id=1, source_target_pairs={{0,1},{1,0},{2,3},{3,2},{4,5},{5,4},{6,7},{7,6},{8,9},{9,8},{10,11... | collective-permute-start | bytes 3145736 | tf_op jit(solution)/shard_map/ppermute | solution.py:342
  66.9 4.6 %collective-permute-start.9 = (bf16[256,2048]{1,0:T(8,128)(2,1)S(1)}, bf16[256,2048]{1,0:T(8,128)(2,1)S(1)}, u32[]{:S(2)}, u32[]{:S(2)}) collective-permute-start(bf16[256,2048]{1,0:T(8,128)(2,1)S(1)} %get-tuple-element.45), channel_id=1, source_target_pairs={{0,1},{1,0},{2,3},{3,2},{4,5},{5,4},{6,7},{7,6},{8,9},{9,8},{10,11... | collective-permute-start | bytes 3145736 | tf_op jit(solution)/shard_map/ppermute | solution.py:342
  69.0 2.9 %collective-permute-start.11 = (bf16[256,2048]{1,0:T(8,128)(2,1)S(1)}, bf16[256,2048]{1,0:T(8,128)(2,1)S(1)}, u32[]{:S(2)}, u32[]{:S(2)}) collective-permute-start(bf16[256,2048]{1,0:T(8,128)(2,1)S(1)} %get-tuple-element.51), channel_id=1, source_target_pairs={{0,1},{1,0},{2,3},{3,2},{4,5},{5,4},{6,7},{7,6},{8,9},{9,8},{10,11... | collective-permute-start | bytes 3145736 | tf_op jit(solution)/shard_map/ppermute | solution.py:342
  105.5 12.1 %collective-permute-start.12 = (bf16[32,4224]{1,0:T(8,128)(2,1)S(1)}, bf16[32,4224]{1,0:T(8,128)(2,1)S(1)}, u32[]{:S(2)}, u32[]{:S(2)}) collective-permute-start(bf16[32,4224]{1,0:T(8,128)(2,1)S(1)} %get-tuple-element.56), channel_id=1, source_target_pairs={{0,224},{32,0},{64,32},{96,64},{128,96},{160,128},{192,160},{224,1... | collective-permute-start | bytes 811016 | tf_op jit(solution)/shard_map/ppermute | solution.py:350
  106.8 10.8 %collective-permute-start.13 = (bf16[32,4224]{1,0:T(8,128)(2,1)S(1)}, bf16[32,4224]{1,0:T(8,128)(2,1)S(1)}, u32[]{:S(2)}, u32[]{:S(2)}) collective-permute-start(bf16[32,4224]{1,0:T(8,128)(2,1)S(1)} %get-tuple-element.57), channel_id=1, source_target_pairs={{0,32},{32,64},{64,96},{96,128},{128,160},{160,192},{192,224},{224... | collective-permute-start | bytes 811016 | tf_op jit(solution)/shard_map/ppermute | solution.py:350
  107.8 9.8 %collective-permute-start.15 = (bf16[16,2176]{1,0:T(8,128)(2,1)S(1)}, bf16[16,2176]{1,0:T(8,128)(2,1)S(1)}, u32[]{:S(2)}, u32[]{:S(2)}) collective-permute-start(bf16[16,2176]{1,0:T(8,128)(2,1)S(1)} %get-tuple-element.61), channel_id=1, source_target_pairs={{0,192},{32,224},{64,0},{96,32},{128,64},{160,96},{192,128},{224,1... | collective-permute-start | bytes 208904 | tf_op jit(solution)/shard_map/ppermute | solution.py:350
  110.5 7.1 %collective-permute-start.14 = (bf16[16,2048]{1,0:T(8,128)(2,1)S(1)}, bf16[16,2048]{1,0:T(8,128)(2,1)S(1)}, u32[]{:S(2)}, u32[]{:S(2)}) collective-permute-start(bf16[16,2048]{1,0:T(8,128)(2,1)S(1)} %get-tuple-element.59), channel_id=1, source_target_pairs={{0,64},{32,96},{64,128},{96,160},{128,192},{160,224},{192,0},{224,... | collective-permute-start | bytes 196616 | tf_op jit(solution)/shard_map/ppermute | solution.py:350
  117.7 9.2 %collective-permute-start.16 = (bf16[16,4224]{1,0:T(8,128)(2,1)S(1)}, bf16[16,4224]{1,0:T(8,128)(2,1)S(1)}, u32[]{:S(2)}, u32[]{:S(2)}) collective-permute-start(bf16[16,4224]{1,0:T(8,128)(2,1)S(1)} %get-tuple-element.62), channel_id=1, source_target_pairs={{0,64},{32,96},{64,128},{96,160},{128,192},{160,224},{192,0},{224,... | collective-permute-start | bytes 405512 | tf_op jit(solution)/shard_map/ppermute | solution.py:350
  119.2 7.7 %collective-permute-start.17 = (bf16[16,4224]{1,0:T(8,128)(2,1)S(1)}, bf16[16,4224]{1,0:T(8,128)(2,1)S(1)}, u32[]{:S(2)}, u32[]{:S(2)}) collective-permute-start(bf16[16,4224]{1,0:T(8,128)(2,1)S(1)} %get-tuple-element.63), channel_id=1, source_target_pairs={{0,192},{32,224},{64,0},{96,32},{128,64},{160,96},{192,128},{224,1... | collective-permute-start | bytes 405512 | tf_op jit(solution)/shard_map/ppermute | solution.py:350

commit v3 on v2

--- a/solution.py
+++ b/solution.py
@@ -81,6 +81,30 @@
         compiler_params=params(63),
         name="pack_rows",
     )(tokens, out_grad, ids_t, weight_t)
+
+
+def hold_kernel(gate_hbm, up_hbm, down_hbm, both_ref, down_ref, sems):
+    copies = [
+        pltpu.make_async_copy(gate_hbm.at[0], both_ref.at[:, pl.ds(0, HALF)], sems.at[0]),
+        pltpu.make_async_copy(up_hbm.at[0], both_ref.at[:, pl.ds(HALF, HALF)], sems.at[1]),
+        pltpu.make_async_copy(down_hbm, down_ref, sems.at[2]),
+    ]
+    for copy in copies:
+        copy.start()
+    for copy in copies:
+        copy.wait()
+
+
+def hold(gate_weight, up_weight, down_weight):
+    return pl.pallas_call(
+        hold_kernel,
+        out_shape=(jax.ShapeDtypeStruct((D, 2 * HALF), BF16), jax.ShapeDtypeStruct((1, HALF, D), BF16)),
+        in_specs=[pl.BlockSpec(memory_space=pltpu.HBM)] * 3,
+        out_specs=(VMEM, VMEM),
+        scratch_shapes=[pltpu.SemaphoreType.DMA((3,))],
+        compiler_params=params(16),
+        name="hold_weights",
+    )(gate_weight, up_weight, down_weight)
 
 
 def spread_kernel(first_ref, *refs):
@@ -136,10 +160,10 @@
     )(first, *blocks)
 
 
-def forward_kernel(in_ref, gate_ref, up_ref, down_ref, back_ref, hidden_ref, gate_out, up_out):
+def forward_kernel(in_ref, both_ref, down_ref, back_ref, hidden_ref, gate_out, up_out):
     rows = in_ref[...]
-    gate = dot(rows, gate_ref[0], 1, 0)
-    up = dot(rows, up_ref[0], 1, 0)
+    gate = dot(rows, both_ref[:, :HALF], 1, 0)
+    up = dot(rows, both_ref[:, HALF:], 1, 0)
     gate_out[...] = gate
     up_out[...] = up
     hidden = (gate * jax.nn.sigmoid(gate) * up).astype(BF16)
@@ -148,18 +172,14 @@
         back_ref[:, i : i + 512] = dot(hidden, down_ref[0, :, i : i + 512], 1, 0).astype(BF16)
 
 
-def backward_kernel(in_ref, gate_in, up_in, gate_ref, up_ref, down_ref, back_ref, pre_ref, up_pre_ref):
+def backward_kernel(in_ref, gate_in, up_in, both_ref, down_ref, back_ref, pre_ref):
     gate = gate_in[...]
     sig = jax.nn.sigmoid(gate)
     hidden_grad = dot(in_ref[...], down_ref[0], 1, 1)
-    pre = (hidden_grad * up_in[...] * sig * (1.0 + gate * (1.0 - sig))).astype(BF16)
-    up_pre = (hidden_grad * gate * sig).astype(BF16)
-    pre_ref[...] = pre
-    up_pre_ref[...] = up_pre
+    pre_ref[:, :HALF] = (hidden_grad * up_in[...] * sig * (1.0 + gate * (1.0 - sig))).astype(BF16)
+    pre_ref[:, HALF:] = (hidden_grad * gate * sig).astype(BF16)
     for i in range(0, D, 512):
-        back_ref[:, i : i + 512] = (
-            dot(pre, gate_ref[0, i : i + 512, :], 1, 1) + dot(up_pre, up_ref[0, i : i + 512, :], 1, 1)
-        ).astype(BF16)
+        back_ref[:, i : i + 512] = dot(pre_ref[...], both_ref[i : i + 512, :], 1, 1).astype(BF16)
 
 
 COST = pl.CostEstimate(flops=6 * ROWS * D * HALF, bytes_accessed=5 * 2**20, transcendentals=ROWS * HALF)
@@ -172,7 +192,7 @@
     return pl.pallas_call(
         forward_kernel,
         out_shape=(WIDE, ACT, ACT32, ACT32),
-        in_specs=[VMEM] * 4,
+        in_specs=[VMEM] * 3,
         out_specs=(VMEM,) * 4,
         compiler_params=params(16),
         cost_estimate=COST,
@@ -183,9 +203,9 @@
 def backward(rows, gate, up, weights):
     return pl.pallas_call(
         backward_kernel,
-        out_shape=(WIDE, ACT, ACT),
-        in_specs=[VMEM] * 6,
-        out_specs=(VMEM,) * 3,
+        out_shape=(WIDE, jax.ShapeDtypeStruct((ROWS, 2 * HALF), BF16)),
+        in_specs=[VMEM] * 5,
+        out_specs=(VMEM,) * 2,
         compiler_params=params(16),
         cost_estimate=COST,
         name="backward_rows",
@@ -209,9 +229,10 @@
     )(*parts)
 
 
-def weight_grad_kernel(x_a, g_a, x_b, g_b, h_a, p_a, u_a, h_b, p_b, u_b, gate_ref, up_ref, down_ref):
-    gate_ref[0] = (dot(x_a[...], p_a[...], 0, 0) + dot(x_b[...], p_b[...], 0, 0)).astype(BF16)
-    up_ref[0] = (dot(x_a[...], u_a[...], 0, 0) + dot(x_b[...], u_b[...], 0, 0)).astype(BF16)
+def weight_grad_kernel(x_a, g_a, x_b, g_b, h_a, p_a, h_b, p_b, gate_ref, up_ref, down_ref):
+    both = dot(x_a[...], p_a[...], 0, 0) + dot(x_b[...], p_b[...], 0, 0)
+    gate_ref[0] = both[:, :HALF].astype(BF16)
+    up_ref[0] = both[:, HALF:].astype(BF16)
     down_ref[0] = (dot(h_a[...], g_a[...], 0, 0) + dot(h_b[...], g_b[...], 0, 0)).astype(BF16)
 
 
@@ -219,7 +240,7 @@
     width = 512
     steps = D // width
     x_spec = pl.BlockSpec((ROWS, width), lambda i: (0, i))
-    act_spec = pl.BlockSpec((ROWS, HALF), lambda i: (0, 0))
+    acts = [pl.BlockSpec((ROWS, HALF), lambda i: (0, 0)), pl.BlockSpec((ROWS, 2 * HALF), lambda i: (0, 0))]
     wide = pl.BlockSpec((1, width, HALF), lambda i: (0, i, 0))
     return pl.pallas_call(
         weight_grad_kernel,
@@ -229,7 +250,7 @@
             jax.ShapeDtypeStruct((1, D, HALF), BF16),
             jax.ShapeDtypeStruct((1, HALF, D), BF16),
         ),
-        in_specs=[x_spec] * 4 + [act_spec] * 6,
+        in_specs=[x_spec] * 4 + acts + acts,
         out_specs=(wide, wide, pl.BlockSpec((1, HALF, width), lambda i: (0, 0, i))),
         compiler_params=params(20),
         cost_estimate=pl.CostEstimate(
@@ -350,24 +371,28 @@
     return lax.ppermute(value, "z", [(i, (i + step) % PLANES) for i in range(PLANES)])
 
 
-def spread_z(own):
+def spread_z(own, weights):
+    below2, above2 = shift(own, 2), shift(own, -2)
     below, above = shift(own, 1), shift(own, -1)
-    below2, above2 = shift(own, 2), shift(own, -2)
+    below2, above2, held = lax.optimization_barrier((below2, above2, hold(*weights)))
     half, other_half = shift(below2[:, :D], 2), shift(above2[:, D:], -2)
     below3, above3 = shift(below2, 1), shift(above2, -1)
-    return own, below, above, below2, above2, below3, above3, half, other_half
-
-
-def reduce_z(own, below2, above2, down_pair, up_pair, half, other_half):
+    return (own, below, above, below2, above2, below3, above3, half, other_half), held
+
+
+def reduce_z(own, below2, above2, down_pair, up_pair, half, other_half, beside):
     from_above, from_below = shift(down_pair, -1), shift(up_pair, 1)
-    up, down = relay(above2, from_below, shift(half, 2), below2, from_above, shift(other_half, -2))
-    return totals(own, from_above, from_below, shift(up, 2), shift(down, -2))
+    half, other_half = shift(half, 2), shift(other_half, -2)
+    half, other_half, beside = lax.optimization_barrier((half, other_half, beside))
+    up, down = relay(above2, from_below, half, below2, from_above, other_half)
+    return totals(own, from_above, from_below, shift(up, 2), shift(down, -2)), beside
 
 
 def body(tokens, expert_ids, route_weight, out_grad, gate_weight, up_weight, down_weight):
     first = (lax.axis_index("z") * CHIPS).astype(jnp.int32).reshape(1)
-    weights = (gate_weight, up_weight, down_weight)
-    blocks = spread_z(pack(tokens, out_grad, expert_ids.T, route_weight.T))
+    first, tokens = lax.optimization_barrier((first, tokens))
+    packed = pack(tokens, out_grad, expert_ids.T, route_weight.T)
+    blocks, weights = spread_z(packed, (gate_weight, up_weight, down_weight))
     send, gathered, mask, weight = spread(first, blocks)
     arrived = over_plane(send)
     rows = arrived[:, :SENT].reshape(ROWS, D)
@@ -376,15 +401,17 @@
     out_a, hidden_a, gate_a, up_a = forward(rows, weights)
     hidden_a, other_rows = lax.optimization_barrier((hidden_a, other_rows))
     out_b, hidden_b, gate_b, up_b = forward(other_rows, weights)
-    grad_b, pre_b, up_pre_b = backward(other_grads, gate_b, up_b, weights)
-    grad_a, pre_a, up_pre_a = backward(grads, gate_a, up_a, weights)
-    summed = pair_sum(out_a, swap_cores(out_b), grad_a, swap_cores(grad_b))
+    grad_b, pre_b = backward(other_grads, gate_b, up_b, weights)
+    from_b, gate_a = lax.optimization_barrier((swap_cores(out_b), gate_a))
+    grad_a, pre_a = backward(grads, gate_a, up_a, weights)
+    summed = pair_sum(out_a, from_b, grad_a, swap_cores(grad_b))
     back = over_plane(summed)
-    gate_grad, up_grad, down_grad = weight_grads(
-        rows, grads, other_rows, other_grads, (hidden_a, pre_a, up_pre_a), (hidden_b, pre_b, up_pre_b)
+    back, pre_a = lax.optimization_barrier((back, pre_a))
+    weight_out = weight_grads(rows, grads, other_rows, other_grads, (hidden_a, pre_a), (hidden_b, pre_b))
+    (layer_out, token_grad, route_t), weight_out = reduce_z(
+        *combine(first, back, gathered, mask, weight), beside=weight_out
     )
-    layer_out, token_grad, route_t = reduce_z(*combine(first, back, gathered, mask, weight))
-    return layer_out, token_grad, route_t.T, gate_grad, up_grad, down_grad
+    return layer_out, token_grad, route_t.T, *weight_out
 
 
 def solution(mesh):

time: 130 us -> 128 us (0.985)
  waiting for transfers between devices: 17.9 us -> 15.2 us
  local copies, waits for them, and re-layouts: 2.19 us -> 4.47 us
    ppermute x14, waiting for transfers between devices: 17.6 us -> 14.4 us  [shift(): lax.ppermute(value, 'z', [(i, (i + step) % PLANES) for i in range(PLANES)])]
    unnamed x8, local copies, waits for them, and re-layouts: 1.94 us -> 4.23 us
    pallas_call x2 -> x3, Pallas kernels: 3.92 us -> 3.84 us  [the longest x2 3.39 us: backward(): pl.pallas_call(backward_kernel, out_shape=(WIDE, jax.ShapeDtypeStruct((RO...]
  transfers between devices with their start and end apart: 18 -> 18, of which waited for: 4 -> 8; matrix products, arithmetic and copies ran while one was open for 0% -> 0% of each run, Pallas kernels for 10% -> 10%
where the time goes in v3:
time: 128 us; the launch traced here: 127 us
  blocking collectives  64.5 us (50%)
  starting transfers between devices  24.2 us (19%)
  Pallas kernels  17.5 us (14%)
  waiting for transfers between devices  15.2 us (12%)
  local copies, waits for them, and re-layouts  4.47 us (3%)
    all_to_all x2, blocking collectives, over_plane(): return lax.all_to_all(blocks, ('y', 'x'), 0, 0, tiled=True)  64.5 us
    ppermute x14, starting transfers between devices, shift(): lax.ppermute(value, 'z', [(i, (i + step) % PLANES) for i in range(PLANES)])  23 us
    ppermute x14, waiting for transfers between devices, shift(): lax.ppermute(value, 'z', [(i, (i + step) % PLANES) for i in range(PLANES)])  14.4 us
    pallas_call x1, Pallas kernels, weight_grads(): pl.pallas_call(weight_grad_kernel, grid=(steps,), out_shape=(jax.ShapeDty...  4.57 us
    unnamed x8, local copies, waits for them, and re-layouts  4.23 us
    pallas_call x2, Pallas kernels, forward(): pl.pallas_call(forward_kernel, out_shape=(WIDE, ACT, ACT32, ACT32), in_sp...  3.74 us
    pallas_call x2, Pallas kernels, backward(): pl.pallas_call(backward_kernel, out_shape=(WIDE, jax.ShapeDtypeStruct((RO...  3.39 us
  transfers between devices with their start and end apart: 18, of which 8 were waited for; matrix products, arithmetic and copies ran while one was open for 0% of the time, Pallas kernels for 10%

profile of v3, /device:TPU:32, one launch (start us, length us, event | category | flops | bytes accessed | tf_op | source)
XLA Modules:
  0.0 126.7 jit_solution(12376705807281498350)
XLA Ops:
  0.6 1.6 %pack_rows.1.refs_0_ = bf16[16,4224]{1,0:T(8,128)(2,1)} custom-call(bf16[16,2048]{1,0:T(8,128)(2,1)} %tok_hbm, bf16[16,2048]{1,0:T(8,128)(2,1)} %grad_hbm.1, s32[8,16]{1,0:T(8,128)} %bitcast.12, f32[8,16]{1,0:T(8,128)} %bitcast.13), custom_call_target="tpu_custom_call" | custom-call | tf_op jit(solution)/shard_map/pack_rows/pallas_call | solution.py:71
  2.2 5.5 %collective-permute-start.3 = (bf16[16,4224]{1,0:T(8,128)(2,1)}, bf16[16,4224]{1,0:T(8,128)(2,1)S(1)}, u32[]{:S(2)}, u32[]{:S(2)}) collective-permute-start(bf16[16,4224]{1,0:T(8,128)(2,1)} %pack_rows.1.refs_0_), channel_id=1, source_target_pairs={{0,192},{32,224},{64,0},{96,32},{128,64},{160,96},{192,128},{224,1... | collective-permute-start | bytes 405512 | tf_op jit(solution)/shard_map/ppermute | solution.py:371
  9.8 1.4 %copy-done = bf16[1,2048,384]{2,1,0:T(8,128)(2,1)S(1)} copy-done((bf16[1,2048,384]{2,1,0:T(8,128)(2,1)S(1)}, bf16[1,2048,384]{2,1,0:T(8,128)(2,1)}, u32[]{:S(2)}) %copy-start) | copy-done | bytes 1572888
  11.2 1.4 %copy-done.1 = bf16[1,2048,384]{2,1,0:T(8,128)(2,1)S(1)} copy-done((bf16[1,2048,384]{2,1,0:T(8,128)(2,1)S(1)}, bf16[1,2048,384]{2,1,0:T(8,128)(2,1)}, u32[]{:S(2)}) %copy-start.1) | copy-done | bytes 1572888
  12.6 1.4 %copy-done.2 = bf16[1,384,2048]{2,1,0:T(8,128)(2,1)S(1)} copy-done((bf16[1,384,2048]{2,1,0:T(8,128)(2,1)S(1)}, bf16[1,384,2048]{2,1,0:T(8,128)(2,1)}, u32[]{:S(2)}) %copy-start.2) | copy-done | bytes 1572888
  14.4 4.0 %collective-permute-done.2.refs_3_ = bf16[16,4224]{1,0:T(8,128)(2,1)S(1)} collective-permute-done((bf16[16,4224]{1,0:T(8,128)(2,1)}, bf16[16,4224]{1,0:T(8,128)(2,1)S(1)}, u32[]{:S(2)}, u32[]{:S(2)}) %collective-permute-start.2) | collective-permute-done | bytes 135200 | tf_op jit(solution)/shard_map/ppermute | solution.py:371
  18.4 2.0 %collective-permute-start.5 = (bf16[16,4224]{1,0:T(8,128)(2,1)S(1)}, bf16[16,4224]{1,0:T(8,128)(2,1)S(1)}, u32[]{:S(2)}, u32[]{:S(2)}) collective-permute-start(bf16[16,4224]{1,0:T(8,128)(2,1)S(1)} %collective-permute-done.3.refs_4_), channel_id=1, source_target_pairs={{0,224},{32,0},{64,32},{96,64},{128,96},{160,128},{192,160},{224,1... | collective-permute-start | bytes 405512 | tf_op jit(solution)/shard_map/ppermute | solution.py:371
  20.5 1.8 %collective-permute-start.7 = (bf16[16,2176]{1,0:T(8,128)(2,1)S(1)}, bf16[16,2176]{1,0:T(8,128)(2,1)S(1)}, u32[]{:S(2)}, u32[]{:S(2)}) collective-permute-start(bf16[16,2176]{1,0:T(8,128)(2,1)S(1)} %slice.13), channel_id=1, source_target_pairs={{0,192},{32,224},{64,0},{96,32},{128,64},{160,96},{192,128},{224,1... | collective-permute-start | bytes 208904 | tf_op jit(solution)/shard_map/ppermute | solution.py:371
  22.3 1.2 collective-permute-start.6
  23.5 5.9 %collective-permute-done.6.refs_7_ = bf16[16,2048]{1,0:T(8,128)(2,1)S(1)} collective-permute-done((bf16[16,2048]{1,0:T(8,128)(2,1)S(1)}, bf16[16,2048]{1,0:T(8,128)(2,1)S(1)}, u32[]{:S(2)}, u32[]{:S(2)}) %collective-permute-start.6) | collective-permute-done | bytes 65568 | tf_op jit(solution)/shard_map/ppermute | solution.py:371
  29.4 1.2 spread_rows.1
  30.6 32.5 %all_to_all.10 = bf16[16,32,2048]{2,1,0:T(8,128)(2,1)S(1)} all-to-all(bf16[16,32,2048]{2,1,0:T(8,128)(2,1)S(1)} %get-tuple-element.62), channel_id=1, replica_groups=mesh['z'=8,'y'=4,'x'=4,'core'=2] {'y','x'}, dimensions={0} | all-to-all | bytes 4194304 | tf_op jit(solution)/shard_map/all_to_all | solution.py:367
  64.0 1.9 %forward_rows.2 = (bf16[256,2048]{1,0:T(8,128)(2,1)S(1)}, bf16[256,384]{1,0:T(8,128)(2,1)S(1)}, f32[256,384]{1,0:T(8,128)S(1)}, f32[256,384]{1,0:T(8,128)S(1)}) custom-call(bf16[256,2048]{1,0:T(8,128)(2,1)S(1)} %bitcast.10, bf16[2048,768]{1,0:T(8,128)(2,1)S(1)} %get-tuple-element.63.both_ref, bf16[1,384,2048]{2,1,0:T(8,128)(2,1)S(1)} %get-tuple-element.64.down_ref), custom_call_target="tpu_custom_call" | custom-call | flops 1207959552 | bytes 5242880 | tf_op jit(solution)/shard_map/forward_rows/pallas_call | solution.py:192
  66.1 1.9 %forward_rows.3 = (bf16[256,2048]{1,0:T(8,128)(2,1)S(1)}, bf16[256,384]{1,0:T(8,128)(2,1)S(1)}, f32[256,384]{1,0:T(8,128)S(1)}, f32[256,384]{1,0:T(8,128)S(1)}) custom-call(bf16[256,2048]{1,0:T(8,128)(2,1)S(1)} %collective-permute-done.8.in_ref.x_b, bf16[2048,768]{1,0:T(8,128)(2,1)S(1)} %get-tuple-element.63.both_ref, ...), custom_call_target="tpu_custom_call" | custom-call | flops 1207959552 | bytes 5242880 | tf_op jit(solution)/shard_map/forward_rows/pallas_call | solution.py:192
  68.2 1.7 %backward_rows.3 = (bf16[256,2048]{1,0:T(8,128)(2,1)S(1)}, bf16[256,768]{1,0:T(8,128)(2,1)S(1)}) custom-call(bf16[256,2048]{1,0:T(8,128)(2,1)S(1)} %collective-permute-done.10.in_ref.g_b, f32[256,384]{1,0:T(8,128)S(1)} %get-tuple-element.74.gate_in, f32[256,384]{1,0:T(8,128)S(1)} %get-tuple-element.75.up_in, ...), custom_call_target="tpu_custom_call" | custom-call | flops 1207959552 | bytes 5242880 | tf_op jit(solution)/shard_map/backward_rows/pallas_call | solution.py:204
  70.8 1.7 %backward_rows.2 = (bf16[256,2048]{1,0:T(8,128)(2,1)S(1)}, bf16[256,768]{1,0:T(8,128)(2,1)S(1)}) custom-call(bf16[256,2048]{1,0:T(8,128)(2,1)S(1)} %bitcast.7, f32[256,384]{1,0:T(8,128)S(1)} %get-tuple-element.71.gate_in, f32[256,384]{1,0:T(8,128)S(1)} %get-tuple-element.72.up_in, bf16[2048,768]{1,0:T(8,128)(2,1)S(1)} %get-tuple-element.63.both_ref, ...), custom_call_target="tpu_custom_call" | custom-call | flops 1207959552 | bytes 5242880 | tf_op jit(solution)/shard_map/backward_rows/pallas_call | solution.py:204
  73.2 32.0 %all_to_all.11.back_ref = bf16[16,32,2048]{2,1,0:T(8,128)(2,1)S(1)} all-to-all(bf16[16,32,2048]{2,1,0:T(8,128)(2,1)S(1)} %sum_halves.1), channel_id=1, replica_groups=mesh['z'=8,'y'=4,'x'=4,'core'=2] {'y','x'}, dimensions={0} | all-to-all | bytes 4194304 | tf_op jit(solution)/shard_map/all_to_all | solution.py:367
  105.1 1.2 combine_rows.1
  106.4 2.0 %collective-permute-start.13 = (bf16[32,4224]{1,0:T(8,128)(2,1)S(1)}, bf16[32,4224]{1,0:T(8,128)(2,1)S(1)}, u32[]{:S(2)}, u32[]{:S(2)}) collective-permute-start(bf16[32,4224]{1,0:T(8,128)(2,1)S(1)} %get-tuple-element.84), channel_id=1, source_target_pairs={{0,32},{32,64},{64,96},{96,128},{128,160},{160,192},{192,224},{224... | collective-permute-start | bytes 811016 | tf_op jit(solution)/shard_map/ppermute | solution.py:371
  108.8 3.8 %collective-permute-start.15 = (bf16[16,2176]{1,0:T(8,128)(2,1)S(1)}, bf16[16,2176]{1,0:T(8,128)(2,1)S(1)}, u32[]{:S(2)}, u32[]{:S(2)}) collective-permute-start(bf16[16,2176]{1,0:T(8,128)(2,1)S(1)} %get-tuple-element.87), channel_id=1, source_target_pairs={{0,192},{32,224},{64,0},{96,32},{128,64},{160,96},{192,128},{224,1... | collective-permute-start | bytes 208904 | tf_op jit(solution)/shard_map/ppermute | solution.py:371
  112.6 4.6 %weight_grads.1 = (bf16[1,2048,384]{2,1,0:T(8,128)(2,1)}, bf16[1,2048,384]{2,1,0:T(8,128)(2,1)}, bf16[1,384,2048]{2,1,0:T(8,128)(2,1)}) custom-call(bf16[256,2048]{1,0:T(8,128)(2,1)S(1)} %bitcast.11, bf16[256,2048]{1,0:T(8,128)(2,1)S(1)} %bitcast.8, bf16[256,2048]{1,0:T(8,128)(2,1)S(1)} %collective-permute-done.8.in_ref.x_b, ...), custom_call_target="tpu_custom_call" | custom-call | flops 2415919104 | bytes 12582912 | tf_op jit(solution)/shard_map/weight_grads/pallas_call | solution.py:245
  117.4 2.0 %collective-permute-start.16 = (bf16[16,4224]{1,0:T(8,128)(2,1)S(1)}, bf16[16,4224]{1,0:T(8,128)(2,1)S(1)}, u32[]{:S(2)}, u32[]{:S(2)}) collective-permute-start(bf16[16,4224]{1,0:T(8,128)(2,1)S(1)} %get-tuple-element.98), channel_id=1, source_target_pairs={{0,64},{32,96},{64,128},{96,160},{128,192},{160,224},{192,0},{224,... | collective-permute-start | bytes 405512 | tf_op jit(solution)/shard_map/ppermute | solution.py:371
  119.4 2.2 %collective-permute-start.17 = (bf16[16,4224]{1,0:T(8,128)(2,1)S(1)}, bf16[16,4224]{1,0:T(8,128)(2,1)S(1)}, u32[]{:S(2)}, u32[]{:S(2)}) collective-permute-start(bf16[16,4224]{1,0:T(8,128)(2,1)S(1)} %get-tuple-element.99), channel_id=1, source_target_pairs={{0,192},{32,224},{64,0},{96,32},{128,64},{160,96},{192,128},{224,1... | collective-permute-start | bytes 405512 | tf_op jit(solution)/shard_map/ppermute | solution.py:371
  121.6 4.1 %collective-permute-done.16.refs_3_ = bf16[16,4224]{1,0:T(8,128)(2,1)S(1)} collective-permute-done((bf16[16,4224]{1,0:T(8,128)(2,1)S(1)}, bf16[16,4224]{1,0:T(8,128)(2,1)S(1)}, u32[]{:S(2)}, u32[]{:S(2)}) %collective-permute-start.16) | collective-permute-done | bytes 135200 | tf_op jit(solution)/shard_map/ppermute | solution.py:371
  (37 shorter events, 6.9 us)
Async XLA Ops:
  2.2 12.2 %collective-permute-start.3 = (bf16[16,4224]{1,0:T(8,128)(2,1)}, bf16[16,4224]{1,0:T(8,128)(2,1)S(1)}, u32[]{:S(2)}, u32[]{:S(2)}) collective-permute-start(bf16[16,4224]{1,0:T(8,128)(2,1)} %pack_rows.1.refs_0_), channel_id=1, source_target_pairs={{0,192},{32,224},{64,0},{96,32},{128,64},{160,96},{192,128},{224,1... | collective-permute-start | bytes 405512 | tf_op jit(solution)/shard_map/ppermute | solution.py:371
  7.7 10.7 %collective-permute-start.2 = (bf16[16,4224]{1,0:T(8,128)(2,1)}, bf16[16,4224]{1,0:T(8,128)(2,1)S(1)}, u32[]{:S(2)}, u32[]{:S(2)}) collective-permute-start(bf16[16,4224]{1,0:T(8,128)(2,1)} %pack_rows.1.refs_0_), channel_id=1, source_target_pairs={{0,64},{32,96},{64,128},{96,160},{128,192},{160,224},{192,0},{224,... | collective-permute-start | bytes 405512 | tf_op jit(solution)/shard_map/ppermute | solution.py:371
  7.7 14.6 %collective-permute-start.1 = (bf16[16,4224]{1,0:T(8,128)(2,1)}, bf16[16,4224]{1,0:T(8,128)(2,1)S(1)}, u32[]{:S(2)}, u32[]{:S(2)}) collective-permute-start(bf16[16,4224]{1,0:T(8,128)(2,1)} %pack_rows.1.refs_0_), channel_id=1, source_target_pairs={{0,224},{32,0},{64,32},{96,64},{128,96},{160,128},{192,160},{224,1... | collective-permute-start | bytes 405512 | tf_op jit(solution)/shard_map/ppermute | solution.py:371
  8.7 14.7 %collective-permute-start = (bf16[16,4224]{1,0:T(8,128)(2,1)}, bf16[16,4224]{1,0:T(8,128)(2,1)S(1)}, u32[]{:S(2)}, u32[]{:S(2)}) collective-permute-start(bf16[16,4224]{1,0:T(8,128)(2,1)} %pack_rows.1.refs_0_), channel_id=1, source_target_pairs={{0,32},{32,64},{64,96},{96,128},{128,160},{160,192},{192,224},{224... | collective-permute-start | bytes 405512 | tf_op jit(solution)/shard_map/ppermute | solution.py:371
  9.7 1.4 %copy-start = (bf16[1,2048,384]{2,1,0:T(8,128)(2,1)S(1)}, bf16[1,2048,384]{2,1,0:T(8,128)(2,1)}, u32[]{:S(2)}) copy-start(bf16[1,2048,384]{2,1,0:T(8,128)(2,1)} %gate_hbm.1) | copy-start | bytes 4718596
  11.2 1.4 %copy-start.1 = (bf16[1,2048,384]{2,1,0:T(8,128)(2,1)S(1)}, bf16[1,2048,384]{2,1,0:T(8,128)(2,1)}, u32[]{:S(2)}) copy-start(bf16[1,2048,384]{2,1,0:T(8,128)(2,1)} %up_hbm.1) | copy-start | bytes 4718596
  12.6 1.4 %copy-start.2 = (bf16[1,384,2048]{2,1,0:T(8,128)(2,1)S(1)}, bf16[1,384,2048]{2,1,0:T(8,128)(2,1)}, u32[]{:S(2)}) copy-start(bf16[1,384,2048]{2,1,0:T(8,128)(2,1)} %down_hbm.1) | copy-start | bytes 4718596
  14.0 15.5 %copy-start.3 = (bf16[16,4224]{1,0:T(8,128)(2,1)S(1)}, bf16[16,4224]{1,0:T(8,128)(2,1)}, u32[]{:S(2)}) copy-start(bf16[16,4224]{1,0:T(8,128)(2,1)} %pack_rows.1.refs_0_) | copy-start | bytes 405508
  18.4 11.0 %collective-permute-start.4 = (bf16[16,4224]{1,0:T(8,128)(2,1)S(1)}, bf16[16,4224]{1,0:T(8,128)(2,1)S(1)}, u32[]{:S(2)}, u32[]{:S(2)}) collective-permute-start(bf16[16,4224]{1,0:T(8,128)(2,1)S(1)} %collective-permute-done.2.refs_3_), channel_id=1, source_target_pairs={{0,32},{32,64},{64,96},{96,128},{128,160},{160,192},{192,224},{224... | collective-permute-start | bytes 405512 | tf_op jit(solution)/shard_map/ppermute | solution.py:371
  18.4 11.0 %collective-permute-start.5 = (bf16[16,4224]{1,0:T(8,128)(2,1)S(1)}, bf16[16,4224]{1,0:T(8,128)(2,1)S(1)}, u32[]{:S(2)}, u32[]{:S(2)}) collective-permute-start(bf16[16,4224]{1,0:T(8,128)(2,1)S(1)} %collective-permute-done.3.refs_4_), channel_id=1, source_target_pairs={{0,224},{32,0},{64,32},{96,64},{128,96},{160,128},{192,160},{224,1... | collective-permute-start | bytes 405512 | tf_op jit(solution)/shard_map/ppermute | solution.py:371
  20.5 9.0 %collective-permute-start.7 = (bf16[16,2176]{1,0:T(8,128)(2,1)S(1)}, bf16[16,2176]{1,0:T(8,128)(2,1)S(1)}, u32[]{:S(2)}, u32[]{:S(2)}) collective-permute-start(bf16[16,2176]{1,0:T(8,128)(2,1)S(1)} %slice.13), channel_id=1, source_target_pairs={{0,192},{32,224},{64,0},{96,32},{128,64},{160,96},{192,128},{224,1... | collective-permute-start | bytes 208904 | tf_op jit(solution)/shard_map/ppermute | solution.py:371
  22.3 7.1 %collective-permute-start.6 = (bf16[16,2048]{1,0:T(8,128)(2,1)S(1)}, bf16[16,2048]{1,0:T(8,128)(2,1)S(1)}, u32[]{:S(2)}, u32[]{:S(2)}) collective-permute-start(bf16[16,2048]{1,0:T(8,128)(2,1)S(1)} %slice.12), channel_id=1, source_target_pairs={{0,64},{32,96},{64,128},{96,160},{128,192},{160,224},{192,0},{224,... | collective-permute-start | bytes 196616 | tf_op jit(solution)/shard_map/ppermute | solution.py:371
  63.4 2.7 %collective-permute-start.8 = (bf16[256,2048]{1,0:T(8,128)(2,1)S(1)}, bf16[256,2048]{1,0:T(8,128)(2,1)S(1)}, u32[]{:S(2)}, u32[]{:S(2)}) collective-permute-start(bf16[256,2048]{1,0:T(8,128)(2,1)S(1)} %bitcast.9), channel_id=1, source_target_pairs={{0,1},{1,0},{2,3},{3,2},{4,5},{5,4},{6,7},{7,6},{8,9},{9,8},{10,11... | collective-permute-start | bytes 3145736 | tf_op jit(solution)/shard_map/ppermute | solution.py:363
  63.5 4.8 %collective-permute-start.10 = (bf16[256,2048]{1,0:T(8,128)(2,1)S(1)}, bf16[256,2048]{1,0:T(8,128)(2,1)S(1)}, u32[]{:S(2)}, u32[]{:S(2)}) collective-permute-start(bf16[256,2048]{1,0:T(8,128)(2,1)S(1)} %bitcast.6), channel_id=1, source_target_pairs={{0,1},{1,0},{2,3},{3,2},{4,5},{5,4},{6,7},{7,6},{8,9},{9,8},{10,11... | collective-permute-start | bytes 3145736 | tf_op jit(solution)/shard_map/ppermute | solution.py:363
  68.0 2.7 %collective-permute-start.9 = (bf16[256,2048]{1,0:T(8,128)(2,1)S(1)}, bf16[256,2048]{1,0:T(8,128)(2,1)S(1)}, u32[]{:S(2)}, u32[]{:S(2)}) collective-permute-start(bf16[256,2048]{1,0:T(8,128)(2,1)S(1)} %get-tuple-element.68), channel_id=1, source_target_pairs={{0,1},{1,0},{2,3},{3,2},{4,5},{5,4},{6,7},{7,6},{8,9},{9,8},{10,11... | collective-permute-start | bytes 3145736 | tf_op jit(solution)/shard_map/ppermute | solution.py:363
  69.9 2.7 %collective-permute-start.11 = (bf16[256,2048]{1,0:T(8,128)(2,1)S(1)}, bf16[256,2048]{1,0:T(8,128)(2,1)S(1)}, u32[]{:S(2)}, u32[]{:S(2)}) collective-permute-start(bf16[256,2048]{1,0:T(8,128)(2,1)S(1)} %get-tuple-element.76), channel_id=1, source_target_pairs={{0,1},{1,0},{2,3},{3,2},{4,5},{5,4},{6,7},{7,6},{8,9},{9,8},{10,11... | collective-permute-start | bytes 3145736 | tf_op jit(solution)/shard_map/ppermute | solution.py:363
  106.4 11.0 %collective-permute-start.12 = (bf16[32,4224]{1,0:T(8,128)(2,1)S(1)}, bf16[32,4224]{1,0:T(8,128)(2,1)S(1)}, u32[]{:S(2)}, u32[]{:S(2)}) collective-permute-start(bf16[32,4224]{1,0:T(8,128)(2,1)S(1)} %get-tuple-element.83), channel_id=1, source_target_pairs={{0,224},{32,0},{64,32},{96,64},{128,96},{160,128},{192,160},{224,1... | collective-permute-start | bytes 811016 | tf_op jit(solution)/shard_map/ppermute | solution.py:371
  106.4 10.9 %collective-permute-start.13 = (bf16[32,4224]{1,0:T(8,128)(2,1)S(1)}, bf16[32,4224]{1,0:T(8,128)(2,1)S(1)}, u32[]{:S(2)}, u32[]{:S(2)}) collective-permute-start(bf16[32,4224]{1,0:T(8,128)(2,1)S(1)} %get-tuple-element.84), channel_id=1, source_target_pairs={{0,32},{32,64},{64,96},{96,128},{128,160},{160,192},{192,224},{224... | collective-permute-start | bytes 811016 | tf_op jit(solution)/shard_map/ppermute | solution.py:371
  108.5 8.8 %collective-permute-start.14 = (bf16[16,2048]{1,0:T(8,128)(2,1)S(1)}, bf16[16,2048]{1,0:T(8,128)(2,1)S(1)}, u32[]{:S(2)}, u32[]{:S(2)}) collective-permute-start(bf16[16,2048]{1,0:T(8,128)(2,1)S(1)} %get-tuple-element.86), channel_id=1, source_target_pairs={{0,64},{32,96},{64,128},{96,160},{128,192},{160,224},{192,0},{224,... | collective-permute-start | bytes 196616 | tf_op jit(solution)/shard_map/ppermute | solution.py:371
  108.8 8.5 %collective-permute-start.15 = (bf16[16,2176]{1,0:T(8,128)(2,1)S(1)}, bf16[16,2176]{1,0:T(8,128)(2,1)S(1)}, u32[]{:S(2)}, u32[]{:S(2)}) collective-permute-start(bf16[16,2176]{1,0:T(8,128)(2,1)S(1)} %get-tuple-element.87), channel_id=1, source_target_pairs={{0,192},{32,224},{64,0},{96,32},{128,64},{160,96},{192,128},{224,1... | collective-permute-start | bytes 208904 | tf_op jit(solution)/shard_map/ppermute | solution.py:371
  117.4 8.4 %collective-permute-start.16 = (bf16[16,4224]{1,0:T(8,128)(2,1)S(1)}, bf16[16,4224]{1,0:T(8,128)(2,1)S(1)}, u32[]{:S(2)}, u32[]{:S(2)}) collective-permute-start(bf16[16,4224]{1,0:T(8,128)(2,1)S(1)} %get-tuple-element.98), channel_id=1, source_target_pairs={{0,64},{32,96},{64,128},{96,160},{128,192},{160,224},{192,0},{224,... | collective-permute-start | bytes 405512 | tf_op jit(solution)/shard_map/ppermute | solution.py:371
  119.4 6.5 %collective-permute-start.17 = (bf16[16,4224]{1,0:T(8,128)(2,1)S(1)}, bf16[16,4224]{1,0:T(8,128)(2,1)S(1)}, u32[]{:S(2)}, u32[]{:S(2)}) collective-permute-start(bf16[16,4224]{1,0:T(8,128)(2,1)S(1)} %get-tuple-element.99), channel_id=1, source_target_pairs={{0,192},{32,224},{64,0},{96,32},{128,64},{160,96},{192,128},{224,1... | collective-permute-start | bytes 405512 | tf_op jit(solution)/shard_map/ppermute | solution.py:371

commit v4 on v3

--- a/solution.py
+++ b/solution.py
@@ -83,11 +83,10 @@
     )(tokens, out_grad, ids_t, weight_t)
 
 
-def hold_kernel(gate_hbm, up_hbm, down_hbm, both_ref, down_ref, sems):
+def hold_kernel(gate_hbm, up_hbm, both_ref, sems):
     copies = [
         pltpu.make_async_copy(gate_hbm.at[0], both_ref.at[:, pl.ds(0, HALF)], sems.at[0]),
         pltpu.make_async_copy(up_hbm.at[0], both_ref.at[:, pl.ds(HALF, HALF)], sems.at[1]),
-        pltpu.make_async_copy(down_hbm, down_ref, sems.at[2]),
     ]
     for copy in copies:
         copy.start()
@@ -95,16 +94,16 @@
         copy.wait()
 
 
-def hold(gate_weight, up_weight, down_weight):
+def hold(gate_weight, up_weight):
     return pl.pallas_call(
         hold_kernel,
-        out_shape=(jax.ShapeDtypeStruct((D, 2 * HALF), BF16), jax.ShapeDtypeStruct((1, HALF, D), BF16)),
-        in_specs=[pl.BlockSpec(memory_space=pltpu.HBM)] * 3,
-        out_specs=(VMEM, VMEM),
-        scratch_shapes=[pltpu.SemaphoreType.DMA((3,))],
+        out_shape=jax.ShapeDtypeStruct((D, 2 * HALF), BF16),
+        in_specs=[pl.BlockSpec(memory_space=pltpu.HBM)] * 2,
+        out_specs=VMEM,
+        scratch_shapes=[pltpu.SemaphoreType.DMA((2,))],
         compiler_params=params(16),
         name="hold_weights",
-    )(gate_weight, up_weight, down_weight)
+    )(gate_weight, up_weight)
 
 
 def spread_kernel(first_ref, *refs):
@@ -392,7 +391,8 @@
     first = (lax.axis_index("z") * CHIPS).astype(jnp.int32).reshape(1)
     first, tokens = lax.optimization_barrier((first, tokens))
     packed = pack(tokens, out_grad, expert_ids.T, route_weight.T)
-    blocks, weights = spread_z(packed, (gate_weight, up_weight, down_weight))
+    blocks, both = spread_z(packed, (gate_weight, up_weight))
+    weights = (both, down_weight)
     send, gathered, mask, weight = spread(first, blocks)
     arrived = over_plane(send)
     rows = arrived[:, :SENT].reshape(ROWS, D)

time: 128 us -> 128 us (level)
  waiting for transfers between devices: 15.2 us -> 17.5 us
    ppermute x14, waiting for transfers between devices: 14.4 us -> 16.9 us  [shift(): lax.ppermute(value, 'z', [(i, (i + step) % PLANES) for i in range(PLANES)])]
  transfers between devices with their start and end apart: 18 -> 18, of which waited for: 8 -> 6; matrix products, arithmetic and copies ran while one was open for 0% -> 0% of each run, Pallas kernels for 10% -> 9%
where the time goes in v4:
time: 128 us; the launch traced here: 127 us
  blocking collectives  63.8 us (50%)
  starting transfers between devices  24.2 us (19%)
  waiting for transfers between devices  17.5 us (14%)
  Pallas kernels  17.3 us (14%)
  local copies, waits for them, and re-layouts  3.63 us (3%)
    all_to_all x2, blocking collectives, over_plane(): return lax.all_to_all(blocks, ('y', 'x'), 0, 0, tiled=True)  63.8 us
    ppermute x14, starting transfers between devices, shift(): lax.ppermute(value, 'z', [(i, (i + step) % PLANES) for i in range(PLANES)])  23 us
    ppermute x14, waiting for transfers between devices, shift(): lax.ppermute(value, 'z', [(i, (i + step) % PLANES) for i in range(PLANES)])  16.9 us
    pallas_call x1, Pallas kernels, weight_grads(): pl.pallas_call(weight_grad_kernel, grid=(steps,), out_shape=(jax.ShapeDty...  4.57 us
    pallas_call x2, Pallas kernels, forward(): pl.pallas_call(forward_kernel, out_shape=(WIDE, ACT, ACT32, ACT32), in_sp...  3.74 us
    pallas_call x2, Pallas kernels, backward(): pl.pallas_call(backward_kernel, out_shape=(WIDE, jax.ShapeDtypeStruct((RO...  3.4 us
    unnamed x8, local copies, waits for them, and re-layouts  3.38 us
  transfers between devices with their start and end apart: 18, of which 6 were waited for; matrix products, arithmetic and copies ran while one was open for 0% of the time, Pallas kernels for 9%

profile of v4, /device:TPU:32, one launch (start us, length us, event | category | flops | bytes accessed | tf_op | source)
XLA Modules:
  0.0 127.3 jit_solution(17829156181945892579)
XLA Ops:
  0.6 1.6 %pack_rows.1.refs_0_ = bf16[16,4224]{1,0:T(8,128)(2,1)} custom-call(bf16[16,2048]{1,0:T(8,128)(2,1)} %tok_hbm, bf16[16,2048]{1,0:T(8,128)(2,1)} %grad_hbm.1, s32[8,16]{1,0:T(8,128)} %bitcast.12, f32[8,16]{1,0:T(8,128)} %bitcast.13), custom_call_target="tpu_custom_call" | custom-call | tf_op jit(solution)/shard_map/pack_rows/pallas_call | solution.py:71
  2.2 5.5 %collective-permute-start.3 = (bf16[16,4224]{1,0:T(8,128)(2,1)}, bf16[16,4224]{1,0:T(8,128)(2,1)S(1)}, u32[]{:S(2)}, u32[]{:S(2)}) collective-permute-start(bf16[16,4224]{1,0:T(8,128)(2,1)} %pack_rows.1.refs_0_), channel_id=1, source_target_pairs={{0,192},{32,224},{64,0},{96,32},{128,64},{160,96},{192,128},{224,1... | collective-permute-start | bytes 405512 | tf_op jit(solution)/shard_map/ppermute | solution.py:370
  9.8 1.4 %copy-done.1 = bf16[1,2048,384]{2,1,0:T(8,128)(2,1)S(1)} copy-done((bf16[1,2048,384]{2,1,0:T(8,128)(2,1)S(1)}, bf16[1,2048,384]{2,1,0:T(8,128)(2,1)}, u32[]{:S(2)}) %copy-start.1) | copy-done | bytes 1572888
  11.2 1.4 %copy-done.2 = bf16[1,2048,384]{2,1,0:T(8,128)(2,1)S(1)} copy-done((bf16[1,2048,384]{2,1,0:T(8,128)(2,1)S(1)}, bf16[1,2048,384]{2,1,0:T(8,128)(2,1)}, u32[]{:S(2)}) %copy-start.2) | copy-done | bytes 1572888
  12.9 5.5 %collective-permute-done.2.refs_3_ = bf16[16,4224]{1,0:T(8,128)(2,1)S(1)} collective-permute-done((bf16[16,4224]{1,0:T(8,128)(2,1)}, bf16[16,4224]{1,0:T(8,128)(2,1)S(1)}, u32[]{:S(2)}, u32[]{:S(2)}) %collective-permute-start.2) | collective-permute-done | bytes 135200 | tf_op jit(solution)/shard_map/ppermute | solution.py:370
  18.4 2.0 %collective-permute-start.5 = (bf16[16,4224]{1,0:T(8,128)(2,1)S(1)}, bf16[16,4224]{1,0:T(8,128)(2,1)S(1)}, u32[]{:S(2)}, u32[]{:S(2)}) collective-permute-start(bf16[16,4224]{1,0:T(8,128)(2,1)S(1)} %collective-permute-done.3.refs_4_), channel_id=1, source_target_pairs={{0,224},{32,0},{64,32},{96,64},{128,96},{160,128},{192,160},{224,1... | collective-permute-start | bytes 405512 | tf_op jit(solution)/shard_map/ppermute | solution.py:370
  20.5 1.8 %collective-permute-start.7 = (bf16[16,2176]{1,0:T(8,128)(2,1)S(1)}, bf16[16,2176]{1,0:T(8,128)(2,1)S(1)}, u32[]{:S(2)}, u32[]{:S(2)}) collective-permute-start(bf16[16,2176]{1,0:T(8,128)(2,1)S(1)} %slice.13), channel_id=1, source_target_pairs={{0,192},{32,224},{64,0},{96,32},{128,64},{160,96},{192,128},{224,1... | collective-permute-start | bytes 208904 | tf_op jit(solution)/shard_map/ppermute | solution.py:370
  22.3 1.2 collective-permute-start.6
  23.5 5.9 %collective-permute-done.6.refs_7_ = bf16[16,2048]{1,0:T(8,128)(2,1)S(1)} collective-permute-done((bf16[16,2048]{1,0:T(8,128)(2,1)S(1)}, bf16[16,2048]{1,0:T(8,128)(2,1)S(1)}, u32[]{:S(2)}, u32[]{:S(2)}) %collective-permute-start.6) | collective-permute-done | bytes 65568 | tf_op jit(solution)/shard_map/ppermute | solution.py:370
  29.4 1.2 spread_rows.1
  30.6 31.8 %all_to_all.10 = bf16[16,32,2048]{2,1,0:T(8,128)(2,1)S(1)} all-to-all(bf16[16,32,2048]{2,1,0:T(8,128)(2,1)S(1)} %get-tuple-element.57), channel_id=1, replica_groups=mesh['z'=8,'y'=4,'x'=4,'core'=2] {'y','x'}, dimensions={0} | all-to-all | bytes 4194304 | tf_op jit(solution)/shard_map/all_to_all | solution.py:366
  63.8 1.9 %forward_rows.2 = (bf16[256,2048]{1,0:T(8,128)(2,1)S(1)}, bf16[256,384]{1,0:T(8,128)(2,1)S(1)}, f32[256,384]{1,0:T(8,128)S(1)}, f32[256,384]{1,0:T(8,128)S(1)}) custom-call(bf16[256,2048]{1,0:T(8,128)(2,1)S(1)} %bitcast.10, bf16[2048,768]{1,0:T(8,128)(2,1)S(1)} %hold_weights.1.both_ref, bf16[1,384,2048]{2,1,0:T(8,128)(2,1)S(1)} %copy-done), custom_call_target="tpu_custom_call" | custom-call | flops 1207959552 | bytes 5242880 | tf_op jit(solution)/shard_map/forward_rows/pallas_call | solution.py:191
  65.7 1.9 %forward_rows.3 = (bf16[256,2048]{1,0:T(8,128)(2,1)S(1)}, bf16[256,384]{1,0:T(8,128)(2,1)S(1)}, f32[256,384]{1,0:T(8,128)S(1)}, f32[256,384]{1,0:T(8,128)S(1)}) custom-call(bf16[256,2048]{1,0:T(8,128)(2,1)S(1)} %collective-permute-done.8.in_ref.x_b, bf16[2048,768]{1,0:T(8,128)(2,1)S(1)} %hold_weights.1.both_ref, bf16[1,384,2048]{2,1,0:T(8,128)(2,1)S(1)} %copy-done), custom_call_target="tpu_custom_call" | custom-call | flops 1207959552 | bytes 5242880 | tf_op jit(solution)/shard_map/forward_rows/pallas_call | solution.py:191
  67.7 1.7 %backward_rows.3 = (bf16[256,2048]{1,0:T(8,128)(2,1)S(1)}, bf16[256,768]{1,0:T(8,128)(2,1)S(1)}) custom-call(bf16[256,2048]{1,0:T(8,128)(2,1)S(1)} %collective-permute-done.10.in_ref.g_b, f32[256,384]{1,0:T(8,128)S(1)} %get-tuple-element.68.gate_in, f32[256,384]{1,0:T(8,128)S(1)} %get-tuple-element.69.up_in, bf16[2048,768]{1,0:T(8,128)(2,1)S(1)} %hold_weights.1.both_ref, ...), custom_call_target="tpu_custom_call" | custom-call | flops 1207959552 | bytes 5242880 | tf_op jit(solution)/shard_map/backward_rows/pallas_call | solution.py:203
  70.3 1.7 %backward_rows.2 = (bf16[256,2048]{1,0:T(8,128)(2,1)S(1)}, bf16[256,768]{1,0:T(8,128)(2,1)S(1)}) custom-call(bf16[256,2048]{1,0:T(8,128)(2,1)S(1)} %bitcast.7, f32[256,384]{1,0:T(8,128)S(1)} %get-tuple-element.65.gate_in, f32[256,384]{1,0:T(8,128)S(1)} %get-tuple-element.66.up_in, bf16[2048,768]{1,0:T(8,128)(2,1)S(1)} %hold_weights.1.both_ref, ...), custom_call_target="tpu_custom_call" | custom-call | flops 1207959552 | bytes 5242880 | tf_op jit(solution)/shard_map/backward_rows/pallas_call | solution.py:203
  72.8 32.0 %all_to_all.11.back_ref = bf16[16,32,2048]{2,1,0:T(8,128)(2,1)S(1)} all-to-all(bf16[16,32,2048]{2,1,0:T(8,128)(2,1)S(1)} %sum_halves.1), channel_id=1, replica_groups=mesh['z'=8,'y'=4,'x'=4,'core'=2] {'y','x'}, dimensions={0} | all-to-all | bytes 4194304 | tf_op jit(solution)/shard_map/all_to_all | solution.py:366
  104.7 1.2 combine_rows.1
  106.1 2.0 %collective-permute-start.13 = (bf16[32,4224]{1,0:T(8,128)(2,1)S(1)}, bf16[32,4224]{1,0:T(8,128)(2,1)S(1)}, u32[]{:S(2)}, u32[]{:S(2)}) collective-permute-start(bf16[32,4224]{1,0:T(8,128)(2,1)S(1)} %get-tuple-element.78), channel_id=1, source_target_pairs={{0,32},{32,64},{64,96},{96,128},{128,160},{160,192},{192,224},{224... | collective-permute-start | bytes 811016 | tf_op jit(solution)/shard_map/ppermute | solution.py:370
  108.1 1.2 collective-permute-start.14
  109.3 2.9 %collective-permute-start.15 = (bf16[16,2176]{1,0:T(8,128)(2,1)S(1)}, bf16[16,2176]{1,0:T(8,128)(2,1)S(1)}, u32[]{:S(2)}, u32[]{:S(2)}) collective-permute-start(bf16[16,2176]{1,0:T(8,128)(2,1)S(1)} %get-tuple-element.81), channel_id=1, source_target_pairs={{0,192},{32,224},{64,0},{96,32},{128,64},{160,96},{192,128},{224,1... | collective-permute-start | bytes 208904 | tf_op jit(solution)/shard_map/ppermute | solution.py:370
  112.2 4.6 %weight_grads.1 = (bf16[1,2048,384]{2,1,0:T(8,128)(2,1)}, bf16[1,2048,384]{2,1,0:T(8,128)(2,1)}, bf16[1,384,2048]{2,1,0:T(8,128)(2,1)}) custom-call(bf16[256,2048]{1,0:T(8,128)(2,1)S(1)} %bitcast.11, bf16[256,2048]{1,0:T(8,128)(2,1)S(1)} %bitcast.8, bf16[256,2048]{1,0:T(8,128)(2,1)S(1)} %collective-permute-done.8.in_ref.x_b, ...), custom_call_target="tpu_custom_call" | custom-call | flops 2415919104 | bytes 12582912 | tf_op jit(solution)/shard_map/weight_grads/pallas_call | solution.py:244
  117.2 2.0 %collective-permute-start.16 = (bf16[16,4224]{1,0:T(8,128)(2,1)S(1)}, bf16[16,4224]{1,0:T(8,128)(2,1)S(1)}, u32[]{:S(2)}, u32[]{:S(2)}) collective-permute-start(bf16[16,4224]{1,0:T(8,128)(2,1)S(1)} %get-tuple-element.92), channel_id=1, source_target_pairs={{0,64},{32,96},{64,128},{96,160},{128,192},{160,224},{192,0},{224,... | collective-permute-start | bytes 405512 | tf_op jit(solution)/shard_map/ppermute | solution.py:370
  119.3 2.2 %collective-permute-start.17 = (bf16[16,4224]{1,0:T(8,128)(2,1)S(1)}, bf16[16,4224]{1,0:T(8,128)(2,1)S(1)}, u32[]{:S(2)}, u32[]{:S(2)}) collective-permute-start(bf16[16,4224]{1,0:T(8,128)(2,1)S(1)} %get-tuple-element.93), channel_id=1, source_target_pairs={{0,192},{32,224},{64,0},{96,32},{128,64},{160,96},{192,128},{224,1... | collective-permute-start | bytes 405512 | tf_op jit(solution)/shard_map/ppermute | solution.py:370
  121.5 5.1 %collective-permute-done.16.refs_3_ = bf16[16,4224]{1,0:T(8,128)(2,1)S(1)} collective-permute-done((bf16[16,4224]{1,0:T(8,128)(2,1)S(1)}, bf16[16,4224]{1,0:T(8,128)(2,1)S(1)}, u32[]{:S(2)}, u32[]{:S(2)}) %collective-permute-start.16) | collective-permute-done | bytes 135200 | tf_op jit(solution)/shard_map/ppermute | solution.py:370
  (37 shorter events, 6.8 us)
Async XLA Ops:
  2.2 10.7 %collective-permute-start.3 = (bf16[16,4224]{1,0:T(8,128)(2,1)}, bf16[16,4224]{1,0:T(8,128)(2,1)S(1)}, u32[]{:S(2)}, u32[]{:S(2)}) collective-permute-start(bf16[16,4224]{1,0:T(8,128)(2,1)} %pack_rows.1.refs_0_), channel_id=1, source_target_pairs={{0,192},{32,224},{64,0},{96,32},{128,64},{160,96},{192,128},{224,1... | collective-permute-start | bytes 405512 | tf_op jit(solution)/shard_map/ppermute | solution.py:370
  7.7 10.7 %collective-permute-start.2 = (bf16[16,4224]{1,0:T(8,128)(2,1)}, bf16[16,4224]{1,0:T(8,128)(2,1)S(1)}, u32[]{:S(2)}, u32[]{:S(2)}) collective-permute-start(bf16[16,4224]{1,0:T(8,128)(2,1)} %pack_rows.1.refs_0_), channel_id=1, source_target_pairs={{0,64},{32,96},{64,128},{96,160},{128,192},{160,224},{192,0},{224,... | collective-permute-start | bytes 405512 | tf_op jit(solution)/shard_map/ppermute | solution.py:370
  7.7 14.6 %collective-permute-start.1 = (bf16[16,4224]{1,0:T(8,128)(2,1)}, bf16[16,4224]{1,0:T(8,128)(2,1)S(1)}, u32[]{:S(2)}, u32[]{:S(2)}) collective-permute-start(bf16[16,4224]{1,0:T(8,128)(2,1)} %pack_rows.1.refs_0_), channel_id=1, source_target_pairs={{0,224},{32,0},{64,32},{96,64},{128,96},{160,128},{192,160},{224,1... | collective-permute-start | bytes 405512 | tf_op jit(solution)/shard_map/ppermute | solution.py:370
  8.7 14.7 %collective-permute-start = (bf16[16,4224]{1,0:T(8,128)(2,1)}, bf16[16,4224]{1,0:T(8,128)(2,1)S(1)}, u32[]{:S(2)}, u32[]{:S(2)}) collective-permute-start(bf16[16,4224]{1,0:T(8,128)(2,1)} %pack_rows.1.refs_0_), channel_id=1, source_target_pairs={{0,32},{32,64},{64,96},{96,128},{128,160},{160,192},{192,224},{224... | collective-permute-start | bytes 405512 | tf_op jit(solution)/shard_map/ppermute | solution.py:370
  9.7 1.4 %copy-start.1 = (bf16[1,2048,384]{2,1,0:T(8,128)(2,1)S(1)}, bf16[1,2048,384]{2,1,0:T(8,128)(2,1)}, u32[]{:S(2)}) copy-start(bf16[1,2048,384]{2,1,0:T(8,128)(2,1)} %gate_hbm.1) | copy-start | bytes 4718596
  11.2 1.4 %copy-start.2 = (bf16[1,2048,384]{2,1,0:T(8,128)(2,1)S(1)}, bf16[1,2048,384]{2,1,0:T(8,128)(2,1)}, u32[]{:S(2)}) copy-start(bf16[1,2048,384]{2,1,0:T(8,128)(2,1)} %up_hbm.1) | copy-start | bytes 4718596
  12.6 16.9 %copy-start.3 = (bf16[16,4224]{1,0:T(8,128)(2,1)S(1)}, bf16[16,4224]{1,0:T(8,128)(2,1)}, u32[]{:S(2)}) copy-start(bf16[16,4224]{1,0:T(8,128)(2,1)} %pack_rows.1.refs_0_) | copy-start | bytes 405508
  18.4 11.0 %collective-permute-start.4 = (bf16[16,4224]{1,0:T(8,128)(2,1)S(1)}, bf16[16,4224]{1,0:T(8,128)(2,1)S(1)}, u32[]{:S(2)}, u32[]{:S(2)}) collective-permute-start(bf16[16,4224]{1,0:T(8,128)(2,1)S(1)} %collective-permute-done.2.refs_3_), channel_id=1, source_target_pairs={{0,32},{32,64},{64,96},{96,128},{128,160},{160,192},{192,224},{224... | collective-permute-start | bytes 405512 | tf_op jit(solution)/shard_map/ppermute | solution.py:370
  18.4 11.0 %collective-permute-start.5 = (bf16[16,4224]{1,0:T(8,128)(2,1)S(1)}, bf16[16,4224]{1,0:T(8,128)(2,1)S(1)}, u32[]{:S(2)}, u32[]{:S(2)}) collective-permute-start(bf16[16,4224]{1,0:T(8,128)(2,1)S(1)} %collective-permute-done.3.refs_4_), channel_id=1, source_target_pairs={{0,224},{32,0},{64,32},{96,64},{128,96},{160,128},{192,160},{224,1... | collective-permute-start | bytes 405512 | tf_op jit(solution)/shard_map/ppermute | solution.py:370
  20.5 9.0 %collective-permute-start.7 = (bf16[16,2176]{1,0:T(8,128)(2,1)S(1)}, bf16[16,2176]{1,0:T(8,128)(2,1)S(1)}, u32[]{:S(2)}, u32[]{:S(2)}) collective-permute-start(bf16[16,2176]{1,0:T(8,128)(2,1)S(1)} %slice.13), channel_id=1, source_target_pairs={{0,192},{32,224},{64,0},{96,32},{128,64},{160,96},{192,128},{224,1... | collective-permute-start | bytes 208904 | tf_op jit(solution)/shard_map/ppermute | solution.py:370
  22.3 7.1 %collective-permute-start.6 = (bf16[16,2048]{1,0:T(8,128)(2,1)S(1)}, bf16[16,2048]{1,0:T(8,128)(2,1)S(1)}, u32[]{:S(2)}, u32[]{:S(2)}) collective-permute-start(bf16[16,2048]{1,0:T(8,128)(2,1)S(1)} %slice.12), channel_id=1, source_target_pairs={{0,64},{32,96},{64,128},{96,160},{128,192},{160,224},{192,0},{224,... | collective-permute-start | bytes 196616 | tf_op jit(solution)/shard_map/ppermute | solution.py:370
  62.4 1.4 %copy-start = (bf16[1,384,2048]{2,1,0:T(8,128)(2,1)S(1)}, bf16[1,384,2048]{2,1,0:T(8,128)(2,1)}, u32[]{:S(2)}) copy-start(bf16[1,384,2048]{2,1,0:T(8,128)(2,1)} %down_ref.7) | copy-start | bytes 4718596
  62.7 3.0 %collective-permute-start.8 = (bf16[256,2048]{1,0:T(8,128)(2,1)S(1)}, bf16[256,2048]{1,0:T(8,128)(2,1)S(1)}, u32[]{:S(2)}, u32[]{:S(2)}) collective-permute-start(bf16[256,2048]{1,0:T(8,128)(2,1)S(1)} %bitcast.9), channel_id=1, source_target_pairs={{0,1},{1,0},{2,3},{3,2},{4,5},{5,4},{6,7},{7,6},{8,9},{9,8},{10,11... | collective-permute-start | bytes 3145736 | tf_op jit(solution)/shard_map/ppermute | solution.py:362
  62.8 4.9 %collective-permute-start.10 = (bf16[256,2048]{1,0:T(8,128)(2,1)S(1)}, bf16[256,2048]{1,0:T(8,128)(2,1)S(1)}, u32[]{:S(2)}, u32[]{:S(2)}) collective-permute-start(bf16[256,2048]{1,0:T(8,128)(2,1)S(1)} %bitcast.6), channel_id=1, source_target_pairs={{0,1},{1,0},{2,3},{3,2},{4,5},{5,4},{6,7},{7,6},{8,9},{9,8},{10,11... | collective-permute-start | bytes 3145736 | tf_op jit(solution)/shard_map/ppermute | solution.py:362
  67.6 2.7 %collective-permute-start.9 = (bf16[256,2048]{1,0:T(8,128)(2,1)S(1)}, bf16[256,2048]{1,0:T(8,128)(2,1)S(1)}, u32[]{:S(2)}, u32[]{:S(2)}) collective-permute-start(bf16[256,2048]{1,0:T(8,128)(2,1)S(1)} %get-tuple-element.62), channel_id=1, source_target_pairs={{0,1},{1,0},{2,3},{3,2},{4,5},{5,4},{6,7},{7,6},{8,9},{9,8},{10,11... | collective-permute-start | bytes 3145736 | tf_op jit(solution)/shard_map/ppermute | solution.py:362
  69.4 2.9 %collective-permute-start.11 = (bf16[256,2048]{1,0:T(8,128)(2,1)S(1)}, bf16[256,2048]{1,0:T(8,128)(2,1)S(1)}, u32[]{:S(2)}, u32[]{:S(2)}) collective-permute-start(bf16[256,2048]{1,0:T(8,128)(2,1)S(1)} %get-tuple-element.70), channel_id=1, source_target_pairs={{0,1},{1,0},{2,3},{3,2},{4,5},{5,4},{6,7},{7,6},{8,9},{9,8},{10,11... | collective-permute-start | bytes 3145736 | tf_op jit(solution)/shard_map/ppermute | solution.py:362
  106.0 11.2 %collective-permute-start.12 = (bf16[32,4224]{1,0:T(8,128)(2,1)S(1)}, bf16[32,4224]{1,0:T(8,128)(2,1)S(1)}, u32[]{:S(2)}, u32[]{:S(2)}) collective-permute-start(bf16[32,4224]{1,0:T(8,128)(2,1)S(1)} %get-tuple-element.77), channel_id=1, source_target_pairs={{0,224},{32,0},{64,32},{96,64},{128,96},{160,128},{192,160},{224,1... | collective-permute-start | bytes 811016 | tf_op jit(solution)/shard_map/ppermute | solution.py:370
  106.1 11.1 %collective-permute-start.13 = (bf16[32,4224]{1,0:T(8,128)(2,1)S(1)}, bf16[32,4224]{1,0:T(8,128)(2,1)S(1)}, u32[]{:S(2)}, u32[]{:S(2)}) collective-permute-start(bf16[32,4224]{1,0:T(8,128)(2,1)S(1)} %get-tuple-element.78), channel_id=1, source_target_pairs={{0,32},{32,64},{64,96},{96,128},{128,160},{160,192},{192,224},{224... | collective-permute-start | bytes 811016 | tf_op jit(solution)/shard_map/ppermute | solution.py:370
  108.1 9.1 %collective-permute-start.14 = (bf16[16,2048]{1,0:T(8,128)(2,1)S(1)}, bf16[16,2048]{1,0:T(8,128)(2,1)S(1)}, u32[]{:S(2)}, u32[]{:S(2)}) collective-permute-start(bf16[16,2048]{1,0:T(8,128)(2,1)S(1)} %get-tuple-element.80), channel_id=1, source_target_pairs={{0,64},{32,96},{64,128},{96,160},{128,192},{160,224},{192,0},{224,... | collective-permute-start | bytes 196616 | tf_op jit(solution)/shard_map/ppermute | solution.py:370
  109.3 7.8 %collective-permute-start.15 = (bf16[16,2176]{1,0:T(8,128)(2,1)S(1)}, bf16[16,2176]{1,0:T(8,128)(2,1)S(1)}, u32[]{:S(2)}, u32[]{:S(2)}) collective-permute-start(bf16[16,2176]{1,0:T(8,128)(2,1)S(1)} %get-tuple-element.81), channel_id=1, source_target_pairs={{0,192},{32,224},{64,0},{96,32},{128,64},{160,96},{192,128},{224,1... | collective-permute-start | bytes 208904 | tf_op jit(solution)/shard_map/ppermute | solution.py:370
  117.2 9.3 %collective-permute-start.16 = (bf16[16,4224]{1,0:T(8,128)(2,1)S(1)}, bf16[16,4224]{1,0:T(8,128)(2,1)S(1)}, u32[]{:S(2)}, u32[]{:S(2)}) collective-permute-start(bf16[16,4224]{1,0:T(8,128)(2,1)S(1)} %get-tuple-element.92), channel_id=1, source_target_pairs={{0,64},{32,96},{64,128},{96,160},{128,192},{160,224},{192,0},{224,... | collective-permute-start | bytes 405512 | tf_op jit(solution)/shard_map/ppermute | solution.py:370
  119.3 7.3 %collective-permute-start.17 = (bf16[16,4224]{1,0:T(8,128)(2,1)S(1)}, bf16[16,4224]{1,0:T(8,128)(2,1)S(1)}, u32[]{:S(2)}, u32[]{:S(2)}) collective-permute-start(bf16[16,4224]{1,0:T(8,128)(2,1)S(1)} %get-tuple-element.93), channel_id=1, source_target_pairs={{0,192},{32,224},{64,0},{96,32},{128,64},{160,96},{192,128},{224,1... | collective-permute-start | bytes 405512 | tf_op jit(solution)/shard_map/ppermute | solution.py:370

commit v5 on v4

--- a/solution.py
+++ b/solution.py
@@ -277,10 +277,12 @@
     weight = weight_ref[...]
     high = weight.astype(BF16)
     low = (weight - high.astype(F32)).astype(BF16)
+    both = jnp.concatenate([high, low], axis=0)
     products = jnp.zeros((GROUP, ROWS), F32)
     for i in range(0, D, 512):
         part = back_ref[:, :SENT, i : i + 512].reshape(ROWS, 512)
-        put(dot(high, part, 1, 0) + dot(low, part, 1, 0), i)
+        total = dot(both, part, 1, 0)
+        put(total[:GROUP] + total[GROUP:], i)
         products = products + dot(all_ref[:, D + i : D + i + 512], part, 1, 1)
         put(dot(mask, back_ref[:, SENT:, i : i + 512].reshape(ROWS, 512), 1, 0), D + i)
     meta = all_ref[:, 2 * D :].astype(F32)
@@ -373,7 +375,7 @@
 def spread_z(own, weights):
     below2, above2 = shift(own, 2), shift(own, -2)
     below, above = shift(own, 1), shift(own, -1)
-    below2, above2, held = lax.optimization_barrier((below2, above2, hold(*weights)))
+    above2, held = lax.optimization_barrier((above2, hold(*weights)))
     half, other_half = shift(below2[:, :D], 2), shift(above2[:, D:], -2)
     below3, above3 = shift(below2, 1), shift(above2, -1)
     return (own, below, above, below2, above2, below3, above3, half, other_half), held

time: 128 us -> 128 us (level)
  no operation moved by 1% of the time
where the time goes in v5:
time: 128 us; the launch traced here: 127 us
  blocking collectives  63.8 us (50%)
  starting transfers between devices  24.2 us (19%)
  waiting for transfers between devices  17.5 us (14%)
  Pallas kernels  17.3 us (14%)
  local copies, waits for them, and re-layouts  3.63 us (3%)
    all_to_all x2, blocking collectives, over_plane(): return lax.all_to_all(blocks, ('y', 'x'), 0, 0, tiled=True)  63.8 us
    ppermute x14, starting transfers between devices, shift(): lax.ppermute(value, 'z', [(i, (i + step) % PLANES) for i in range(PLANES)])  23 us
    ppermute x14, waiting for transfers between devices, shift(): lax.ppermute(value, 'z', [(i, (i + step) % PLANES) for i in range(PLANES)])  16.9 us
    pallas_call x1, Pallas kernels, weight_grads(): pl.pallas_call(weight_grad_kernel, grid=(steps,), out_shape=(jax.ShapeDty...  4.57 us
    pallas_call x2, Pallas kernels, forward(): pl.pallas_call(forward_kernel, out_shape=(WIDE, ACT, ACT32, ACT32), in_sp...  3.74 us
    pallas_call x2, Pallas kernels, backward(): pl.pallas_call(backward_kernel, out_shape=(WIDE, jax.ShapeDtypeStruct((RO...  3.4 us
    unnamed x8, local copies, waits for them, and re-layouts  3.38 us
  transfers between devices with their start and end apart: 18, of which 6 were waited for; matrix products, arithmetic and copies ran while one was open for 0% of the time, Pallas kernels for 9%

profile of v5, /device:TPU:32, one launch (start us, length us, event | category | flops | bytes accessed | tf_op | source)
XLA Modules:
  0.0 127.3 jit_solution(13709933839111810652)
XLA Ops:
  0.6 1.6 %pack_rows.1.refs_0_ = bf16[16,4224]{1,0:T(8,128)(2,1)} custom-call(bf16[16,2048]{1,0:T(8,128)(2,1)} %tok_hbm, bf16[16,2048]{1,0:T(8,128)(2,1)} %grad_hbm.1, s32[8,16]{1,0:T(8,128)} %bitcast.12, f32[8,16]{1,0:T(8,128)} %bitcast.13), custom_call_target="tpu_custom_call" | custom-call | tf_op jit(solution)/shard_map/pack_rows/pallas_call | solution.py:71
  2.2 5.5 %collective-permute-start.3 = (bf16[16,4224]{1,0:T(8,128)(2,1)}, bf16[16,4224]{1,0:T(8,128)(2,1)S(1)}, u32[]{:S(2)}, u32[]{:S(2)}) collective-permute-start(bf16[16,4224]{1,0:T(8,128)(2,1)} %pack_rows.1.refs_0_), channel_id=1, source_target_pairs={{0,192},{32,224},{64,0},{96,32},{128,64},{160,96},{192,128},{224,1... | collective-permute-start | bytes 405512 | tf_op jit(solution)/shard_map/ppermute | solution.py:372
  9.8 1.4 %copy-done.1 = bf16[1,2048,384]{2,1,0:T(8,128)(2,1)S(1)} copy-done((bf16[1,2048,384]{2,1,0:T(8,128)(2,1)S(1)}, bf16[1,2048,384]{2,1,0:T(8,128)(2,1)}, u32[]{:S(2)}) %copy-start.1) | copy-done | bytes 1572888
  11.2 1.4 %copy-done.2 = bf16[1,2048,384]{2,1,0:T(8,128)(2,1)S(1)} copy-done((bf16[1,2048,384]{2,1,0:T(8,128)(2,1)S(1)}, bf16[1,2048,384]{2,1,0:T(8,128)(2,1)}, u32[]{:S(2)}) %copy-start.2) | copy-done | bytes 1572888
  12.9 5.5 %collective-permute-done.2.refs_3_ = bf16[16,4224]{1,0:T(8,128)(2,1)S(1)} collective-permute-done((bf16[16,4224]{1,0:T(8,128)(2,1)}, bf16[16,4224]{1,0:T(8,128)(2,1)S(1)}, u32[]{:S(2)}, u32[]{:S(2)}) %collective-permute-start.2) | collective-permute-done | bytes 135200 | tf_op jit(solution)/shard_map/ppermute | solution.py:372
  18.4 2.0 %collective-permute-start.5 = (bf16[16,4224]{1,0:T(8,128)(2,1)S(1)}, bf16[16,4224]{1,0:T(8,128)(2,1)S(1)}, u32[]{:S(2)}, u32[]{:S(2)}) collective-permute-start(bf16[16,4224]{1,0:T(8,128)(2,1)S(1)} %collective-permute-done.3.refs_4_), channel_id=1, source_target_pairs={{0,224},{32,0},{64,32},{96,64},{128,96},{160,128},{192,160},{224,1... | collective-permute-start | bytes 405512 | tf_op jit(solution)/shard_map/ppermute | solution.py:372
  20.5 1.8 %collective-permute-start.7 = (bf16[16,2176]{1,0:T(8,128)(2,1)S(1)}, bf16[16,2176]{1,0:T(8,128)(2,1)S(1)}, u32[]{:S(2)}, u32[]{:S(2)}) collective-permute-start(bf16[16,2176]{1,0:T(8,128)(2,1)S(1)} %slice.13), channel_id=1, source_target_pairs={{0,192},{32,224},{64,0},{96,32},{128,64},{160,96},{192,128},{224,1... | collective-permute-start | bytes 208904 | tf_op jit(solution)/shard_map/ppermute | solution.py:372
  22.3 1.2 collective-permute-start.6
  23.5 5.9 %collective-permute-done.6.refs_7_ = bf16[16,2048]{1,0:T(8,128)(2,1)S(1)} collective-permute-done((bf16[16,2048]{1,0:T(8,128)(2,1)S(1)}, bf16[16,2048]{1,0:T(8,128)(2,1)S(1)}, u32[]{:S(2)}, u32[]{:S(2)}) %collective-permute-start.6) | collective-permute-done | bytes 65568 | tf_op jit(solution)/shard_map/ppermute | solution.py:372
  29.4 1.2 spread_rows.1
  30.6 31.8 %all_to_all.10 = bf16[16,32,2048]{2,1,0:T(8,128)(2,1)S(1)} all-to-all(bf16[16,32,2048]{2,1,0:T(8,128)(2,1)S(1)} %get-tuple-element.55), channel_id=1, replica_groups=mesh['z'=8,'y'=4,'x'=4,'core'=2] {'y','x'}, dimensions={0} | all-to-all | bytes 4194304 | tf_op jit(solution)/shard_map/all_to_all | solution.py:368
  63.8 1.9 %forward_rows.2 = (bf16[256,2048]{1,0:T(8,128)(2,1)S(1)}, bf16[256,384]{1,0:T(8,128)(2,1)S(1)}, f32[256,384]{1,0:T(8,128)S(1)}, f32[256,384]{1,0:T(8,128)S(1)}) custom-call(bf16[256,2048]{1,0:T(8,128)(2,1)S(1)} %bitcast.10, bf16[2048,768]{1,0:T(8,128)(2,1)S(1)} %hold_weights.1.both_ref, bf16[1,384,2048]{2,1,0:T(8,128)(2,1)S(1)} %copy-done), custom_call_target="tpu_custom_call" | custom-call | flops 1207959552 | bytes 5242880 | tf_op jit(solution)/shard_map/forward_rows/pallas_call | solution.py:191
  65.7 1.9 %forward_rows.3 = (bf16[256,2048]{1,0:T(8,128)(2,1)S(1)}, bf16[256,384]{1,0:T(8,128)(2,1)S(1)}, f32[256,384]{1,0:T(8,128)S(1)}, f32[256,384]{1,0:T(8,128)S(1)}) custom-call(bf16[256,2048]{1,0:T(8,128)(2,1)S(1)} %collective-permute-done.8.in_ref.x_b, bf16[2048,768]{1,0:T(8,128)(2,1)S(1)} %hold_weights.1.both_ref, bf16[1,384,2048]{2,1,0:T(8,128)(2,1)S(1)} %copy-done), custom_call_target="tpu_custom_call" | custom-call | flops 1207959552 | bytes 5242880 | tf_op jit(solution)/shard_map/forward_rows/pallas_call | solution.py:191
  67.7 1.7 %backward_rows.3 = (bf16[256,2048]{1,0:T(8,128)(2,1)S(1)}, bf16[256,768]{1,0:T(8,128)(2,1)S(1)}) custom-call(bf16[256,2048]{1,0:T(8,128)(2,1)S(1)} %collective-permute-done.10.in_ref.g_b, f32[256,384]{1,0:T(8,128)S(1)} %get-tuple-element.66.gate_in, f32[256,384]{1,0:T(8,128)S(1)} %get-tuple-element.67.up_in, bf16[2048,768]{1,0:T(8,128)(2,1)S(1)} %hold_weights.1.both_ref, ...), custom_call_target="tpu_custom_call" | custom-call | flops 1207959552 | bytes 5242880 | tf_op jit(solution)/shard_map/backward_rows/pallas_call | solution.py:203
  70.3 1.7 %backward_rows.2 = (bf16[256,2048]{1,0:T(8,128)(2,1)S(1)}, bf16[256,768]{1,0:T(8,128)(2,1)S(1)}) custom-call(bf16[256,2048]{1,0:T(8,128)(2,1)S(1)} %bitcast.7, f32[256,384]{1,0:T(8,128)S(1)} %get-tuple-element.63.gate_in, f32[256,384]{1,0:T(8,128)S(1)} %get-tuple-element.64.up_in, bf16[2048,768]{1,0:T(8,128)(2,1)S(1)} %hold_weights.1.both_ref, ...), custom_call_target="tpu_custom_call" | custom-call | flops 1207959552 | bytes 5242880 | tf_op jit(solution)/shard_map/backward_rows/pallas_call | solution.py:203
  72.8 32.0 %all_to_all.11.back_ref = bf16[16,32,2048]{2,1,0:T(8,128)(2,1)S(1)} all-to-all(bf16[16,32,2048]{2,1,0:T(8,128)(2,1)S(1)} %sum_halves.1), channel_id=1, replica_groups=mesh['z'=8,'y'=4,'x'=4,'core'=2] {'y','x'}, dimensions={0} | all-to-all | bytes 4194304 | tf_op jit(solution)/shard_map/all_to_all | solution.py:368
  104.7 1.2 combine_rows.1
  106.0 2.0 %collective-permute-start.13 = (bf16[32,4224]{1,0:T(8,128)(2,1)S(1)}, bf16[32,4224]{1,0:T(8,128)(2,1)S(1)}, u32[]{:S(2)}, u32[]{:S(2)}) collective-permute-start(bf16[32,4224]{1,0:T(8,128)(2,1)S(1)} %get-tuple-element.76), channel_id=1, source_target_pairs={{0,32},{32,64},{64,96},{96,128},{128,160},{160,192},{192,224},{224... | collective-permute-start | bytes 811016 | tf_op jit(solution)/shard_map/ppermute | solution.py:372
  108.0 1.2 collective-permute-start.14
  109.3 2.9 %collective-permute-start.15 = (bf16[16,2176]{1,0:T(8,128)(2,1)S(1)}, bf16[16,2176]{1,0:T(8,128)(2,1)S(1)}, u32[]{:S(2)}, u32[]{:S(2)}) collective-permute-start(bf16[16,2176]{1,0:T(8,128)(2,1)S(1)} %get-tuple-element.79), channel_id=1, source_target_pairs={{0,192},{32,224},{64,0},{96,32},{128,64},{160,96},{192,128},{224,1... | collective-permute-start | bytes 208904 | tf_op jit(solution)/shard_map/ppermute | solution.py:372
  112.2 4.6 %weight_grads.1 = (bf16[1,2048,384]{2,1,0:T(8,128)(2,1)}, bf16[1,2048,384]{2,1,0:T(8,128)(2,1)}, bf16[1,384,2048]{2,1,0:T(8,128)(2,1)}) custom-call(bf16[256,2048]{1,0:T(8,128)(2,1)S(1)} %bitcast.11, bf16[256,2048]{1,0:T(8,128)(2,1)S(1)} %bitcast.8, bf16[256,2048]{1,0:T(8,128)(2,1)S(1)} %collective-permute-done.8.in_ref.x_b, ...), custom_call_target="tpu_custom_call" | custom-call | flops 2415919104 | bytes 12582912 | tf_op jit(solution)/shard_map/weight_grads/pallas_call | solution.py:244
  117.2 2.0 %collective-permute-start.16 = (bf16[16,4224]{1,0:T(8,128)(2,1)S(1)}, bf16[16,4224]{1,0:T(8,128)(2,1)S(1)}, u32[]{:S(2)}, u32[]{:S(2)}) collective-permute-start(bf16[16,4224]{1,0:T(8,128)(2,1)S(1)} %get-tuple-element.90), channel_id=1, source_target_pairs={{0,64},{32,96},{64,128},{96,160},{128,192},{160,224},{192,0},{224,... | collective-permute-start | bytes 405512 | tf_op jit(solution)/shard_map/ppermute | solution.py:372
  119.2 2.2 %collective-permute-start.17 = (bf16[16,4224]{1,0:T(8,128)(2,1)S(1)}, bf16[16,4224]{1,0:T(8,128)(2,1)S(1)}, u32[]{:S(2)}, u32[]{:S(2)}) collective-permute-start(bf16[16,4224]{1,0:T(8,128)(2,1)S(1)} %get-tuple-element.91), channel_id=1, source_target_pairs={{0,192},{32,224},{64,0},{96,32},{128,64},{160,96},{192,128},{224,1... | collective-permute-start | bytes 405512 | tf_op jit(solution)/shard_map/ppermute | solution.py:372
  121.4 5.1 %collective-permute-done.16.refs_3_ = bf16[16,4224]{1,0:T(8,128)(2,1)S(1)} collective-permute-done((bf16[16,4224]{1,0:T(8,128)(2,1)S(1)}, bf16[16,4224]{1,0:T(8,128)(2,1)S(1)}, u32[]{:S(2)}, u32[]{:S(2)}) %collective-permute-start.16) | collective-permute-done | bytes 135200 | tf_op jit(solution)/shard_map/ppermute | solution.py:372
  (37 shorter events, 6.8 us)
Async XLA Ops:
  2.2 10.7 %collective-permute-start.3 = (bf16[16,4224]{1,0:T(8,128)(2,1)}, bf16[16,4224]{1,0:T(8,128)(2,1)S(1)}, u32[]{:S(2)}, u32[]{:S(2)}) collective-permute-start(bf16[16,4224]{1,0:T(8,128)(2,1)} %pack_rows.1.refs_0_), channel_id=1, source_target_pairs={{0,192},{32,224},{64,0},{96,32},{128,64},{160,96},{192,128},{224,1... | collective-permute-start | bytes 405512 | tf_op jit(solution)/shard_map/ppermute | solution.py:372
  7.7 10.7 %collective-permute-start.2 = (bf16[16,4224]{1,0:T(8,128)(2,1)}, bf16[16,4224]{1,0:T(8,128)(2,1)S(1)}, u32[]{:S(2)}, u32[]{:S(2)}) collective-permute-start(bf16[16,4224]{1,0:T(8,128)(2,1)} %pack_rows.1.refs_0_), channel_id=1, source_target_pairs={{0,64},{32,96},{64,128},{96,160},{128,192},{160,224},{192,0},{224,... | collective-permute-start | bytes 405512 | tf_op jit(solution)/shard_map/ppermute | solution.py:372
  7.7 14.6 %collective-permute-start.1 = (bf16[16,4224]{1,0:T(8,128)(2,1)}, bf16[16,4224]{1,0:T(8,128)(2,1)S(1)}, u32[]{:S(2)}, u32[]{:S(2)}) collective-permute-start(bf16[16,4224]{1,0:T(8,128)(2,1)} %pack_rows.1.refs_0_), channel_id=1, source_target_pairs={{0,224},{32,0},{64,32},{96,64},{128,96},{160,128},{192,160},{224,1... | collective-permute-start | bytes 405512 | tf_op jit(solution)/shard_map/ppermute | solution.py:372
  8.7 14.7 %collective-permute-start = (bf16[16,4224]{1,0:T(8,128)(2,1)}, bf16[16,4224]{1,0:T(8,128)(2,1)S(1)}, u32[]{:S(2)}, u32[]{:S(2)}) collective-permute-start(bf16[16,4224]{1,0:T(8,128)(2,1)} %pack_rows.1.refs_0_), channel_id=1, source_target_pairs={{0,32},{32,64},{64,96},{96,128},{128,160},{160,192},{192,224},{224... | collective-permute-start | bytes 405512 | tf_op jit(solution)/shard_map/ppermute | solution.py:372
  9.7 1.4 %copy-start.1 = (bf16[1,2048,384]{2,1,0:T(8,128)(2,1)S(1)}, bf16[1,2048,384]{2,1,0:T(8,128)(2,1)}, u32[]{:S(2)}) copy-start(bf16[1,2048,384]{2,1,0:T(8,128)(2,1)} %gate_hbm.1) | copy-start | bytes 4718596
  11.2 1.4 %copy-start.2 = (bf16[1,2048,384]{2,1,0:T(8,128)(2,1)S(1)}, bf16[1,2048,384]{2,1,0:T(8,128)(2,1)}, u32[]{:S(2)}) copy-start(bf16[1,2048,384]{2,1,0:T(8,128)(2,1)} %up_hbm.1) | copy-start | bytes 4718596
  12.6 16.9 %copy-start.3 = (bf16[16,4224]{1,0:T(8,128)(2,1)S(1)}, bf16[16,4224]{1,0:T(8,128)(2,1)}, u32[]{:S(2)}) copy-start(bf16[16,4224]{1,0:T(8,128)(2,1)} %pack_rows.1.refs_0_) | copy-start | bytes 405508
  18.4 11.0 %collective-permute-start.4 = (bf16[16,4224]{1,0:T(8,128)(2,1)S(1)}, bf16[16,4224]{1,0:T(8,128)(2,1)S(1)}, u32[]{:S(2)}, u32[]{:S(2)}) collective-permute-start(bf16[16,4224]{1,0:T(8,128)(2,1)S(1)} %collective-permute-done.2.refs_3_), channel_id=1, source_target_pairs={{0,32},{32,64},{64,96},{96,128},{128,160},{160,192},{192,224},{224... | collective-permute-start | bytes 405512 | tf_op jit(solution)/shard_map/ppermute | solution.py:372
  18.4 11.0 %collective-permute-start.5 = (bf16[16,4224]{1,0:T(8,128)(2,1)S(1)}, bf16[16,4224]{1,0:T(8,128)(2,1)S(1)}, u32[]{:S(2)}, u32[]{:S(2)}) collective-permute-start(bf16[16,4224]{1,0:T(8,128)(2,1)S(1)} %collective-permute-done.3.refs_4_), channel_id=1, source_target_pairs={{0,224},{32,0},{64,32},{96,64},{128,96},{160,128},{192,160},{224,1... | collective-permute-start | bytes 405512 | tf_op jit(solution)/shard_map/ppermute | solution.py:372
  20.5 9.0 %collective-permute-start.7 = (bf16[16,2176]{1,0:T(8,128)(2,1)S(1)}, bf16[16,2176]{1,0:T(8,128)(2,1)S(1)}, u32[]{:S(2)}, u32[]{:S(2)}) collective-permute-start(bf16[16,2176]{1,0:T(8,128)(2,1)S(1)} %slice.13), channel_id=1, source_target_pairs={{0,192},{32,224},{64,0},{96,32},{128,64},{160,96},{192,128},{224,1... | collective-permute-start | bytes 208904 | tf_op jit(solution)/shard_map/ppermute | solution.py:372
  22.3 7.1 %collective-permute-start.6 = (bf16[16,2048]{1,0:T(8,128)(2,1)S(1)}, bf16[16,2048]{1,0:T(8,128)(2,1)S(1)}, u32[]{:S(2)}, u32[]{:S(2)}) collective-permute-start(bf16[16,2048]{1,0:T(8,128)(2,1)S(1)} %slice.16), channel_id=1, source_target_pairs={{0,64},{32,96},{64,128},{96,160},{128,192},{160,224},{192,0},{224,... | collective-permute-start | bytes 196616 | tf_op jit(solution)/shard_map/ppermute | solution.py:372
  62.4 1.4 %copy-start = (bf16[1,384,2048]{2,1,0:T(8,128)(2,1)S(1)}, bf16[1,384,2048]{2,1,0:T(8,128)(2,1)}, u32[]{:S(2)}) copy-start(bf16[1,384,2048]{2,1,0:T(8,128)(2,1)} %down_ref.7) | copy-start | bytes 4718596
  62.7 3.0 %collective-permute-start.8 = (bf16[256,2048]{1,0:T(8,128)(2,1)S(1)}, bf16[256,2048]{1,0:T(8,128)(2,1)S(1)}, u32[]{:S(2)}, u32[]{:S(2)}) collective-permute-start(bf16[256,2048]{1,0:T(8,128)(2,1)S(1)} %bitcast.9), channel_id=1, source_target_pairs={{0,1},{1,0},{2,3},{3,2},{4,5},{5,4},{6,7},{7,6},{8,9},{9,8},{10,11... | collective-permute-start | bytes 3145736 | tf_op jit(solution)/shard_map/ppermute | solution.py:364
  62.8 4.9 %collective-permute-start.10 = (bf16[256,2048]{1,0:T(8,128)(2,1)S(1)}, bf16[256,2048]{1,0:T(8,128)(2,1)S(1)}, u32[]{:S(2)}, u32[]{:S(2)}) collective-permute-start(bf16[256,2048]{1,0:T(8,128)(2,1)S(1)} %bitcast.6), channel_id=1, source_target_pairs={{0,1},{1,0},{2,3},{3,2},{4,5},{5,4},{6,7},{7,6},{8,9},{9,8},{10,11... | collective-permute-start | bytes 3145736 | tf_op jit(solution)/shard_map/ppermute | solution.py:364
  67.6 2.7 %collective-permute-start.9 = (bf16[256,2048]{1,0:T(8,128)(2,1)S(1)}, bf16[256,2048]{1,0:T(8,128)(2,1)S(1)}, u32[]{:S(2)}, u32[]{:S(2)}) collective-permute-start(bf16[256,2048]{1,0:T(8,128)(2,1)S(1)} %get-tuple-element.60), channel_id=1, source_target_pairs={{0,1},{1,0},{2,3},{3,2},{4,5},{5,4},{6,7},{7,6},{8,9},{9,8},{10,11... | collective-permute-start | bytes 3145736 | tf_op jit(solution)/shard_map/ppermute | solution.py:364
  69.4 2.9 %collective-permute-start.11 = (bf16[256,2048]{1,0:T(8,128)(2,1)S(1)}, bf16[256,2048]{1,0:T(8,128)(2,1)S(1)}, u32[]{:S(2)}, u32[]{:S(2)}) collective-permute-start(bf16[256,2048]{1,0:T(8,128)(2,1)S(1)} %get-tuple-element.68), channel_id=1, source_target_pairs={{0,1},{1,0},{2,3},{3,2},{4,5},{5,4},{6,7},{7,6},{8,9},{9,8},{10,11... | collective-permute-start | bytes 3145736 | tf_op jit(solution)/shard_map/ppermute | solution.py:364
  105.9 11.2 %collective-permute-start.12 = (bf16[32,4224]{1,0:T(8,128)(2,1)S(1)}, bf16[32,4224]{1,0:T(8,128)(2,1)S(1)}, u32[]{:S(2)}, u32[]{:S(2)}) collective-permute-start(bf16[32,4224]{1,0:T(8,128)(2,1)S(1)} %get-tuple-element.75), channel_id=1, source_target_pairs={{0,224},{32,0},{64,32},{96,64},{128,96},{160,128},{192,160},{224,1... | collective-permute-start | bytes 811016 | tf_op jit(solution)/shard_map/ppermute | solution.py:372
  106.0 11.1 %collective-permute-start.13 = (bf16[32,4224]{1,0:T(8,128)(2,1)S(1)}, bf16[32,4224]{1,0:T(8,128)(2,1)S(1)}, u32[]{:S(2)}, u32[]{:S(2)}) collective-permute-start(bf16[32,4224]{1,0:T(8,128)(2,1)S(1)} %get-tuple-element.76), channel_id=1, source_target_pairs={{0,32},{32,64},{64,96},{96,128},{128,160},{160,192},{192,224},{224... | collective-permute-start | bytes 811016 | tf_op jit(solution)/shard_map/ppermute | solution.py:372
  108.0 9.1 %collective-permute-start.14 = (bf16[16,2048]{1,0:T(8,128)(2,1)S(1)}, bf16[16,2048]{1,0:T(8,128)(2,1)S(1)}, u32[]{:S(2)}, u32[]{:S(2)}) collective-permute-start(bf16[16,2048]{1,0:T(8,128)(2,1)S(1)} %get-tuple-element.78), channel_id=1, source_target_pairs={{0,64},{32,96},{64,128},{96,160},{128,192},{160,224},{192,0},{224,... | collective-permute-start | bytes 196616 | tf_op jit(solution)/shard_map/ppermute | solution.py:372
  109.3 7.8 %collective-permute-start.15 = (bf16[16,2176]{1,0:T(8,128)(2,1)S(1)}, bf16[16,2176]{1,0:T(8,128)(2,1)S(1)}, u32[]{:S(2)}, u32[]{:S(2)}) collective-permute-start(bf16[16,2176]{1,0:T(8,128)(2,1)S(1)} %get-tuple-element.79), channel_id=1, source_target_pairs={{0,192},{32,224},{64,0},{96,32},{128,64},{160,96},{192,128},{224,1... | collective-permute-start | bytes 208904 | tf_op jit(solution)/shard_map/ppermute | solution.py:372
  117.2 9.3 %collective-permute-start.16 = (bf16[16,4224]{1,0:T(8,128)(2,1)S(1)}, bf16[16,4224]{1,0:T(8,128)(2,1)S(1)}, u32[]{:S(2)}, u32[]{:S(2)}) collective-permute-start(bf16[16,4224]{1,0:T(8,128)(2,1)S(1)} %get-tuple-element.90), channel_id=1, source_target_pairs={{0,64},{32,96},{64,128},{96,160},{128,192},{160,224},{192,0},{224,... | collective-permute-start | bytes 405512 | tf_op jit(solution)/shard_map/ppermute | solution.py:372
  119.2 7.3 %collective-permute-start.17 = (bf16[16,4224]{1,0:T(8,128)(2,1)S(1)}, bf16[16,4224]{1,0:T(8,128)(2,1)S(1)}, u32[]{:S(2)}, u32[]{:S(2)}) collective-permute-start(bf16[16,4224]{1,0:T(8,128)(2,1)S(1)} %get-tuple-element.91), channel_id=1, source_target_pairs={{0,192},{32,224},{64,0},{96,32},{128,64},{160,96},{192,128},{224,1... | collective-permute-start | bytes 405512 | tf_op jit(solution)/shard_map/ppermute | solution.py:372

commit v6 on v5

--- a/solution.py
+++ b/solution.py
@@ -167,8 +167,8 @@
     up_out[...] = up
     hidden = (gate * jax.nn.sigmoid(gate) * up).astype(BF16)
     hidden_ref[...] = hidden
-    for i in range(0, D, 512):
-        back_ref[:, i : i + 512] = dot(hidden, down_ref[0, :, i : i + 512], 1, 0).astype(BF16)
+    for i in range(0, D, 1024):
+        back_ref[:, i : i + 1024] = dot(hidden, down_ref[0, :, i : i + 1024], 1, 0).astype(BF16)
 
 
 def backward_kernel(in_ref, gate_in, up_in, both_ref, down_ref, back_ref, pre_ref):
@@ -177,8 +177,8 @@
     hidden_grad = dot(in_ref[...], down_ref[0], 1, 1)
     pre_ref[:, :HALF] = (hidden_grad * up_in[...] * sig * (1.0 + gate * (1.0 - sig))).astype(BF16)
     pre_ref[:, HALF:] = (hidden_grad * gate * sig).astype(BF16)
-    for i in range(0, D, 512):
-        back_ref[:, i : i + 512] = dot(pre_ref[...], both_ref[i : i + 512, :], 1, 1).astype(BF16)
+    for i in range(0, D, 1024):
+        back_ref[:, i : i + 1024] = dot(pre_ref[...], both_ref[i : i + 1024, :], 1, 1).astype(BF16)
 
 
 COST = pl.CostEstimate(flops=6 * ROWS * D * HALF, bytes_accessed=5 * 2**20, transcendentals=ROWS * HALF)

time: 128 us -> 128 us (level)
  no operation moved by 1% of the time
where the time goes in v6:
time: 128 us; the launch traced here: 127 us
  blocking collectives  63.8 us (50%)
  starting transfers between devices  24.2 us (19%)
  waiting for transfers between devices  17.5 us (14%)
  Pallas kernels  17.3 us (14%)
  local copies, waits for them, and re-layouts  3.63 us (3%)
    all_to_all x2, blocking collectives, over_plane(): return lax.all_to_all(blocks, ('y', 'x'), 0, 0, tiled=True)  63.8 us
    ppermute x14, starting transfers between devices, shift(): lax.ppermute(value, 'z', [(i, (i + step) % PLANES) for i in range(PLANES)])  23 us
    ppermute x14, waiting for transfers between devices, shift(): lax.ppermute(value, 'z', [(i, (i + step) % PLANES) for i in range(PLANES)])  17 us
    pallas_call x1, Pallas kernels, weight_grads(): pl.pallas_call(weight_grad_kernel, grid=(steps,), out_shape=(jax.ShapeDty...  4.57 us
    pallas_call x2, Pallas kernels, forward(): pl.pallas_call(forward_kernel, out_shape=(WIDE, ACT, ACT32, ACT32), in_sp...  3.74 us
    pallas_call x2, Pallas kernels, backward(): pl.pallas_call(backward_kernel, out_shape=(WIDE, jax.ShapeDtypeStruct((RO...  3.39 us
    unnamed x8, local copies, waits for them, and re-layouts  3.38 us
  transfers between devices with their start and end apart: 18, of which 6 were waited for; matrix products, arithmetic and copies ran while one was open for 0% of the time, Pallas kernels for 9%

profile of v6, /device:TPU:32, one launch (start us, length us, event | category | flops | bytes accessed | tf_op | source)
XLA Modules:
  0.0 127.3 jit_solution(9891341077107512415)
XLA Ops:
  0.6 1.6 %pack_rows.1.refs_0_ = bf16[16,4224]{1,0:T(8,128)(2,1)} custom-call(bf16[16,2048]{1,0:T(8,128)(2,1)} %tok_hbm, bf16[16,2048]{1,0:T(8,128)(2,1)} %grad_hbm.1, s32[8,16]{1,0:T(8,128)} %bitcast.12, f32[8,16]{1,0:T(8,128)} %bitcast.13), custom_call_target="tpu_custom_call" | custom-call | tf_op jit(solution)/shard_map/pack_rows/pallas_call | solution.py:71
  2.2 5.5 %collective-permute-start.3 = (bf16[16,4224]{1,0:T(8,128)(2,1)}, bf16[16,4224]{1,0:T(8,128)(2,1)S(1)}, u32[]{:S(2)}, u32[]{:S(2)}) collective-permute-start(bf16[16,4224]{1,0:T(8,128)(2,1)} %pack_rows.1.refs_0_), channel_id=1, source_target_pairs={{0,192},{32,224},{64,0},{96,32},{128,64},{160,96},{192,128},{224,1... | collective-permute-start | bytes 405512 | tf_op jit(solution)/shard_map/ppermute | solution.py:372
  9.8 1.4 %copy-done.1 = bf16[1,2048,384]{2,1,0:T(8,128)(2,1)S(1)} copy-done((bf16[1,2048,384]{2,1,0:T(8,128)(2,1)S(1)}, bf16[1,2048,384]{2,1,0:T(8,128)(2,1)}, u32[]{:S(2)}) %copy-start.1) | copy-done | bytes 1572888
  11.2 1.4 %copy-done.2 = bf16[1,2048,384]{2,1,0:T(8,128)(2,1)S(1)} copy-done((bf16[1,2048,384]{2,1,0:T(8,128)(2,1)S(1)}, bf16[1,2048,384]{2,1,0:T(8,128)(2,1)}, u32[]{:S(2)}) %copy-start.2) | copy-done | bytes 1572888
  12.9 5.5 %collective-permute-done.2.refs_3_ = bf16[16,4224]{1,0:T(8,128)(2,1)S(1)} collective-permute-done((bf16[16,4224]{1,0:T(8,128)(2,1)}, bf16[16,4224]{1,0:T(8,128)(2,1)S(1)}, u32[]{:S(2)}, u32[]{:S(2)}) %collective-permute-start.2) | collective-permute-done | bytes 135200 | tf_op jit(solution)/shard_map/ppermute | solution.py:372
  18.4 2.0 %collective-permute-start.5 = (bf16[16,4224]{1,0:T(8,128)(2,1)S(1)}, bf16[16,4224]{1,0:T(8,128)(2,1)S(1)}, u32[]{:S(2)}, u32[]{:S(2)}) collective-permute-start(bf16[16,4224]{1,0:T(8,128)(2,1)S(1)} %collective-permute-done.3.refs_4_), channel_id=1, source_target_pairs={{0,224},{32,0},{64,32},{96,64},{128,96},{160,128},{192,160},{224,1... | collective-permute-start | bytes 405512 | tf_op jit(solution)/shard_map/ppermute | solution.py:372
  20.5 1.8 %collective-permute-start.7 = (bf16[16,2176]{1,0:T(8,128)(2,1)S(1)}, bf16[16,2176]{1,0:T(8,128)(2,1)S(1)}, u32[]{:S(2)}, u32[]{:S(2)}) collective-permute-start(bf16[16,2176]{1,0:T(8,128)(2,1)S(1)} %slice.13), channel_id=1, source_target_pairs={{0,192},{32,224},{64,0},{96,32},{128,64},{160,96},{192,128},{224,1... | collective-permute-start | bytes 208904 | tf_op jit(solution)/shard_map/ppermute | solution.py:372
  22.3 1.2 collective-permute-start.6
  23.5 5.9 %collective-permute-done.6.refs_7_ = bf16[16,2048]{1,0:T(8,128)(2,1)S(1)} collective-permute-done((bf16[16,2048]{1,0:T(8,128)(2,1)S(1)}, bf16[16,2048]{1,0:T(8,128)(2,1)S(1)}, u32[]{:S(2)}, u32[]{:S(2)}) %collective-permute-start.6) | collective-permute-done | bytes 65568 | tf_op jit(solution)/shard_map/ppermute | solution.py:372
  29.4 1.2 spread_rows.1
  30.6 31.8 %all_to_all.10 = bf16[16,32,2048]{2,1,0:T(8,128)(2,1)S(1)} all-to-all(bf16[16,32,2048]{2,1,0:T(8,128)(2,1)S(1)} %get-tuple-element.55), channel_id=1, replica_groups=mesh['z'=8,'y'=4,'x'=4,'core'=2] {'y','x'}, dimensions={0} | all-to-all | bytes 4194304 | tf_op jit(solution)/shard_map/all_to_all | solution.py:368
  63.8 1.9 %forward_rows.2 = (bf16[256,2048]{1,0:T(8,128)(2,1)S(1)}, bf16[256,384]{1,0:T(8,128)(2,1)S(1)}, f32[256,384]{1,0:T(8,128)S(1)}, f32[256,384]{1,0:T(8,128)S(1)}) custom-call(bf16[256,2048]{1,0:T(8,128)(2,1)S(1)} %bitcast.10, bf16[2048,768]{1,0:T(8,128)(2,1)S(1)} %hold_weights.1.both_ref, bf16[1,384,2048]{2,1,0:T(8,128)(2,1)S(1)} %copy-done), custom_call_target="tpu_custom_call" | custom-call | flops 1207959552 | bytes 5242880 | tf_op jit(solution)/shard_map/forward_rows/pallas_call | solution.py:191
  65.7 1.9 %forward_rows.3 = (bf16[256,2048]{1,0:T(8,128)(2,1)S(1)}, bf16[256,384]{1,0:T(8,128)(2,1)S(1)}, f32[256,384]{1,0:T(8,128)S(1)}, f32[256,384]{1,0:T(8,128)S(1)}) custom-call(bf16[256,2048]{1,0:T(8,128)(2,1)S(1)} %collective-permute-done.8.in_ref.x_b, bf16[2048,768]{1,0:T(8,128)(2,1)S(1)} %hold_weights.1.both_ref, bf16[1,384,2048]{2,1,0:T(8,128)(2,1)S(1)} %copy-done), custom_call_target="tpu_custom_call" | custom-call | flops 1207959552 | bytes 5242880 | tf_op jit(solution)/shard_map/forward_rows/pallas_call | solution.py:191
  67.7 1.7 %backward_rows.3 = (bf16[256,2048]{1,0:T(8,128)(2,1)S(1)}, bf16[256,768]{1,0:T(8,128)(2,1)S(1)}) custom-call(bf16[256,2048]{1,0:T(8,128)(2,1)S(1)} %collective-permute-done.10.in_ref.g_b, f32[256,384]{1,0:T(8,128)S(1)} %get-tuple-element.66.gate_in, f32[256,384]{1,0:T(8,128)S(1)} %get-tuple-element.67.up_in, bf16[2048,768]{1,0:T(8,128)(2,1)S(1)} %hold_weights.1.both_ref, ...), custom_call_target="tpu_custom_call" | custom-call | flops 1207959552 | bytes 5242880 | tf_op jit(solution)/shard_map/backward_rows/pallas_call | solution.py:203
  70.3 1.7 %backward_rows.2 = (bf16[256,2048]{1,0:T(8,128)(2,1)S(1)}, bf16[256,768]{1,0:T(8,128)(2,1)S(1)}) custom-call(bf16[256,2048]{1,0:T(8,128)(2,1)S(1)} %bitcast.7, f32[256,384]{1,0:T(8,128)S(1)} %get-tuple-element.63.gate_in, f32[256,384]{1,0:T(8,128)S(1)} %get-tuple-element.64.up_in, bf16[2048,768]{1,0:T(8,128)(2,1)S(1)} %hold_weights.1.both_ref, ...), custom_call_target="tpu_custom_call" | custom-call | flops 1207959552 | bytes 5242880 | tf_op jit(solution)/shard_map/backward_rows/pallas_call | solution.py:203
  72.8 32.0 %all_to_all.11.back_ref = bf16[16,32,2048]{2,1,0:T(8,128)(2,1)S(1)} all-to-all(bf16[16,32,2048]{2,1,0:T(8,128)(2,1)S(1)} %sum_halves.1), channel_id=1, replica_groups=mesh['z'=8,'y'=4,'x'=4,'core'=2] {'y','x'}, dimensions={0} | all-to-all | bytes 4194304 | tf_op jit(solution)/shard_map/all_to_all | solution.py:368
  104.7 1.2 combine_rows.1
  106.0 2.0 %collective-permute-start.13 = (bf16[32,4224]{1,0:T(8,128)(2,1)S(1)}, bf16[32,4224]{1,0:T(8,128)(2,1)S(1)}, u32[]{:S(2)}, u32[]{:S(2)}) collective-permute-start(bf16[32,4224]{1,0:T(8,128)(2,1)S(1)} %get-tuple-element.76), channel_id=1, source_target_pairs={{0,32},{32,64},{64,96},{96,128},{128,160},{160,192},{192,224},{224... | collective-permute-start | bytes 811016 | tf_op jit(solution)/shard_map/ppermute | solution.py:372
  108.0 1.2 collective-permute-start.14
  109.3 2.9 %collective-permute-start.15 = (bf16[16,2176]{1,0:T(8,128)(2,1)S(1)}, bf16[16,2176]{1,0:T(8,128)(2,1)S(1)}, u32[]{:S(2)}, u32[]{:S(2)}) collective-permute-start(bf16[16,2176]{1,0:T(8,128)(2,1)S(1)} %get-tuple-element.79), channel_id=1, source_target_pairs={{0,192},{32,224},{64,0},{96,32},{128,64},{160,96},{192,128},{224,1... | collective-permute-start | bytes 208904 | tf_op jit(solution)/shard_map/ppermute | solution.py:372
  112.2 4.6 %weight_grads.1 = (bf16[1,2048,384]{2,1,0:T(8,128)(2,1)}, bf16[1,2048,384]{2,1,0:T(8,128)(2,1)}, bf16[1,384,2048]{2,1,0:T(8,128)(2,1)}) custom-call(bf16[256,2048]{1,0:T(8,128)(2,1)S(1)} %bitcast.11, bf16[256,2048]{1,0:T(8,128)(2,1)S(1)} %bitcast.8, bf16[256,2048]{1,0:T(8,128)(2,1)S(1)} %collective-permute-done.8.in_ref.x_b, ...), custom_call_target="tpu_custom_call" | custom-call | flops 2415919104 | bytes 12582912 | tf_op jit(solution)/shard_map/weight_grads/pallas_call | solution.py:244
  117.2 2.0 %collective-permute-start.16 = (bf16[16,4224]{1,0:T(8,128)(2,1)S(1)}, bf16[16,4224]{1,0:T(8,128)(2,1)S(1)}, u32[]{:S(2)}, u32[]{:S(2)}) collective-permute-start(bf16[16,4224]{1,0:T(8,128)(2,1)S(1)} %get-tuple-element.90), channel_id=1, source_target_pairs={{0,64},{32,96},{64,128},{96,160},{128,192},{160,224},{192,0},{224,... | collective-permute-start | bytes 405512 | tf_op jit(solution)/shard_map/ppermute | solution.py:372
  119.2 2.2 %collective-permute-start.17 = (bf16[16,4224]{1,0:T(8,128)(2,1)S(1)}, bf16[16,4224]{1,0:T(8,128)(2,1)S(1)}, u32[]{:S(2)}, u32[]{:S(2)}) collective-permute-start(bf16[16,4224]{1,0:T(8,128)(2,1)S(1)} %get-tuple-element.91), channel_id=1, source_target_pairs={{0,192},{32,224},{64,0},{96,32},{128,64},{160,96},{192,128},{224,1... | collective-permute-start | bytes 405512 | tf_op jit(solution)/shard_map/ppermute | solution.py:372
  121.4 5.1 %collective-permute-done.16.refs_3_ = bf16[16,4224]{1,0:T(8,128)(2,1)S(1)} collective-permute-done((bf16[16,4224]{1,0:T(8,128)(2,1)S(1)}, bf16[16,4224]{1,0:T(8,128)(2,1)S(1)}, u32[]{:S(2)}, u32[]{:S(2)}) %collective-permute-start.16) | collective-permute-done | bytes 135200 | tf_op jit(solution)/shard_map/ppermute | solution.py:372
  (37 shorter events, 6.8 us)
Async XLA Ops:
  2.2 10.7 %collective-permute-start.3 = (bf16[16,4224]{1,0:T(8,128)(2,1)}, bf16[16,4224]{1,0:T(8,128)(2,1)S(1)}, u32[]{:S(2)}, u32[]{:S(2)}) collective-permute-start(bf16[16,4224]{1,0:T(8,128)(2,1)} %pack_rows.1.refs_0_), channel_id=1, source_target_pairs={{0,192},{32,224},{64,0},{96,32},{128,64},{160,96},{192,128},{224,1... | collective-permute-start | bytes 405512 | tf_op jit(solution)/shard_map/ppermute | solution.py:372
  7.7 10.7 %collective-permute-start.2 = (bf16[16,4224]{1,0:T(8,128)(2,1)}, bf16[16,4224]{1,0:T(8,128)(2,1)S(1)}, u32[]{:S(2)}, u32[]{:S(2)}) collective-permute-start(bf16[16,4224]{1,0:T(8,128)(2,1)} %pack_rows.1.refs_0_), channel_id=1, source_target_pairs={{0,64},{32,96},{64,128},{96,160},{128,192},{160,224},{192,0},{224,... | collective-permute-start | bytes 405512 | tf_op jit(solution)/shard_map/ppermute | solution.py:372
  7.7 14.6 %collective-permute-start.1 = (bf16[16,4224]{1,0:T(8,128)(2,1)}, bf16[16,4224]{1,0:T(8,128)(2,1)S(1)}, u32[]{:S(2)}, u32[]{:S(2)}) collective-permute-start(bf16[16,4224]{1,0:T(8,128)(2,1)} %pack_rows.1.refs_0_), channel_id=1, source_target_pairs={{0,224},{32,0},{64,32},{96,64},{128,96},{160,128},{192,160},{224,1... | collective-permute-start | bytes 405512 | tf_op jit(solution)/shard_map/ppermute | solution.py:372
  8.7 14.7 %collective-permute-start = (bf16[16,4224]{1,0:T(8,128)(2,1)}, bf16[16,4224]{1,0:T(8,128)(2,1)S(1)}, u32[]{:S(2)}, u32[]{:S(2)}) collective-permute-start(bf16[16,4224]{1,0:T(8,128)(2,1)} %pack_rows.1.refs_0_), channel_id=1, source_target_pairs={{0,32},{32,64},{64,96},{96,128},{128,160},{160,192},{192,224},{224... | collective-permute-start | bytes 405512 | tf_op jit(solution)/shard_map/ppermute | solution.py:372
  9.7 1.4 %copy-start.1 = (bf16[1,2048,384]{2,1,0:T(8,128)(2,1)S(1)}, bf16[1,2048,384]{2,1,0:T(8,128)(2,1)}, u32[]{:S(2)}) copy-start(bf16[1,2048,384]{2,1,0:T(8,128)(2,1)} %gate_hbm.1) | copy-start | bytes 4718596
  11.2 1.4 %copy-start.2 = (bf16[1,2048,384]{2,1,0:T(8,128)(2,1)S(1)}, bf16[1,2048,384]{2,1,0:T(8,128)(2,1)}, u32[]{:S(2)}) copy-start(bf16[1,2048,384]{2,1,0:T(8,128)(2,1)} %up_hbm.1) | copy-start | bytes 4718596
  12.6 16.9 %copy-start.3 = (bf16[16,4224]{1,0:T(8,128)(2,1)S(1)}, bf16[16,4224]{1,0:T(8,128)(2,1)}, u32[]{:S(2)}) copy-start(bf16[16,4224]{1,0:T(8,128)(2,1)} %pack_rows.1.refs_0_) | copy-start | bytes 405508
  18.4 11.0 %collective-permute-start.4 = (bf16[16,4224]{1,0:T(8,128)(2,1)S(1)}, bf16[16,4224]{1,0:T(8,128)(2,1)S(1)}, u32[]{:S(2)}, u32[]{:S(2)}) collective-permute-start(bf16[16,4224]{1,0:T(8,128)(2,1)S(1)} %collective-permute-done.2.refs_3_), channel_id=1, source_target_pairs={{0,32},{32,64},{64,96},{96,128},{128,160},{160,192},{192,224},{224... | collective-permute-start | bytes 405512 | tf_op jit(solution)/shard_map/ppermute | solution.py:372
  18.4 11.0 %collective-permute-start.5 = (bf16[16,4224]{1,0:T(8,128)(2,1)S(1)}, bf16[16,4224]{1,0:T(8,128)(2,1)S(1)}, u32[]{:S(2)}, u32[]{:S(2)}) collective-permute-start(bf16[16,4224]{1,0:T(8,128)(2,1)S(1)} %collective-permute-done.3.refs_4_), channel_id=1, source_target_pairs={{0,224},{32,0},{64,32},{96,64},{128,96},{160,128},{192,160},{224,1... | collective-permute-start | bytes 405512 | tf_op jit(solution)/shard_map/ppermute | solution.py:372
  20.5 9.0 %collective-permute-start.7 = (bf16[16,2176]{1,0:T(8,128)(2,1)S(1)}, bf16[16,2176]{1,0:T(8,128)(2,1)S(1)}, u32[]{:S(2)}, u32[]{:S(2)}) collective-permute-start(bf16[16,2176]{1,0:T(8,128)(2,1)S(1)} %slice.13), channel_id=1, source_target_pairs={{0,192},{32,224},{64,0},{96,32},{128,64},{160,96},{192,128},{224,1... | collective-permute-start | bytes 208904 | tf_op jit(solution)/shard_map/ppermute | solution.py:372
  22.3 7.1 %collective-permute-start.6 = (bf16[16,2048]{1,0:T(8,128)(2,1)S(1)}, bf16[16,2048]{1,0:T(8,128)(2,1)S(1)}, u32[]{:S(2)}, u32[]{:S(2)}) collective-permute-start(bf16[16,2048]{1,0:T(8,128)(2,1)S(1)} %slice.16), channel_id=1, source_target_pairs={{0,64},{32,96},{64,128},{96,160},{128,192},{160,224},{192,0},{224,... | collective-permute-start | bytes 196616 | tf_op jit(solution)/shard_map/ppermute | solution.py:372
  62.4 1.4 %copy-start = (bf16[1,384,2048]{2,1,0:T(8,128)(2,1)S(1)}, bf16[1,384,2048]{2,1,0:T(8,128)(2,1)}, u32[]{:S(2)}) copy-start(bf16[1,384,2048]{2,1,0:T(8,128)(2,1)} %down_ref.7) | copy-start | bytes 4718596
  62.7 3.0 %collective-permute-start.8 = (bf16[256,2048]{1,0:T(8,128)(2,1)S(1)}, bf16[256,2048]{1,0:T(8,128)(2,1)S(1)}, u32[]{:S(2)}, u32[]{:S(2)}) collective-permute-start(bf16[256,2048]{1,0:T(8,128)(2,1)S(1)} %bitcast.9), channel_id=1, source_target_pairs={{0,1},{1,0},{2,3},{3,2},{4,5},{5,4},{6,7},{7,6},{8,9},{9,8},{10,11... | collective-permute-start | bytes 3145736 | tf_op jit(solution)/shard_map/ppermute | solution.py:364
  62.8 4.9 %collective-permute-start.10 = (bf16[256,2048]{1,0:T(8,128)(2,1)S(1)}, bf16[256,2048]{1,0:T(8,128)(2,1)S(1)}, u32[]{:S(2)}, u32[]{:S(2)}) collective-permute-start(bf16[256,2048]{1,0:T(8,128)(2,1)S(1)} %bitcast.6), channel_id=1, source_target_pairs={{0,1},{1,0},{2,3},{3,2},{4,5},{5,4},{6,7},{7,6},{8,9},{9,8},{10,11... | collective-permute-start | bytes 3145736 | tf_op jit(solution)/shard_map/ppermute | solution.py:364
  67.6 2.7 %collective-permute-start.9 = (bf16[256,2048]{1,0:T(8,128)(2,1)S(1)}, bf16[256,2048]{1,0:T(8,128)(2,1)S(1)}, u32[]{:S(2)}, u32[]{:S(2)}) collective-permute-start(bf16[256,2048]{1,0:T(8,128)(2,1)S(1)} %get-tuple-element.60), channel_id=1, source_target_pairs={{0,1},{1,0},{2,3},{3,2},{4,5},{5,4},{6,7},{7,6},{8,9},{9,8},{10,11... | collective-permute-start | bytes 3145736 | tf_op jit(solution)/shard_map/ppermute | solution.py:364
  69.4 2.9 %collective-permute-start.11 = (bf16[256,2048]{1,0:T(8,128)(2,1)S(1)}, bf16[256,2048]{1,0:T(8,128)(2,1)S(1)}, u32[]{:S(2)}, u32[]{:S(2)}) collective-permute-start(bf16[256,2048]{1,0:T(8,128)(2,1)S(1)} %get-tuple-element.68), channel_id=1, source_target_pairs={{0,1},{1,0},{2,3},{3,2},{4,5},{5,4},{6,7},{7,6},{8,9},{9,8},{10,11... | collective-permute-start | bytes 3145736 | tf_op jit(solution)/shard_map/ppermute | solution.py:364
  105.9 11.2 %collective-permute-start.12 = (bf16[32,4224]{1,0:T(8,128)(2,1)S(1)}, bf16[32,4224]{1,0:T(8,128)(2,1)S(1)}, u32[]{:S(2)}, u32[]{:S(2)}) collective-permute-start(bf16[32,4224]{1,0:T(8,128)(2,1)S(1)} %get-tuple-element.75), channel_id=1, source_target_pairs={{0,224},{32,0},{64,32},{96,64},{128,96},{160,128},{192,160},{224,1... | collective-permute-start | bytes 811016 | tf_op jit(solution)/shard_map/ppermute | solution.py:372
  106.0 11.1 %collective-permute-start.13 = (bf16[32,4224]{1,0:T(8,128)(2,1)S(1)}, bf16[32,4224]{1,0:T(8,128)(2,1)S(1)}, u32[]{:S(2)}, u32[]{:S(2)}) collective-permute-start(bf16[32,4224]{1,0:T(8,128)(2,1)S(1)} %get-tuple-element.76), channel_id=1, source_target_pairs={{0,32},{32,64},{64,96},{96,128},{128,160},{160,192},{192,224},{224... | collective-permute-start | bytes 811016 | tf_op jit(solution)/shard_map/ppermute | solution.py:372
  108.0 9.1 %collective-permute-start.14 = (bf16[16,2048]{1,0:T(8,128)(2,1)S(1)}, bf16[16,2048]{1,0:T(8,128)(2,1)S(1)}, u32[]{:S(2)}, u32[]{:S(2)}) collective-permute-start(bf16[16,2048]{1,0:T(8,128)(2,1)S(1)} %get-tuple-element.78), channel_id=1, source_target_pairs={{0,64},{32,96},{64,128},{96,160},{128,192},{160,224},{192,0},{224,... | collective-permute-start | bytes 196616 | tf_op jit(solution)/shard_map/ppermute | solution.py:372
  109.3 7.8 %collective-permute-start.15 = (bf16[16,2176]{1,0:T(8,128)(2,1)S(1)}, bf16[16,2176]{1,0:T(8,128)(2,1)S(1)}, u32[]{:S(2)}, u32[]{:S(2)}) collective-permute-start(bf16[16,2176]{1,0:T(8,128)(2,1)S(1)} %get-tuple-element.79), channel_id=1, source_target_pairs={{0,192},{32,224},{64,0},{96,32},{128,64},{160,96},{192,128},{224,1... | collective-permute-start | bytes 208904 | tf_op jit(solution)/shard_map/ppermute | solution.py:372
  117.2 9.3 %collective-permute-start.16 = (bf16[16,4224]{1,0:T(8,128)(2,1)S(1)}, bf16[16,4224]{1,0:T(8,128)(2,1)S(1)}, u32[]{:S(2)}, u32[]{:S(2)}) collective-permute-start(bf16[16,4224]{1,0:T(8,128)(2,1)S(1)} %get-tuple-element.90), channel_id=1, source_target_pairs={{0,64},{32,96},{64,128},{96,160},{128,192},{160,224},{192,0},{224,... | collective-permute-start | bytes 405512 | tf_op jit(solution)/shard_map/ppermute | solution.py:372
  119.2 7.3 %collective-permute-start.17 = (bf16[16,4224]{1,0:T(8,128)(2,1)S(1)}, bf16[16,4224]{1,0:T(8,128)(2,1)S(1)}, u32[]{:S(2)}, u32[]{:S(2)}) collective-permute-start(bf16[16,4224]{1,0:T(8,128)(2,1)S(1)} %get-tuple-element.91), channel_id=1, source_target_pairs={{0,192},{32,224},{64,0},{96,32},{128,64},{160,96},{192,128},{224,1... | collective-permute-start | bytes 405512 | tf_op jit(solution)/shard_map/ppermute | solution.py:372
